TPU v7x, 32 devices: a whole 2x2x4 slice. The times are simulated.
32 devices in a mesh: dp: 2 (over y), ctx: 8 (over z, x), tensor: 2 (over core).
Axes of the slice: x: 2, y: 2, z: 4, core: 2. Of those that a mesh axis runs over, the one named last changes fastest.
Arguments:
- tokens: bfloat16 [2, 2, 2048, 768], P(None, 'dp', 'ctx'), may hold values from -6 to 6
- prefix: int32 [2, 2], P(None, 'dp'), may hold values from 204 to 1024
- w_query: bfloat16 [768, 768], P(('dp', 'ctx'), 'tensor'), may hold values from -0.21875 to 0.21875
- w_key: bfloat16 [768, 768], P(('dp', 'ctx'), 'tensor'), may hold values from -0.21875 to 0.21875
- w_value: bfloat16 [768, 768], P(('dp', 'ctx'), 'tensor'), may hold values from -0.21875 to 0.21875
- w_score: bfloat16 [768, 12], P(('dp', 'ctx'), 'tensor'), may hold values from -0.4375 to 0.4375
- w_attn_out: bfloat16 [768, 768], P('tensor', ('dp', 'ctx')), may hold values from -1.5 to 1.5
- w_fc: bfloat16 [768, 3072], P(('dp', 'ctx'), 'tensor'), may hold values from -0.21875 to 0.21875
- w_proj: bfloat16 [3072, 768], P('tensor', ('dp', 'ctx')), may hold values from -0.109375 to 0.109375
- ln1_gain: bfloat16 [768], P(('dp', 'ctx')), may hold values from 0.5 to 1.5
- ln1_bias: bfloat16 [768], P(('dp', 'ctx')), may hold values from -2 to 2
- ln2_gain: bfloat16 [768], P(('dp', 'ctx')), may hold values from 0.5 to 1.5
- ln2_bias: bfloat16 [768], P(('dp', 'ctx')), may hold values from -2 to 2
- attn_bias: bfloat16 [768], P(('dp', 'ctx')), may hold values from -2 to 2
- fc_bias: bfloat16 [3072], P('tensor'), may hold values from -2 to 2
- proj_bias: bfloat16 [768], P(('dp', 'ctx')), may hold values from -2 to 2
- cotangent: bfloat16 [2, 2, 2048, 768], P(None, 'dp', 'ctx'), may hold values from -6 to 6
Outputs:
- output: bfloat16 [2, 2, 2048, 768], P(None, 'dp', 'ctx')
- tokens_grad: float32 [2, 2, 2048, 768], P(None, 'dp', 'ctx')
- w_query_grad: float32 [768, 768], P(('dp', 'ctx'), 'tensor')
- w_key_grad: float32 [768, 768], P(('dp', 'ctx'), 'tensor')
- w_value_grad: float32 [768, 768], P(('dp', 'ctx'), 'tensor')
- w_score_grad: float32 [768, 12], P(('dp', 'ctx'), 'tensor')
- w_attn_out_grad: float32 [768, 768], P('tensor', ('dp', 'ctx'))
- w_fc_grad: float32 [768, 3072], P(('dp', 'ctx'), 'tensor')
- w_proj_grad: float32 [3072, 768], P('tensor', ('dp', 'ctx'))
- ln1_gain_grad: float32 [768], P(('dp', 'ctx'))
- ln1_bias_grad: float32 [768], P(('dp', 'ctx'))
- ln2_gain_grad: float32 [768], P(('dp', 'ctx'))
- ln2_bias_grad: float32 [768], P(('dp', 'ctx'))
- attn_bias_grad: float32 [768], P(('dp', 'ctx'))
- fc_bias_grad: float32 [3072], P('tensor')
- proj_bias_grad: float32 [768], P(('dp', 'ctx'))
All inputs are finite; a program needn't handle non-finite values.
Results may differ from a plain program's by a relative error of at most 0.017.
Values may be sent and summed in bfloat16 or wider, within the bound.
No kernel may reach another device: no remote copies, remote signals or barrier semaphores. Data moves between devices by JAX's collectives and lax.ppermute only.
A program may use at most 192 MiB of HBM per device.

v0:
```python
from functools import partial

import jax
import jax.numpy as jnp
from jax import lax
from jax.sharding import PartitionSpec as P

WIN = 64
TOPK = 64


norm_epsilon = 1e-05
search_steps = 24
search_bound = 64.0


def layer_normalize(values, norm_gain, norm_shift):
    centre = jnp.mean(values, axis=-1, keepdims=True)
    centred = values - centre
    spread = jnp.mean(centred * centred, axis=-1, keepdims=True)
    return centred * lax.rsqrt(spread + norm_epsilon) * norm_gain + norm_shift


def gelu_tanh(values):
    return jax.nn.gelu(values, approximate=True)


def split_heads(values, head_count):
    seq_count, row_count, full_width = values.shape
    shaped = values.reshape(seq_count, row_count, head_count, full_width // head_count)
    return shaped.transpose(0, 2, 1, 3).reshape(
        seq_count * head_count, row_count, full_width // head_count
    )


def join_heads(values, seq_count):
    item_count, row_count, head_width = values.shape
    head_count = item_count // seq_count
    shaped = values.reshape(seq_count, head_count, row_count, head_width)
    return shaped.transpose(0, 2, 1, 3).reshape(seq_count, row_count, head_count * head_width)


def threshold_search(score_row, candidate):
    score_mat = score_row[None, :]
    lower_end = jnp.zeros((candidate.shape[0],), score_row.dtype) - search_bound
    upper_end = jnp.zeros((candidate.shape[0],), score_row.dtype) + search_bound

    def bisect(step, bounds):
        lower_now, upper_now = bounds
        centre_val = 0.5 * (lower_now + upper_now)
        filled = jnp.sum(
            jnp.where(candidate, jax.nn.sigmoid(score_mat - centre_val[:, None]), 0.0), axis=1
        )
        above = filled > TOPK
        return (jnp.where(above, centre_val, lower_now), jnp.where(above, upper_now, centre_val))

    lower_end, upper_end = lax.fori_loop(0, search_steps, bisect, (lower_end, upper_end))
    return 0.5 * (lower_end + upper_end)


def sparse_mask(score_row, candidate, pivot):
    score_mat = score_row[None, :]
    mask = jnp.where(candidate, jax.nn.sigmoid(score_mat - pivot[:, None]), 0.0)
    enough = jnp.sum(jnp.where(candidate, 1.0, 0.0), axis=1) > TOPK
    return jnp.where(enough[:, None], mask, jnp.where(candidate, 1.0, 0.0))


def masked_logits(query_head, key_head, prefix_len, first_row):
    query_pos = first_row + jnp.arange(query_head.shape[0], dtype=jnp.int32)
    key_pos = jnp.arange(key_head.shape[0], dtype=jnp.int32)
    logits = jnp.einsum(
        "qd,kd->qk", query_head, key_head, preferred_element_type=jnp.float32
    ) * query_head.shape[1] ** (-0.5)
    allowed = (key_pos[None, :] <= query_pos[:, None]) | (key_pos[None, :] < prefix_len)
    nearby = jnp.abs(query_pos[:, None] - key_pos[None, :]) < WIN
    return (logits, allowed, allowed & nearby, allowed & jnp.logical_not(nearby))


def attend_item(packed, first_row):
    query_head, key_head, value_head, score_head, prefix_len = packed
    logits, allowed, local_keys, candidate = masked_logits(
        query_head, key_head, prefix_len, first_row
    )
    score_row = score_head.astype(jnp.float32)
    pivot = threshold_search(score_row, candidate)
    mask = sparse_mask(score_row, candidate, pivot)
    key_gate = jnp.where(local_keys, 1.0, mask)
    row_top = jnp.max(jnp.where(local_keys, logits, -1e30), axis=1, keepdims=True)
    weights = key_gate * jnp.exp(jnp.where(allowed, logits - row_top, -1e30))
    row_total = jnp.sum(weights, axis=1, keepdims=True)
    probs_low = (weights / row_total).astype(jnp.bfloat16)
    attended = jnp.dot(probs_low, value_head, preferred_element_type=jnp.float32)
    return (attended, (row_top + jnp.log(row_total))[:, 0], pivot)


def attend_back_item(packed, first_row):
    query_head, key_head, value_head, score_head, prefix_len, log_total, pivot, grad_head = packed
    logits, allowed, local_keys, candidate = masked_logits(
        query_head, key_head, prefix_len, first_row
    )
    score_row = score_head.astype(jnp.float32)
    mask, mask_pull = jax.vjp(
        lambda row_values: sparse_mask(row_values, candidate, pivot), score_row
    )
    key_gate = jnp.where(local_keys, 1.0, mask)
    unit_probs = jnp.exp(jnp.where(allowed, logits - log_total[:, None], -1e30))
    probs = key_gate * unit_probs
    probs_low = probs.astype(jnp.bfloat16)
    grad_probs = jnp.einsum("qd,kd->qk", grad_head, value_head, preferred_element_type=jnp.float32)
    row_dot = jnp.sum(probs * grad_probs, axis=1, keepdims=True)
    spread = unit_probs * (grad_probs - row_dot)
    grad_logits = (key_gate * spread).astype(jnp.bfloat16)
    grad_score = mask_pull(jnp.where(local_keys, 0.0, spread))[0]
    scale_factor = query_head.shape[1] ** (-0.5)
    grad_query = jnp.dot(grad_logits, key_head, preferred_element_type=jnp.float32) * scale_factor
    grad_key = (
        jnp.einsum("qk,qd->kd", grad_logits, query_head, preferred_element_type=jnp.float32)
        * scale_factor
    )
    grad_value = jnp.einsum("qk,qd->kd", probs_low, grad_head, preferred_element_type=jnp.float32)
    return (grad_query, grad_key, grad_value, grad_score)


def on_device(
    tokens,
    prefix,
    w_query,
    w_key,
    w_value,
    w_score,
    w_attn_out,
    w_fc,
    w_proj,
    ln1_gain,
    ln1_bias,
    ln2_gain,
    ln2_bias,
    attn_bias,
    fc_bias,
    proj_bias,
    cotangent,
):
    micro_count, seq_count, tok_count, model_width = tokens.shape
    head_local = w_score.shape[1]
    row_count = seq_count * tok_count
    first_row = lax.axis_index("ctx") * tok_count
    fc_shift = fc_bias.astype(jnp.float32)
    outputs = []
    input_grads = []
    running = None
    fc_bias_local = jnp.zeros(fc_bias.shape, jnp.float32)
    for micro_index in range(micro_count):
        full_weights = (
            lax.all_gather(w_query, ("dp", "ctx"), axis=0, tiled=True),
            lax.all_gather(w_key, ("dp", "ctx"), axis=0, tiled=True),
            lax.all_gather(w_value, ("dp", "ctx"), axis=0, tiled=True),
            lax.all_gather(w_score, ("dp", "ctx"), axis=0, tiled=True),
            lax.all_gather(w_fc, ("dp", "ctx"), axis=0, tiled=True),
            lax.all_gather(w_attn_out, ("dp", "ctx"), axis=1, tiled=True),
            lax.all_gather(w_proj, ("dp", "ctx"), axis=1, tiled=True),
            lax.all_gather(ln1_gain, ("dp", "ctx"), axis=0, tiled=True),
            lax.all_gather(ln1_bias, ("dp", "ctx"), axis=0, tiled=True),
            lax.all_gather(ln2_gain, ("dp", "ctx"), axis=0, tiled=True),
            lax.all_gather(ln2_bias, ("dp", "ctx"), axis=0, tiled=True),
            lax.all_gather(attn_bias, ("dp", "ctx"), axis=0, tiled=True),
            lax.all_gather(proj_bias, ("dp", "ctx"), axis=0, tiled=True),
        )
        (
            full_query,
            full_key,
            full_value,
            full_score,
            full_fc,
            full_attn_out,
            full_proj,
            gain_one,
            shift_one,
            gain_two,
            shift_two,
            attn_shift,
            proj_shift,
        ) = full_weights
        block = tokens[micro_index].reshape(row_count, model_width).astype(jnp.float32)
        norm_one, pull_one = jax.vjp(
            layer_normalize, block, gain_one.astype(jnp.float32), shift_one.astype(jnp.float32)
        )
        normed_low = norm_one.astype(jnp.bfloat16)
        queries = jnp.dot(normed_low, full_query, preferred_element_type=jnp.float32).astype(
            jnp.bfloat16
        )
        keys_low = jnp.dot(normed_low, full_key, preferred_element_type=jnp.float32).astype(
            jnp.bfloat16
        )
        values_low = jnp.dot(normed_low, full_value, preferred_element_type=jnp.float32).astype(
            jnp.bfloat16
        )
        scores_low = jnp.dot(normed_low, full_score, preferred_element_type=jnp.float32).astype(
            jnp.bfloat16
        )
        keys_all, values_all, scores_all = (
            lax.all_gather(keys_low.reshape(seq_count, tok_count, -1), "ctx", axis=1, tiled=True),
            lax.all_gather(values_low.reshape(seq_count, tok_count, -1), "ctx", axis=1, tiled=True),
            lax.all_gather(scores_low.reshape(seq_count, tok_count, -1), "ctx", axis=1, tiled=True),
        )
        query_items = split_heads(queries.reshape(seq_count, tok_count, -1), head_local)
        key_items = split_heads(keys_all, head_local)
        value_items = split_heads(values_all, head_local)
        score_items = scores_all.transpose(0, 2, 1).reshape(seq_count * head_local, -1)
        prefix_items = jnp.repeat(prefix[micro_index], head_local)
        attended, log_totals, pivots = lax.map(
            partial(attend_item, first_row=first_row),
            (query_items, key_items, value_items, score_items, prefix_items),
        )
        merged_low = join_heads(attended, seq_count).reshape(row_count, -1).astype(jnp.bfloat16)
        attn_sum = lax.psum(
            jnp.dot(merged_low, full_attn_out, preferred_element_type=jnp.float32).astype(
                jnp.bfloat16
            ),
            "tensor",
        ).astype(jnp.float32)
        middle = block + attn_sum + attn_shift.astype(jnp.float32)
        norm_two, pull_two = jax.vjp(
            layer_normalize, middle, gain_two.astype(jnp.float32), shift_two.astype(jnp.float32)
        )
        normed_two_low = norm_two.astype(jnp.bfloat16)
        hidden_pre = jnp.dot(normed_two_low, full_fc, preferred_element_type=jnp.float32) + fc_shift
        active, pull_gelu = jax.vjp(gelu_tanh, hidden_pre)
        active_low = active.astype(jnp.bfloat16)
        mlp_sum = lax.psum(
            jnp.dot(active_low, full_proj, preferred_element_type=jnp.float32).astype(jnp.bfloat16),
            "tensor",
        ).astype(jnp.float32)
        result = middle + mlp_sum + proj_shift.astype(jnp.float32)
        outputs.append(result.reshape(seq_count, tok_count, model_width).astype(jnp.bfloat16))
        grad_low = cotangent[micro_index].reshape(row_count, model_width)
        grad_out = grad_low.astype(jnp.float32)
        grad_proj_shift = jnp.sum(grad_out, axis=0)
        grad_proj = jnp.einsum(
            "rf,rd->fd", active_low, grad_low, preferred_element_type=jnp.float32
        )
        grad_active = jnp.einsum(
            "rd,fd->rf", grad_low, full_proj, preferred_element_type=jnp.float32
        )
        grad_pre_low = pull_gelu(grad_active)[0].astype(jnp.bfloat16)
        fc_bias_local = fc_bias_local + jnp.sum(grad_pre_low.astype(jnp.float32), axis=0)
        grad_fc = jnp.einsum(
            "rd,rf->df", normed_two_low, grad_pre_low, preferred_element_type=jnp.float32
        )
        grad_norm_two = lax.psum(
            jnp.einsum(
                "rf,df->rd", grad_pre_low, full_fc, preferred_element_type=jnp.float32
            ).astype(jnp.bfloat16),
            "tensor",
        ).astype(jnp.float32)
        grad_middle_norm, grad_gain_two, grad_shift_two = pull_two(grad_norm_two)
        grad_middle = grad_out + grad_middle_norm
        grad_attn_shift = jnp.sum(grad_middle, axis=0)
        grad_middle_low = grad_middle.astype(jnp.bfloat16)
        grad_attn_out = jnp.einsum(
            "rh,rd->hd", merged_low, grad_middle_low, preferred_element_type=jnp.float32
        )
        grad_merged_low = jnp.einsum(
            "rd,hd->rh", grad_middle_low, full_attn_out, preferred_element_type=jnp.float32
        ).astype(jnp.bfloat16)
        grad_items = split_heads(grad_merged_low.reshape(seq_count, tok_count, -1), head_local)
        grad_q_items, grad_k_items, grad_v_items, grad_s_items = lax.map(
            partial(attend_back_item, first_row=first_row),
            (
                query_items,
                key_items,
                value_items,
                score_items,
                prefix_items,
                log_totals,
                pivots,
                grad_items,
            ),
        )
        grad_keys, grad_values, grad_scores = (
            lax.psum_scatter(
                join_heads(grad_k_items, seq_count).astype(jnp.bfloat16),
                "ctx",
                scatter_dimension=1,
                tiled=True,
            ).astype(jnp.float32),
            lax.psum_scatter(
                join_heads(grad_v_items, seq_count).astype(jnp.bfloat16),
                "ctx",
                scatter_dimension=1,
                tiled=True,
            ).astype(jnp.float32),
            lax.psum_scatter(
                grad_s_items.reshape(seq_count, head_local, -1)
                .transpose(0, 2, 1)
                .astype(jnp.bfloat16),
                "ctx",
                scatter_dimension=1,
                tiled=True,
            ).astype(jnp.float32),
        )
        grad_keys_low = grad_keys.reshape(row_count, -1).astype(jnp.bfloat16)
        grad_values_low = grad_values.reshape(row_count, -1).astype(jnp.bfloat16)
        grad_scores_low = grad_scores.reshape(row_count, -1).astype(jnp.bfloat16)
        grad_queries_low = (
            join_heads(grad_q_items, seq_count).reshape(row_count, -1).astype(jnp.bfloat16)
        )
        grad_query_w = jnp.einsum(
            "rd,rh->dh", normed_low, grad_queries_low, preferred_element_type=jnp.float32
        )
        grad_key_w = jnp.einsum(
            "rd,rh->dh", normed_low, grad_keys_low, preferred_element_type=jnp.float32
        )
        grad_value_w = jnp.einsum(
            "rd,rh->dh", normed_low, grad_values_low, preferred_element_type=jnp.float32
        )
        grad_score_w = jnp.einsum(
            "rd,rh->dh", normed_low, grad_scores_low, preferred_element_type=jnp.float32
        )
        partial_norm = jnp.einsum(
            "rh,dh->rd", grad_queries_low, full_query, preferred_element_type=jnp.float32
        )
        partial_norm = partial_norm + jnp.einsum(
            "rh,dh->rd", grad_keys_low, full_key, preferred_element_type=jnp.float32
        )
        partial_norm = partial_norm + jnp.einsum(
            "rh,dh->rd", grad_values_low, full_value, preferred_element_type=jnp.float32
        )
        partial_norm = partial_norm + jnp.einsum(
            "rh,dh->rd", grad_scores_low, full_score, preferred_element_type=jnp.float32
        )
        grad_norm_one = lax.psum(partial_norm.astype(jnp.bfloat16), "tensor").astype(jnp.float32)
        grad_block_norm, grad_gain_one, grad_shift_one = pull_one(grad_norm_one)
        input_grads.append(
            (grad_middle + grad_block_norm).reshape(seq_count, tok_count, model_width)
        )
        local_grads = (
            grad_query_w,
            grad_key_w,
            grad_value_w,
            grad_score_w,
            grad_fc,
            grad_attn_out,
            grad_proj,
            grad_gain_one,
            grad_shift_one,
            grad_gain_two,
            grad_shift_two,
            grad_attn_shift,
            grad_proj_shift,
        )
        summed = (
            lax.psum_scatter(local_grads[0], ("dp", "ctx"), scatter_dimension=0, tiled=True),
            lax.psum_scatter(local_grads[1], ("dp", "ctx"), scatter_dimension=0, tiled=True),
            lax.psum_scatter(local_grads[2], ("dp", "ctx"), scatter_dimension=0, tiled=True),
            lax.psum_scatter(local_grads[3], ("dp", "ctx"), scatter_dimension=0, tiled=True),
            lax.psum_scatter(local_grads[4], ("dp", "ctx"), scatter_dimension=0, tiled=True),
            lax.psum_scatter(local_grads[5], ("dp", "ctx"), scatter_dimension=1, tiled=True),
            lax.psum_scatter(local_grads[6], ("dp", "ctx"), scatter_dimension=1, tiled=True),
            lax.psum_scatter(local_grads[7], ("dp", "ctx"), scatter_dimension=0, tiled=True),
            lax.psum_scatter(local_grads[8], ("dp", "ctx"), scatter_dimension=0, tiled=True),
            lax.psum_scatter(local_grads[9], ("dp", "ctx"), scatter_dimension=0, tiled=True),
            lax.psum_scatter(local_grads[10], ("dp", "ctx"), scatter_dimension=0, tiled=True),
            lax.psum_scatter(local_grads[11], ("dp", "ctx"), scatter_dimension=0, tiled=True),
            lax.psum_scatter(local_grads[12], ("dp", "ctx"), scatter_dimension=0, tiled=True),
        )
        running = summed if running is None else jax.tree.map(jnp.add, running, summed)
    fc_bias_total = lax.psum(fc_bias_local, ("dp", "ctx"))
    (
        sum_query,
        sum_key,
        sum_value,
        sum_score,
        sum_fc,
        sum_attn_out,
        sum_proj,
        sum_gain_one,
        sum_shift_one,
        sum_gain_two,
        sum_shift_two,
        sum_attn_shift,
        sum_proj_shift,
    ) = running
    return (
        jnp.stack(outputs),
        jnp.stack(input_grads),
        sum_query,
        sum_key,
        sum_value,
        sum_score,
        sum_attn_out,
        sum_fc,
        sum_proj,
        sum_gain_one,
        sum_shift_one,
        sum_gain_two,
        sum_shift_two,
        sum_attn_shift,
        fc_bias_total,
        sum_proj_shift,
    )


def solution(mesh):
    in_specs = (
        P(None, "dp", "ctx", None),
        P(None, "dp"),
        P(("dp", "ctx"), "tensor"),
        P(("dp", "ctx"), "tensor"),
        P(("dp", "ctx"), "tensor"),
        P(("dp", "ctx"), "tensor"),
        P("tensor", ("dp", "ctx")),
        P(("dp", "ctx"), "tensor"),
        P("tensor", ("dp", "ctx")),
        P(("dp", "ctx")),
        P(("dp", "ctx")),
        P(("dp", "ctx")),
        P(("dp", "ctx")),
        P(("dp", "ctx")),
        P("tensor"),
        P(("dp", "ctx")),
        P(None, "dp", "ctx", None),
    )
    out_specs = (
        P(None, "dp", "ctx", None),
        P(None, "dp", "ctx", None),
        P(("dp", "ctx"), "tensor"),
        P(("dp", "ctx"), "tensor"),
        P(("dp", "ctx"), "tensor"),
        P(("dp", "ctx"), "tensor"),
        P("tensor", ("dp", "ctx")),
        P(("dp", "ctx"), "tensor"),
        P("tensor", ("dp", "ctx")),
        P(("dp", "ctx")),
        P(("dp", "ctx")),
        P(("dp", "ctx")),
        P(("dp", "ctx")),
        P(("dp", "ctx")),
        P("tensor"),
        P(("dp", "ctx")),
    )
    return jax.shard_map(
        on_device, mesh=mesh, in_specs=in_specs, out_specs=out_specs, check_vma=False
    )
```

profile of v0, /device:TPU:0, one launch (start us, length us, event | category | flops | bytes accessed | tf_op | source)
XLA Modules:
  0.0 2769.4 jit_solution(9530000114085247279)
XLA Ops:
  15.1 78.5 %all-reduce.13 = (bf16[768]{0:T(1024)(128)(2,1)S(1)}, bf16[768]{0:T(1024)(128)(2,1)S(1)}, bf16[768]{0:T(1024)(128)(2,1)}, bf16[768]{0:T(1024)(128)(2,1)}, bf16[768]{0:T(1024)(128)(2,1)}, /*index=5*/bf16[768]{0:T(1024)(128)(2,1)}) all-reduce(bf16[768]{0:T(1024)(128)(2,1)S(1)} %dynamic-update-slice, ...), channel_id=1, replica_groups=mesh['dp'=2,'ctx'=8,'tensor'=2] {'dp','ctx'}, use_global_device_ids=true, to_apply=%add.1 | all-reduce | flops 4608 | bytes 18432
  96.9 39.2 %all_gather.75 = bf16[768,384]{1,0:T(8,128)(2,1)S(1)} all-gather(bf16[48,384]{1,0:T(8,128)(2,1)} %param.32), channel_id=1, replica_groups=mesh['dp'=2,'ctx'=8,'tensor'=2] {'dp','ctx'}, dimensions={0}, use_global_device_ids=true | all-gather | bytes 626688 | tf_op jit(solution)/shard_map/all_gather | solution.py:155
  139.1 42.4 %all_gather.77 = bf16[768,384]{1,0:T(8,128)(2,1)S(1)} all-gather(bf16[48,384]{1,0:T(8,128)(2,1)S(1)} %copy-done.67), channel_id=1, replica_groups=mesh['dp'=2,'ctx'=8,'tensor'=2] {'dp','ctx'}, dimensions={0}, use_global_device_ids=true | all-gather | bytes 626688 | tf_op jit(solution)/shard_map/all_gather | solution.py:156
  183.5 36.3 %all-gather.6 = bf16[16,48,6]{1,2,0:T(8,128)(2,1)S(1)} all-gather(bf16[1,48,6]{1,2,0:T(8,128)(2,1)S(1)} %bitcast.634), channel_id=1, replica_groups=mesh['dp'=2,'ctx'=8,'tensor'=2] {'dp','ctx'}, dimensions={0}, use_global_device_ids=true | all-gather | bytes 9792 | tf_op jit(solution)/shard_map/all_gather | solution.py:157
  219.9 41.1 %all_gather.74 = bf16[768,384]{1,0:T(8,128)(2,1)S(1)} all-gather(bf16[48,384]{1,0:T(8,128)(2,1)S(1)} %copy-done.68), channel_id=1, replica_groups=mesh['dp'=2,'ctx'=8,'tensor'=2] {'dp','ctx'}, dimensions={0}, use_global_device_ids=true | all-gather | bytes 626688 | tf_op jit(solution)/shard_map/all_gather | solution.py:154
  263.6 30.5 %all-gather = bf16[2048,6]{0,1:T(8,128)(2,1)S(1)} all-gather(bf16[256,6]{0,1:T(8,128)(2,1)S(1)} %convolution_convert_fusion.15), channel_id=2, replica_groups=mesh['dp'=2,'ctx'=8,'tensor'=2] {'ctx'}, dimensions={0}, use_global_device_ids=true | all-gather | bytes 27648 | tf_op jit(solution)/shard_map/all_gather | solution.py:203
  294.7 40.5 %all_gather.79 = bf16[384,768]{0,1:T(8,128)(2,1)S(1)} all-gather(bf16[384,48]{0,1:T(8,128)(2,1)S(1)} %copy-done.69), channel_id=1, replica_groups=mesh['dp'=2,'ctx'=8,'tensor'=2] {'dp','ctx'}, dimensions={1}, use_global_device_ids=true | all-gather | bytes 626688 | tf_op jit(solution)/shard_map/all_gather | solution.py:159
  347.2 317.9 %while.87 = (s32[]{:T(128)}, bf16[6,256,64]{1,2,0:T(8,128)(2,1)}, f32[6,256]{1,0:T(8,128)}, f32[6,256]{1,0:T(8,128)}, s32[]{:T(128)}, /*index=5*/s32[6]{0:T(128)...) while((s32[]{:T(128)}, bf16[6,256,64]{1,2,0:T(8,128)(2,1)}, ...), condition=%wide.region_9.10_spmd, body=%wide.region_2.9_spmd.sunk | while | flops 159390720 | bytes 9643897 | solution.py:210
  349.1 3.3 select_reduce_fusion.14
  352.5 38.4 %while.92 = (s32[]{:T(128)}, f32[256]{0:T(256)S(1)}, f32[256]{0:T(256)S(1)}, f32[1,2048]{1,0:T(1,128)S(1)}, pred[2048]{0:T(1024)(128)(4,1)S(1)}, /*index=5*/s32[256]{0:T(256)S(1)}, s32[]{:T(128)}, s32[]{:T(128)}) while((s32[]{:T(128)}, f32[256]{0:T(256)S(1)}, f32[256]{0:T(256)S(1)}, f32[1,2048]{1,0:T(1,128)S(1)}, ...), condition=%wide.region_6.6_spmd.clone, body=%wide.region_4.5_spmd.clone.sunk | while | flops 6818307 | bytes 21608 | solution.py:57
  402.1 3.3 select_reduce_fusion.14
  405.4 38.4 %while.92 = (s32[]{:T(128)}, f32[256]{0:T(256)S(1)}, f32[256]{0:T(256)S(1)}, f32[1,2048]{1,0:T(1,128)S(1)}, pred[2048]{0:T(1024)(128)(4,1)S(1)}, /*index=5*/s32[256]{0:T(256)S(1)}, s32[]{:T(128)}, s32[]{:T(128)}) while((s32[]{:T(128)}, f32[256]{0:T(256)S(1)}, f32[256]{0:T(256)S(1)}, f32[1,2048]{1,0:T(1,128)S(1)}, ...), condition=%wide.region_6.6_spmd.clone, body=%wide.region_4.5_spmd.clone.sunk | while | flops 6818307 | bytes 21608 | solution.py:57
  455.1 3.3 select_reduce_fusion.14
  458.4 38.4 %while.92 = (s32[]{:T(128)}, f32[256]{0:T(256)S(1)}, f32[256]{0:T(256)S(1)}, f32[1,2048]{1,0:T(1,128)S(1)}, pred[2048]{0:T(1024)(128)(4,1)S(1)}, /*index=5*/s32[256]{0:T(256)S(1)}, s32[]{:T(128)}, s32[]{:T(128)}) while((s32[]{:T(128)}, f32[256]{0:T(256)S(1)}, f32[256]{0:T(256)S(1)}, f32[1,2048]{1,0:T(1,128)S(1)}, ...), condition=%wide.region_6.6_spmd.clone, body=%wide.region_4.5_spmd.clone.sunk | while | flops 6818307 | bytes 21608 | solution.py:57
  508.1 3.3 select_reduce_fusion.14
  511.4 38.4 %while.92 = (s32[]{:T(128)}, f32[256]{0:T(256)S(1)}, f32[256]{0:T(256)S(1)}, f32[1,2048]{1,0:T(1,128)S(1)}, pred[2048]{0:T(1024)(128)(4,1)S(1)}, /*index=5*/s32[256]{0:T(256)S(1)}, s32[]{:T(128)}, s32[]{:T(128)}) while((s32[]{:T(128)}, f32[256]{0:T(256)S(1)}, f32[256]{0:T(256)S(1)}, f32[1,2048]{1,0:T(1,128)S(1)}, ...), condition=%wide.region_6.6_spmd.clone, body=%wide.region_4.5_spmd.clone.sunk | while | flops 6818307 | bytes 21608 | solution.py:57
  561.1 3.3 select_reduce_fusion.14
  564.4 38.4 %while.92 = (s32[]{:T(128)}, f32[256]{0:T(256)S(1)}, f32[256]{0:T(256)S(1)}, f32[1,2048]{1,0:T(1,128)S(1)}, pred[2048]{0:T(1024)(128)(4,1)S(1)}, /*index=5*/s32[256]{0:T(256)S(1)}, s32[]{:T(128)}, s32[]{:T(128)}) while((s32[]{:T(128)}, f32[256]{0:T(256)S(1)}, f32[256]{0:T(256)S(1)}, f32[1,2048]{1,0:T(1,128)S(1)}, ...), condition=%wide.region_6.6_spmd.clone, body=%wide.region_4.5_spmd.clone.sunk | while | flops 6818307 | bytes 21608 | solution.py:57
  614.1 3.3 select_reduce_fusion.14
  617.4 38.4 %while.92 = (s32[]{:T(128)}, f32[256]{0:T(256)S(1)}, f32[256]{0:T(256)S(1)}, f32[1,2048]{1,0:T(1,128)S(1)}, pred[2048]{0:T(1024)(128)(4,1)S(1)}, /*index=5*/s32[256]{0:T(256)S(1)}, s32[]{:T(128)}, s32[]{:T(128)}) while((s32[]{:T(128)}, f32[256]{0:T(256)S(1)}, f32[256]{0:T(256)S(1)}, f32[1,2048]{1,0:T(1,128)S(1)}, ...), condition=%wide.region_6.6_spmd.clone, body=%wide.region_4.5_spmd.clone.sunk | while | flops 6818307 | bytes 21608 | solution.py:57
  668.9 14.4 all-reduce.21.cloned.1.call-done
  689.6 32.5 %all-gather.3 = bf16[2048,6]{0,1:T(8,128)(2,1)} all-gather(bf16[256,6]{0,1:T(8,128)(2,1)S(1)} %convolution_convert_fusion.14), channel_id=5, replica_groups=mesh['dp'=2,'ctx'=8,'tensor'=2] {'ctx'}, dimensions={0}, use_global_device_ids=true | all-gather | bytes 27648 | tf_op jit(solution)/shard_map/all_gather | solution.py:203
  722.1 9.9 all-gather.22.cloned.1.call-done
  736.4 41.4 %all-gather.24.cloned.1.call-done = bf16[2048,384]{1,0:T(8,128)(2,1)} async-done(((bf16[256,384]{1,0:T(8,128)(2,1)}), bf16[2048,384]{1,0:T(8,128)(2,1)}) %all-gather.24.cloned.1.call-update) | async-done | bytes 1572880 | tf_op jit(solution)/shard_map/all_gather | solution.py:202
  784.8 307.0 %while.89 = (s32[]{:T(128)}, bf16[6,256,64]{1,2,0:T(8,128)(2,1)}, f32[6,256]{1,0:T(8,128)S(1)}, f32[6,256]{1,0:T(8,128)}, s32[]{:T(128)}, /*index=5*/s32[6]{0:T(...) while((s32[]{:T(128)}, bf16[6,256,64]{1,2,0:T(8,128)(2,1)}, ...), condition=%wide.region_23.24_spmd, body=%wide.region_16.23_spmd.sunk | while | flops 159390720 | bytes 9639773 | solution.py:210
  786.8 3.3 select_reduce_fusion.15
  790.9 38.4 %while.93 = (s32[]{:T(128)}, f32[256]{0:T(256)S(1)}, f32[256]{0:T(256)S(1)}, f32[1,2048]{1,0:T(1,128)S(1)}, pred[2048]{0:T(1024)(128)(4,1)S(1)}, /*index=5*/s32[256]{0:T(256)S(1)}, s32[]{:T(128)}, s32[]{:T(128)}) while((s32[]{:T(128)}, f32[256]{0:T(256)S(1)}, f32[256]{0:T(256)S(1)}, f32[1,2048]{1,0:T(1,128)S(1)}, ...), condition=%wide.region_20.20_spmd.clone, body=%wide.region_18.19_spmd.clone.sunk | while | flops 6818307 | bytes 21608 | solution.py:57
  837.9 3.3 select_reduce_fusion.15
  842.0 38.4 %while.93 = (s32[]{:T(128)}, f32[256]{0:T(256)S(1)}, f32[256]{0:T(256)S(1)}, f32[1,2048]{1,0:T(1,128)S(1)}, pred[2048]{0:T(1024)(128)(4,1)S(1)}, /*index=5*/s32[256]{0:T(256)S(1)}, s32[]{:T(128)}, s32[]{:T(128)}) while((s32[]{:T(128)}, f32[256]{0:T(256)S(1)}, f32[256]{0:T(256)S(1)}, f32[1,2048]{1,0:T(1,128)S(1)}, ...), condition=%wide.region_20.20_spmd.clone, body=%wide.region_18.19_spmd.clone.sunk | while | flops 6818307 | bytes 21608 | solution.py:57
  889.1 3.3 select_reduce_fusion.15
  893.2 38.4 %while.93 = (s32[]{:T(128)}, f32[256]{0:T(256)S(1)}, f32[256]{0:T(256)S(1)}, f32[1,2048]{1,0:T(1,128)S(1)}, pred[2048]{0:T(1024)(128)(4,1)S(1)}, /*index=5*/s32[256]{0:T(256)S(1)}, s32[]{:T(128)}, s32[]{:T(128)}) while((s32[]{:T(128)}, f32[256]{0:T(256)S(1)}, f32[256]{0:T(256)S(1)}, f32[1,2048]{1,0:T(1,128)S(1)}, ...), condition=%wide.region_20.20_spmd.clone, body=%wide.region_18.19_spmd.clone.sunk | while | flops 6818307 | bytes 21608 | solution.py:57
  940.3 3.3 select_reduce_fusion.15
  944.3 38.4 %while.93 = (s32[]{:T(128)}, f32[256]{0:T(256)S(1)}, f32[256]{0:T(256)S(1)}, f32[1,2048]{1,0:T(1,128)S(1)}, pred[2048]{0:T(1024)(128)(4,1)S(1)}, /*index=5*/s32[256]{0:T(256)S(1)}, s32[]{:T(128)}, s32[]{:T(128)}) while((s32[]{:T(128)}, f32[256]{0:T(256)S(1)}, f32[256]{0:T(256)S(1)}, f32[1,2048]{1,0:T(1,128)S(1)}, ...), condition=%wide.region_20.20_spmd.clone, body=%wide.region_18.19_spmd.clone.sunk | while | flops 6818307 | bytes 21608 | solution.py:57
  991.4 3.3 select_reduce_fusion.15
  995.5 38.4 %while.93 = (s32[]{:T(128)}, f32[256]{0:T(256)S(1)}, f32[256]{0:T(256)S(1)}, f32[1,2048]{1,0:T(1,128)S(1)}, pred[2048]{0:T(1024)(128)(4,1)S(1)}, /*index=5*/s32[256]{0:T(256)S(1)}, s32[]{:T(128)}, s32[]{:T(128)}) while((s32[]{:T(128)}, f32[256]{0:T(256)S(1)}, f32[256]{0:T(256)S(1)}, f32[1,2048]{1,0:T(1,128)S(1)}, ...), condition=%wide.region_20.20_spmd.clone, body=%wide.region_18.19_spmd.clone.sunk | while | flops 6818307 | bytes 21608 | solution.py:57
  1042.6 3.3 select_reduce_fusion.15
  1046.7 38.4 %while.93 = (s32[]{:T(128)}, f32[256]{0:T(256)S(1)}, f32[256]{0:T(256)S(1)}, f32[1,2048]{1,0:T(1,128)S(1)}, pred[2048]{0:T(1024)(128)(4,1)S(1)}, /*index=5*/s32[256]{0:T(256)S(1)}, s32[]{:T(128)}, s32[]{:T(128)}) while((s32[]{:T(128)}, f32[256]{0:T(256)S(1)}, f32[256]{0:T(256)S(1)}, f32[1,2048]{1,0:T(1,128)S(1)}, ...), condition=%wide.region_20.20_spmd.clone, body=%wide.region_18.19_spmd.clone.sunk | while | flops 6818307 | bytes 21608 | solution.py:57
  1097.7 13.8 all-reduce.23.cloned.1.call-done
  1114.2 44.5 %all-gather.14.cloned.1.call-done = bf16[768,1536]{1,0:T(8,128)(2,1)} async-done(((bf16[48,1536]{1,0:T(8,128)(2,1)}), bf16[768,1536]{1,0:T(8,128)(2,1)}) %all-gather.14.cloned.1.call-update) | async-done | bytes 2359312 | tf_op jit(solution)/shard_map/all_gather | solution.py:158
  1158.7 3.8 convolution_add_fusion.2
  1164.6 57.6 %all-gather.16.cloned.1.call-done = bf16[1536,768]{0,1:T(8,128)(2,1)} async-done(((bf16[1536,48]{0,1:T(8,128)(2,1)}), bf16[1536,768]{0,1:T(8,128)(2,1)}) %all-gather.16.cloned.1.call-update) | async-done | bytes 2359312 | tf_op jit(solution)/shard_map/all_gather | solution.py:160
  1222.2 4.3 convert_reduce_fusion.1
  1233.7 17.6 all-reduce.27.cloned.1.call-done
  1261.7 109.7 %while.90 = (s32[]{:T(128)}, bf16[6,256,64]{1,2,0:T(8,128)(2,1)S(1)}, bf16[6,2048,64]{1,2,0:T(8,128)(2,1)}, bf16[6,2048,64]{1,2,0:T(8,128)(2,1)}, bf16[6,2048]{1...) while((s32[]{:T(128)}, ...), condition=%wide.region_35.36_spmd, body=%wide.region_31.35_spmd.sunk | while | flops 376588288 | bytes 18711228 | solution.py:266
  1267.6 3.3 multiply_reduce_fusion.6
  1373.7 109.9 %while.91 = (s32[]{:T(128)}, bf16[6,256,64]{1,2,0:T(8,128)(2,1)S(1)}, bf16[6,2048,64]{1,2,0:T(8,128)(2,1)S(1)}, bf16[6,2048,64]{1,2,0:T(8,128)(2,1)}, bf16[6,204...) while((s32[]{:T(128)}, ...), condition=%wide.region_49.50_spmd, body=%wide.region_45.49_spmd.sunk | while | flops 376588288 | bytes 18711228 | solution.py:266
  1398.6 3.3 multiply_reduce_fusion.7
  1435.2 3.3 multiply_reduce_fusion.7
  1487.0 4.2 convolution_convert_fusion.2
  1495.5 43.5 %reduce-scatter.26.cloned.1.call-done = bf16[1,256,6]{1,2,0:T(8,128)(2,1)} async-done(((bf16[1,2048,6]{1,2,0:T(8,128)(2,1)}), bf16[1,256,6]{1,2,0:T(8,128)(2,1)}) %reduce-scatter.26.cloned.1.call-update) | async-done | bytes 3088 | tf_op jit(solution)/shard_map/reduce_scatter | solution.py:292
  1542.8 64.7 %reduce-scatter.22.cloned.1.call-done = bf16[1,256,384]{1,2,0:T(8,128)(2,1)} async-done(((bf16[1,2048,384]{1,2,0:T(8,128)(2,1)}), bf16[1,256,384]{1,2,0:T(8,128)(2,1)}) %reduce-scatter.22.cloned.1.call-update) | async-done | bytes 196624 | tf_op jit(solution)/shard_map/reduce_scatter | solution.py:280
  1609.7 65.8 %reduce-scatter.24.cloned.1.call-done = bf16[1,256,384]{1,2,0:T(8,128)(2,1)} async-done(((bf16[1,2048,384]{1,2,0:T(8,128)(2,1)}), bf16[1,256,384]{1,2,0:T(8,128)(2,1)}) %reduce-scatter.24.cloned.1.call-update) | async-done | bytes 196624 | tf_op jit(solution)/shard_map/reduce_scatter | solution.py:286
  1678.8 64.8 %reduce-scatter.16.cloned.1.call-done = bf16[1,256,384]{1,2,0:T(8,128)(2,1)} async-done(((bf16[1,2048,384]{1,2,0:T(8,128)(2,1)}), bf16[1,256,384]{1,2,0:T(8,128)(2,1)}) %reduce-scatter.16.cloned.1.call-update) | async-done | bytes 196624 | tf_op jit(solution)/shard_map/reduce_scatter | solution.py:280
  1745.0 66.7 %reduce-scatter.18.cloned.1.call-done = bf16[1,256,384]{1,2,0:T(8,128)(2,1)} async-done(((bf16[1,2048,384]{1,2,0:T(8,128)(2,1)}), bf16[1,256,384]{1,2,0:T(8,128)(2,1)}) %reduce-scatter.18.cloned.1.call-update) | async-done | bytes 196624 | tf_op jit(solution)/shard_map/reduce_scatter | solution.py:286
  1842.8 94.7 %reduce-scatter.40.cloned.1.call-done = f32[48,6]{1,0:T(8,128)} async-done(((f32[768,6]{1,0:T(8,128)}), f32[48,6]{1,0:T(8,128)}) %reduce-scatter.40.cloned.1.call-update) | async-done | bytes 1168
  1938.9 21.3 all-reduce.25.cloned.1.call-done
  1961.9 4.0 fusion.179
  1965.9 77.1 %all-reduce.12 = (f32[768]{0:T(1024)S(1)}, f32[768]{0:T(1024)S(1)}, f32[768]{0:T(1024)S(1)}, f32[768]{0:T(1024)S(1)}, f32[768]{0:T(1024)S(1)}, /*index=5*/f32[1536]{0:T(1024)}, f32[768]{0:T(1024)S(1)}) all-reduce(f32[768]{0:T(1024)S(1)} %add.483, f32[768]{0:T(1024)S(1)} %add.484, ...), channel_id=34, replica_groups=mesh['dp'=2,'ctx'=8,'tensor'=2] {'dp','ctx'}, use_global_device_ids=true, to_apply=%region_71.72.clone | all-reduce | flops 6144 | bytes 49152
  2052.8 38.2 %reduce-scatter.28.cloned.1.call-done = f32[48,384]{1,0:T(8,128)} async-done(((f32[768,384]{1,0:T(8,128)}), f32[48,384]{1,0:T(8,128)}) %reduce-scatter.28.cloned.1.call-update) | async-done | bytes 73744 | tf_op jit(solution)/shard_map/reduce_scatter | solution.py:352
  2090.9 128.5 %reduce-scatter.34.cloned.1.call-done = f32[384,48]{0,1:T(8,128)} async-done(((f32[384,768]{0,1:T(8,128)}), f32[384,48]{0,1:T(8,128)}) %reduce-scatter.34.cloned.1.call-update) | async-done | bytes 73744 | tf_op jit(solution)/shard_map/reduce_scatter | solution.py:357
  2219.5 128.5 %reduce-scatter.30.cloned.1.call-done = f32[48,384]{1,0:T(8,128)} async-done(((f32[768,384]{1,0:T(8,128)}), f32[48,384]{1,0:T(8,128)}) %reduce-scatter.30.cloned.1.call-update) | async-done | bytes 73744 | tf_op jit(solution)/shard_map/reduce_scatter | solution.py:353
  2348.0 128.6 %reduce-scatter.32.cloned.1.call-done = f32[48,384]{1,0:T(8,128)} async-done(((f32[768,384]{1,0:T(8,128)}), f32[48,384]{1,0:T(8,128)}) %reduce-scatter.32.cloned.1.call-update) | async-done | bytes 73744 | tf_op jit(solution)/shard_map/reduce_scatter | solution.py:354
  2476.5 142.7 %reduce-scatter.36.cloned.1.call-done = f32[48,1536]{1,0:T(8,128)} async-done(((f32[768,1536]{1,0:T(8,128)}), f32[48,1536]{1,0:T(8,128)}) %reduce-scatter.36.cloned.1.call-update) | async-done | bytes 294928 | tf_op jit(solution)/shard_map/reduce_scatter | solution.py:356
  2619.2 142.2 %reduce-scatter.38.cloned.1.call-done = f32[1536,48]{0,1:T(8,128)} async-done(((f32[1536,768]{0,1:T(8,128)}), f32[1536,48]{0,1:T(8,128)}) %reduce-scatter.38.cloned.1.call-update) | async-done | bytes 294928 | tf_op jit(solution)/shard_map/reduce_scatter | solution.py:358
  (1581 shorter events, 929.0 us)
Async XLA Ops:
  8.0 131.1 %copy-start.67 = (bf16[48,384]{1,0:T(8,128)(2,1)S(1)}, bf16[48,384]{1,0:T(8,128)(2,1)}, u32[]{:S(2)}) copy-start(bf16[48,384]{1,0:T(8,128)(2,1)} %param.33) | copy-start | bytes 110596
  8.0 327.2 %all-gather.18.cloned.1.call-start = ((), (), s32[]{:S(2)}) async-start(), calls=%async_computation.23 | async-start | bytes 1769472 | tf_op jit(solution)/shard_map/all_gather | solution.py:201
  93.6 595.6 %copy-start.48 = (f32[768]{0:T(1024)}, f32[768]{0:T(1024)S(1)}, u32[]{:S(2)}) copy-start(f32[768]{0:T(1024)S(1)} %convert_element_type.412) | copy-start | bytes 9220
  93.6 595.6 %copy-start.44 = (f32[768]{0:T(1024)}, f32[768]{0:T(1024)S(1)}, u32[]{:S(2)}) copy-start(f32[768]{0:T(1024)S(1)} %convert_element_type.411) | copy-start | bytes 9220
  95.5 86.8 %copy-start = (bf16[2,1,256,768]{3,2,1,0:T(8,128)(2,1)S(1)}, bf16[2,1,256,768]{3,2,1,0:T(8,128)(2,1)}, u32[]{:S(2)}) copy-start(bf16[2,1,256,768]{3,2,1,0:T(8,128)(2,1)} %param.29) | copy-start | bytes 2359300
  95.5 167.8 %copy-start.58 = (f32[256]{0:T(256)}, f32[256]{0:T(256)S(1)}, u32[]{:S(2)}) copy-start(f32[256]{0:T(256)S(1)} %broadcast_multiply_fusion.3) | copy-start | bytes 3076
  96.8 86.6 %copy-start.85 = (f32[256]{0:T(256)}, f32[256]{0:T(256)S(1)}, u32[]{:S(2)}) copy-start(f32[256]{0:T(256)S(1)} %fusion.167) | copy-start | bytes 3076
  96.8 166.5 %copy-start.70 = (f32[256]{0:T(256)}, f32[256]{0:T(256)S(1)}, u32[]{:S(2)}) copy-start(f32[256]{0:T(256)S(1)} %fusion.227) | copy-start | bytes 3076
  136.9 46.7 %copy-start.94 = (bf16[48,6]{0,1:T(8,128)(2,1)S(1)}, bf16[48,6]{0,1:T(8,128)(2,1)}, u32[]{:S(2)}) copy-start(bf16[48,6]{0,1:T(8,128)(2,1)} %param.34) | copy-start | bytes 1732
  139.0 80.9 %copy-start.68 = (bf16[48,384]{1,0:T(8,128)(2,1)S(1)}, bf16[48,384]{1,0:T(8,128)(2,1)}, u32[]{:S(2)}) copy-start(bf16[48,384]{1,0:T(8,128)(2,1)} %param.31) | copy-start | bytes 110596
  139.1 200.6 %all-gather.20.cloned.1.call-start = ((), (), s32[]{:S(2)}) async-start(), calls=%async_computation.24 | async-start | bytes 1769472 | tf_op jit(solution)/shard_map/all_gather | solution.py:202
  183.5 499.9 %all-reduce.21.cloned.1.call-start = ((), (), s32[]{:S(2)}) async-start(), calls=%async_computation.13 | async-start | bytes 786432 | tf_op jit(solution)/shard_map/psum | solution.py:215
  219.9 469.3 %copy-start.54 = (bf16[768,6]{0,1:T(8,128)(2,1)}, bf16[768,6]{0,1:T(8,128)(2,1)S(1)}, u32[]{:S(2)}) copy-start(bf16[768,6]{0,1:T(8,128)(2,1)S(1)} %reshape.710) | copy-start | bytes 27652
  261.8 32.3 %copy-start.96 = (s32[2,1]{0,1:T(1,128)S(1)}, s32[2,1]{0,1:T(1,128)}, u32[]{:S(2)}) copy-start(s32[2,1]{0,1:T(1,128)} %param.30) | copy-start | bytes 28
  261.8 32.9 %copy-start.69 = (bf16[384,48]{0,1:T(8,128)(2,1)S(1)}, bf16[384,48]{0,1:T(8,128)(2,1)}, u32[]{:S(2)}) copy-start(bf16[384,48]{0,1:T(8,128)(2,1)} %param.35) | copy-start | bytes 110596
  665.1 20.0 copy-start.17
  667.3 19.2 copy-start.20
  667.3 64.7 %all-gather.22.cloned.1.call-start = ((), (), s32[]{:S(2)}) async-start(), calls=%async_computation.25 | async-start | bytes 1769472 | tf_op jit(solution)/shard_map/all_gather | solution.py:201
  668.3 587.2 %copy-start.42 = (f32[768]{0:T(1024)}, f32[768]{0:T(1024)S(1)}, u32[]{:S(2)}) copy-start(f32[768]{0:T(1024)S(1)} %convert_element_type.424) | copy-start | bytes 9220
  668.9 20.3 copy-start.56
  686.4 91.5 %all-gather.24.cloned.1.call-start = ((), (), s32[]{:S(2)}) async-start(), calls=%async_computation.26 | async-start | bytes 1769472 | tf_op jit(solution)/shard_map/all_gather | solution.py:202
  687.6 423.8 %all-reduce.23.cloned.1.call-start = ((), (), s32[]{:S(2)}) async-start(), calls=%async_computation.16 | async-start | bytes 786432 | tf_op jit(solution)/shard_map/psum | solution.py:215
  784.8 310.8 %copy-start.93 = (bf16[1536]{0:T(1024)(128)(2,1)S(1)}, bf16[1536]{0:T(1024)(128)(2,1)}, u32[]{:S(2)}) copy-start(bf16[1536]{0:T(1024)(128)(2,1)} %param.43) | copy-start | bytes 9220
  1091.8 19.6 copy-start.1
  1094.0 64.7 %all-gather.14.cloned.1.call-start = ((), (), s32[]{:S(2)}) async-start(), calls=%async_computation.14 | async-start | bytes 2506752 | tf_op jit(solution)/shard_map/all_gather | solution.py:158
  1094.6 127.7 %all-gather.16.cloned.1.call-start = ((), (), s32[]{:S(2)}) async-start(), calls=%async_computation.15 | async-start | bytes 2506752 | tf_op jit(solution)/shard_map/all_gather | solution.py:160
  1095.2 156.1 %all-reduce.27.cloned.1.call-start = ((), (), s32[]{:S(2)}) async-start(), calls=%async_computation.35 | async-start | bytes 1572864 | tf_op jit(solution)/shard_map/psum | solution.py:249
  1096.3 66.2 %copy-start.50 = (f32[768]{0:T(1024)}, f32[768]{0:T(1024)S(1)}, u32[]{:S(2)}) copy-start(f32[768]{0:T(1024)S(1)} %convert_element_type.426) | copy-start | bytes 9220
  1097.0 158.5 %copy-start.46 = (f32[768]{0:T(1024)}, f32[768]{0:T(1024)S(1)}, u32[]{:S(2)}) copy-start(f32[768]{0:T(1024)S(1)} %convert_element_type.425) | copy-start | bytes 9220
  1097.7 157.8 %copy-start.61 = (f32[256]{0:T(256)}, f32[256]{0:T(256)S(1)}, u32[]{:S(2)}) copy-start(f32[256]{0:T(256)S(1)} %broadcast_multiply_fusion.2) | copy-start | bytes 3076
  1111.5 47.2 %copy-start.3 = (bf16[256,768]{1,0:T(8,128)(2,1)S(1)}, bf16[256,768]{1,0:T(8,128)(2,1)}, u32[]{:S(2)}) copy-start(bf16[256,768]{1,0:T(8,128)(2,1)} %all-reduce.23.cloned.1.call-done) | copy-start | bytes 1179652
  1112.9 142.5 %copy-start.65 = (f32[256]{0:T(256)}, f32[256]{0:T(256)S(1)}, u32[]{:S(2)}) copy-start(f32[256]{0:T(256)S(1)} %get-tuple-element.752) | copy-start | bytes 3076
  1112.9 142.5 %copy-start.75 = (f32[256]{0:T(256)}, f32[256]{0:T(256)S(1)}, u32[]{:S(2)}) copy-start(f32[256]{0:T(256)S(1)} %get-tuple-element.751) | copy-start | bytes 3076
  1114.2 141.3 %copy-start.77 = (f32[256]{0:T(256)}, f32[256]{0:T(256)S(1)}, u32[]{:S(2)}) copy-start(f32[256]{0:T(256)S(1)} %fusion.230) | copy-start | bytes 3076
  1162.5 59.7 %copy-start.9 = (bf16[2,1,256,768]{3,2,1,0:T(8,128)(2,1)S(1)}, bf16[2,1,256,768]{3,2,1,0:T(8,128)(2,1)}, u32[]{:S(2)}) copy-start(bf16[2,1,256,768]{3,2,1,0:T(8,128)(2,1)} %param.45) | copy-start | bytes 2359300
  1222.2 5.2 copy-start.100
  1233.6 260.2 %reduce-scatter.20.cloned.1.call-start = ((), (), s32[]{:S(2)}) async-start(), calls=%async_computation.19 | async-start | bytes 36864 | tf_op jit(solution)/shard_map/reduce_scatter | solution.py:292
  1372.0 167.1 %reduce-scatter.26.cloned.1.call-start = ((), (), s32[]{:S(2)}) async-start(), calls=%async_computation.22 | async-start | bytes 36864 | tf_op jit(solution)/shard_map/reduce_scatter | solution.py:292
  1483.6 9.4 copy-start.26
  1484.2 123.2 %reduce-scatter.22.cloned.1.call-start = ((), (), s32[]{:S(2)}) async-start(), calls=%async_computation.20 | async-start | bytes 1769472 | tf_op jit(solution)/shard_map/reduce_scatter | solution.py:280
  1484.8 190.6 %reduce-scatter.24.cloned.1.call-start = ((), (), s32[]{:S(2)}) async-start(), calls=%async_computation.21 | async-start | bytes 1769472 | tf_op jit(solution)/shard_map/reduce_scatter | solution.py:286
  1485.6 258.1 %reduce-scatter.16.cloned.1.call-start = ((), (), s32[]{:S(2)}) async-start(), calls=%async_computation.17 | async-start | bytes 1769472 | tf_op jit(solution)/shard_map/reduce_scatter | solution.py:280
  1486.1 325.6 %reduce-scatter.18.cloned.1.call-start = ((), (), s32[]{:S(2)}) async-start(), calls=%async_computation.18 | async-start | bytes 1769472 | tf_op jit(solution)/shard_map/reduce_scatter | solution.py:286
  1486.9 450.6 %reduce-scatter.40.cloned.1.call-start = ((), (), s32[]{:S(2)}) async-start(), calls=%async_computation.33 | async-start | bytes 417792
  1493.0 46.1 %copy-start.57 = (f32[256]{0:T(256)S(1)}, f32[256]{0:T(256)}, u32[]{:S(2)}) copy-start(f32[256]{0:T(256)} %copy-done.56) | copy-start | bytes 3076
  1493.4 114.0 %copy-start.18 = (bf16[768,384]{1,0:T(8,128)(2,1)S(1)}, bf16[768,384]{1,0:T(8,128)(2,1)}, u32[]{:S(2)}) copy-start(bf16[768,384]{1,0:T(8,128)(2,1)} %copy-done.16) | copy-start | bytes 1769476
  1495.5 179.9 %copy-start.21 = (bf16[768,384]{1,0:T(8,128)(2,1)S(1)}, bf16[768,384]{1,0:T(8,128)(2,1)}, u32[]{:S(2)}) copy-start(bf16[768,384]{1,0:T(8,128)(2,1)} %copy-done.19) | copy-start | bytes 1769476
  1542.5 417.7 %all-reduce.25.cloned.1.call-start = ((), (), s32[]{:S(2)}) async-start(), calls=%async_computation.34 | async-start | bytes 3145728 | tf_op jit(solution)/shard_map/psum | solution.py:229
  1609.7 67.4 %copy-start.55 = (bf16[768,6]{0,1:T(8,128)(2,1)S(1)}, bf16[768,6]{0,1:T(8,128)(2,1)}, u32[]{:S(2)}) copy-start(bf16[768,6]{0,1:T(8,128)(2,1)} %copy-done.54) | copy-start | bytes 27652
  1745.0 70.0 %copy-start.32 = (bf16[6,256,64]{1,2,0:T(8,128)(2,1)S(1)}, bf16[6,256,64]{1,2,0:T(8,128)(2,1)}, u32[]{:S(2)}) copy-start(bf16[6,256,64]{1,2,0:T(8,128)(2,1)} %copy-done.30) | copy-start | bytes 589828
  1745.0 70.0 %copy-start.72 = (f32[256]{0:T(256)S(1)}, f32[256]{0:T(256)}, u32[]{:S(2)}) copy-start(f32[256]{0:T(256)} %copy-done.70) | copy-start | bytes 3076
  1814.9 276.0 %reduce-scatter.28.cloned.1.call-start = ((), (), s32[]{:S(2)}) async-start(), calls=%async_computation.27 | async-start | bytes 1253376 | tf_op jit(solution)/shard_map/reduce_scatter | solution.py:352
  1817.2 402.3 %reduce-scatter.34.cloned.1.call-start = ((), (), s32[]{:S(2)}) async-start(), calls=%async_computation.30 | async-start | bytes 1253376 | tf_op jit(solution)/shard_map/reduce_scatter | solution.py:357
  1819.8 528.2 %reduce-scatter.30.cloned.1.call-start = ((), (), s32[]{:S(2)}) async-start(), calls=%async_computation.28 | async-start | bytes 1253376 | tf_op jit(solution)/shard_map/reduce_scatter | solution.py:353
  1822.4 654.1 %reduce-scatter.32.cloned.1.call-start = ((), (), s32[]{:S(2)}) async-start(), calls=%async_computation.29 | async-start | bytes 1253376 | tf_op jit(solution)/shard_map/reduce_scatter | solution.py:354
  1825.0 794.3 %reduce-scatter.36.cloned.1.call-start = ((), (), s32[]{:S(2)}) async-start(), calls=%async_computation.31 | async-start | bytes 5013504 | tf_op jit(solution)/shard_map/reduce_scatter | solution.py:356
  1830.4 931.0 %reduce-scatter.38.cloned.1.call-start = ((), (), s32[]{:S(2)}) async-start(), calls=%async_computation.32 | async-start | bytes 5013504 | tf_op jit(solution)/shard_map/reduce_scatter | solution.py:358
  1836.7 5.0 copy-start.79
  1836.7 5.5 copy-start.81
  1836.7 5.5 copy-start.82
  1836.7 123.5 %copy-start.60 = (f32[256]{0:T(256)S(1)}, f32[256]{0:T(256)}, u32[]{:S(2)}) copy-start(f32[256]{0:T(256)} %copy-done.58) | copy-start | bytes 3076
  1836.7 125.1 %copy-start.86 = (f32[256]{0:T(256)S(1)}, f32[256]{0:T(256)}, u32[]{:S(2)}) copy-start(f32[256]{0:T(256)} %copy-done.85) | copy-start | bytes 3076
  1836.7 125.1 %copy-start.88 = (f32[256]{0:T(256)S(1)}, f32[256]{0:T(256)}, u32[]{:S(2)}) copy-start(f32[256]{0:T(256)} %copy-done.87) | copy-start | bytes 3076
  1961.8 88.0 %copy-start.25 = (bf16[256,768]{1,0:T(8,128)(2,1)S(1)}, bf16[256,768]{1,0:T(8,128)(2,1)}, u32[]{:S(2)}) copy-start(bf16[256,768]{1,0:T(8,128)(2,1)} %get-tuple-element.705) | copy-start | bytes 1179652
  (65 other events, 130.7 us)
Sparse Core Ops, SparseCore 0:
  139.2 44.0 all-gather.17
  186.0 45.4 all-gather.19
  667.4 15.8 all-reduce.20
  686.5 45.4 all-gather.21
  734.8 43.0 all-gather.23
  1094.1 17.2 all-reduce.22
  1233.8 17.4 all-reduce.26
  1372.1 54.7 reduce-scatter.19
  1484.3 54.6 reduce-scatter.25
  1542.8 64.6 reduce-scatter.21
  1610.9 64.4 reduce-scatter.23
  1679.1 64.4 reduce-scatter.15
  1747.1 64.5 reduce-scatter.17
  1816.9 120.4 reduce-scatter.39
  1940.4 19.6 all-reduce.24
  1966.1 124.8 reduce-scatter.27
  2096.8 122.6 reduce-scatter.33
  2225.4 122.5 reduce-scatter.29
  2354.0 122.4 reduce-scatter.31
  2482.9 136.2 reduce-scatter.35
  2625.0 136.4 reduce-scatter.37
Sparse Core Ops, SparseCore 1:
  1097.2 61.4 all-gather.13
  1161.3 60.8 all-gather.15
where the time goes:
time: 2780 us; the launch traced here: 2770 us
  waiting for transfers between devices  1330 us (48%)
  other arithmetic  605 us (22%)
  blocking collectives  418 us (15%)
  matrix products  265 us (10%)
  local copies, waits for them, and re-layouts  119 us (4%)
    reduce_sum x288, other arithmetic, bisect(): jnp.sum(jnp.where(candidate, jax.nn.sigmoid(score_mat - centre_val[:, Non...  448 us
    unnamed x2, blocking collectives  156 us
    reduce_scatter x1, waiting for transfers between devices, on_device(): lax.psum_scatter(local_grads[4], ('dp', 'ctx'), scatter_dimension=0, tile...  143 us
    reduce_scatter x1, waiting for transfers between devices, on_device(): lax.psum_scatter(local_grads[6], ('dp', 'ctx'), scatter_dimension=1, tile...  142 us
    reduce_scatter x2, waiting for transfers between devices, on_device(): lax.psum_scatter(join_heads(grad_v_items, seq_count).astype(jnp.bfloat16)...  132 us
    reduce_scatter x2, waiting for transfers between devices, on_device(): lax.psum_scatter(join_heads(grad_k_items, seq_count).astype(jnp.bfloat16)...  129 us
    reduce_scatter x1, waiting for transfers between devices, on_device(): lax.psum_scatter(local_grads[2], ('dp', 'ctx'), scatter_dimension=0, tile...  129 us
    reduce_scatter x1, waiting for transfers between devices, on_device(): lax.psum_scatter(local_grads[5], ('dp', 'ctx'), scatter_dimension=1, tile...  129 us
  transfers between devices with their start and end apart: 23, of which 20 were waited for; matrix products, arithmetic and copies ran while one was open for 7% of the time, Pallas kernels for 0%

commit v1 on v0

v1 whole, which is shorter than its diff:
```python
from functools import partial

import jax
import jax.numpy as jnp
import numpy as np
from jax import lax
from jax.experimental import pallas as pl
from jax.experimental.pallas import tpu as pltpu
from jax.sharding import PartitionSpec as P

WIN = 64
TOPK = 64
HEAD = 64
LANES = 128

norm_epsilon = 1e-05
search_steps = 24
search_bound = 64.0

CHUNK = 256
FAR = 1e9
OPEN_PIVOT = -1e6
NEWTON_TOLERANCE = 3e-3
NT = (((1,), (1,)), ((), ()))


def over_chunks(first, rows, prefix, body, carry):
    below = lax.div(jnp.maximum(first - (WIN - 1), 0), CHUNK)
    total = lax.div(jnp.maximum(first + rows, prefix) + CHUNK - 1, CHUNK)
    above = jnp.minimum(lax.div(first + rows + WIN - 1 + CHUNK - 1, CHUNK), total)
    whole = jnp.maximum(lax.div(prefix, CHUNK), above)
    carry = lax.fori_loop(0, below, body(False), carry)
    carry = lax.fori_loop(below, above, body(True), carry)
    carry = lax.fori_loop(above, whole, body(False), carry)
    return lax.fori_loop(whole, total, body(True), carry)


def fold(values, how):
    return how(values.reshape(values.shape[0] // 8, 8, values.shape[1]), axis=0)


def own_head(values, slot):
    lane = lax.broadcasted_iota(jnp.int32, values.shape, 1)
    kept = jnp.where(lax.div(lane, HEAD) == slot, values.astype(jnp.float32), 0.0)
    return kept.astype(jnp.bfloat16)


def masks(start, first, prefix, rows):
    key = lax.broadcasted_iota(jnp.int32, (CHUNK, rows), 0)
    row = lax.broadcasted_iota(jnp.int32, (CHUNK, rows), 1)
    behind = row - key + (first - start)
    allowed = (behind >= 0) | (key < prefix - start)
    return allowed, allowed & (jnp.abs(behind) < WIN)


def forward_kernel(table, prefix_ref, p_ref, vt_ref, o_ref, lse_ref, pivot_ref, sm_ref, st_ref):
    unit_count, rows, _ = o_ref.shape
    prefix = prefix_ref[0]
    lane = lax.broadcasted_iota(jnp.int32, (1, rows), 1)

    def unit(step, guess):
        slot, first, place = table[step, 0], table[step, 1], table[step, 2]
        query = own_head(p_ref[pl.ds(pl.multiple_of(first, rows), rows), 0:LANES], slot)
        score_lane = pl.multiple_of((3 + slot) * LANES, LANES)

        def build(masked):
            def run(chunk, top):
                start = pl.multiple_of(chunk * CHUNK, CHUNK)
                here = pl.ds(start, CHUNK)
                logits = lax.dot_general(
                    p_ref[here, LANES : 2 * LANES], query, NT, preferred_element_type=jnp.float32
                )
                score = p_ref[here, pl.ds(score_lane, LANES)].astype(jnp.float32)[:, :rows]
                if masked:
                    allowed, local = masks(start, first, prefix, rows)
                    logits = jnp.where(allowed, logits, -1e30)
                    score = jnp.where(local, FAR, jnp.where(allowed, score, -FAR))
                    top = jnp.maximum(top, fold(jnp.where(local, logits, -1e30), jnp.max))
                st_ref[here, :] = logits
                sm_ref[here, :] = score
                return top

            return run

        top = over_chunks(first, rows, prefix, build, jnp.full((8, rows), -1e30, jnp.float32))
        top = jnp.max(top, axis=0, keepdims=True)

        row = first + lane
        local_count = (
            jnp.minimum(row, WIN - 1) + 1 + jnp.clip(prefix - 1 - row, 0, WIN - 1)
        ).astype(jnp.float32)
        candidates = jnp.maximum(row + 1, prefix).astype(jnp.float32) - local_count
        chunks = lax.div(jnp.maximum(first + rows, prefix) + CHUNK - 1, CHUNK)
        entries = (chunks * CHUNK).astype(jnp.float32)
        searched = candidates > TOPK
        count = jnp.maximum(candidates, TOPK + 1.0)
        goal = jnp.log(TOPK / (count - TOPK))

        def measure(half):
            def run(chunk, sums):
                bent = jnp.tanh(sm_ref[pl.ds(pl.multiple_of(chunk * CHUNK, CHUNK), CHUNK), :] - half)
                return sums[0] + fold(bent, jnp.sum), sums[1] + fold(bent * bent, jnp.sum)

            zero = jnp.zeros((8, rows), jnp.float32)
            first_sum, second_sum = lax.fori_loop(0, chunks, run, (zero, zero))
            filled = 0.5 * (entries + jnp.sum(first_sum, axis=0, keepdims=True)) - local_count
            slope = 0.25 * (entries - jnp.sum(second_sum, axis=0, keepdims=True))
            return filled, slope

        def improve(state):
            turn, _, half, lower, upper, done = state
            filled, slope = measure(half)
            above = filled > TOPK
            lower = jnp.where(above, half, lower)
            upper = jnp.where(above, upper, half)
            newton = (filled - TOPK) / slope
            held = jnp.clip(filled, 1e-3, count - 1e-3)
            bent = (jnp.log(held / (count - held)) - goal) * (held * (count - held) / (count * slope))
            close = jnp.abs(newton) <= NEWTON_TOLERANCE
            following = half + 0.5 * jnp.where(close, newton, bent)
            inside = (following > lower) & (following < upper)
            halve = (turn >= 12) & (lax.rem(turn, 2) == 1)
            middle = 0.5 * (lower + upper)
            following = jnp.where(close | (inside & jnp.logical_not(halve)), following, middle)
            half = jnp.where(done > 0.0, half, following)
            done = jnp.where(close, 1.0, done)
            return turn + 1, jnp.min(done), half, lower, upper, done

        start_done = jnp.where(searched, 0.0, 1.0)
        bound = jnp.full((1, rows), 0.5 * search_bound, jnp.float32)
        _, _, half, lower, upper, done = lax.while_loop(
            lambda state: (state[0] < 12 + 2 * search_steps) & (state[1] < 0.5),
            improve,
            (0, jnp.min(start_done), guess, -bound, bound, start_done),
        )
        half = jnp.where(done > 0.0, half, 0.5 * (lower + upper))
        pivot = jnp.where(searched, half, OPEN_PIVOT)

        def weigh(chunk, sums):
            here = pl.ds(pl.multiple_of(chunk * CHUNK, CHUNK), CHUNK)
            raised = jnp.exp(st_ref[here, :] - top)
            weight = raised / (1.0 + jnp.exp(2.0 * (pivot - sm_ref[here, :])))
            merged = sums[1] + jnp.dot(
                vt_ref[:, here], weight.astype(jnp.bfloat16), preferred_element_type=jnp.float32
            )
            return sums[0] + fold(weight, jnp.sum), merged

        total, merged = lax.fori_loop(
            0,
            chunks,
            weigh,
            (jnp.zeros((8, rows), jnp.float32), jnp.zeros((LANES, rows), jnp.float32)),
        )
        total = jnp.sum(total, axis=0, keepdims=True)
        merged = merged / total
        own = jnp.where(slot == 0, merged[:HEAD], merged[HEAD:])
        o_ref[place] = own.T
        lse_ref[place] = top + jnp.log(total)
        pivot_ref[place] = pivot
        return jnp.where(searched, half, guess)

    lax.fori_loop(0, unit_count, unit, jnp.zeros((1, rows), jnp.float32))


def backward_kernel(
    table, prefix_ref, p_ref, kt_ref, do_ref, dot_ref, lse_ref, pivot_ref, d_ref, dq_ref, dk_ref, dv_ref, ds_ref
):
    unit_count, rows, _ = do_ref.shape
    length = p_ref.shape[0]
    prefix = prefix_ref[0]

    def clear(chunk, _):
        here = pl.ds(pl.multiple_of(chunk * CHUNK, CHUNK), CHUNK)
        for ref in (dq_ref, dk_ref, dv_ref):
            ref[here, :] = jnp.zeros((CHUNK, LANES), jnp.float32)
        for slot in range(2):
            ds_ref[slot, here, :] = jnp.zeros((CHUNK, rows), jnp.float32)
        return 0

    lax.fori_loop(0, length // CHUNK, clear, 0)

    def unit(step, _):
        slot, first, place = table[step, 0], table[step, 1], table[step, 2]
        whose = pl.ds(pl.multiple_of(first, rows), rows)
        query = own_head(p_ref[whose, 0:LANES], slot)
        grad = own_head(do_ref[place], slot)
        row_dot, lse, pivot = dot_ref[place], lse_ref[place], pivot_ref[place]
        score_lane = pl.multiple_of((3 + slot) * LANES, LANES)

        def body(masked):
            def run(chunk, grad_query):
                start = pl.multiple_of(chunk * CHUNK, CHUNK)
                here = pl.ds(start, CHUNK)
                logits = lax.dot_general(
                    p_ref[here, LANES : 2 * LANES], query, NT, preferred_element_type=jnp.float32
                )
                grad_probs = lax.dot_general(
                    p_ref[here, 2 * LANES : 3 * LANES], grad, NT, preferred_element_type=jnp.float32
                )
                score = p_ref[here, pl.ds(score_lane, LANES)].astype(jnp.float32)[:, :rows]
                if masked:
                    allowed, local = masks(start, first, prefix, rows)
                    logits = jnp.where(allowed, logits, -1e30)
                    score = jnp.where(local, FAR, jnp.where(allowed, score, -FAR))
                unit_probs = jnp.exp(logits - lse)
                gate = 1.0 / (1.0 + jnp.exp(2.0 * (pivot - score)))
                probs = gate * unit_probs
                grad_logits = probs * (grad_probs - row_dot)
                ds_ref[slot, here, :] += grad_logits * (1.0 - gate)
                low = grad_logits.astype(jnp.bfloat16)
                dk_ref[here, :] += jnp.dot(low, query, preferred_element_type=jnp.float32)
                dv_ref[here, :] += jnp.dot(
                    probs.astype(jnp.bfloat16), grad, preferred_element_type=jnp.float32
                )
                return grad_query + jnp.dot(
                    kt_ref[:, here], low, preferred_element_type=jnp.float32
                )

            return run

        grad_query = over_chunks(
            first, rows, prefix, body, jnp.zeros((LANES, rows), jnp.float32)
        ).T
        lane = lax.broadcasted_iota(jnp.int32, grad_query.shape, 1)
        dq_ref[whose, :] += jnp.where(lax.div(lane, HEAD) == slot, grad_query, 0.0)
        return 0

    lax.fori_loop(0, unit_count, unit, 0)

    def finish(chunk, _):
        here = pl.ds(pl.multiple_of(chunk * CHUNK, CHUNK), CHUNK)
        d_ref[here, 0:LANES] = (dq_ref[here, :] * HEAD**-0.5).astype(jnp.bfloat16)
        d_ref[here, LANES : 2 * LANES] = dk_ref[here, :].astype(jnp.bfloat16)
        d_ref[here, 2 * LANES : 3 * LANES] = dv_ref[here, :].astype(jnp.bfloat16)
        lane = lax.broadcasted_iota(jnp.int32, (CHUNK, LANES), 1)
        columns = [jnp.sum(ds_ref[slot, here, :], axis=1, keepdims=True) for slot in range(2)]
        grad_score = jnp.where(lane == 0, columns[0], jnp.where(lane == 1, columns[1], 0.0))
        d_ref[here, 3 * LANES : 4 * LANES] = grad_score.astype(jnp.bfloat16)
        return 0

    lax.fori_loop(0, length // CHUNK, finish, 0)


VMEM_LIMIT = 48 * 1024 * 1024


def attend(table, prefix, projected, values_t, rows):
    unit_count = table.shape[0]
    length = projected.shape[0]
    smem = pl.BlockSpec(memory_space=pltpu.SMEM)
    vmem = pl.BlockSpec(memory_space=pltpu.VMEM)
    pairs = unit_count * rows * length
    return pl.pallas_call(
        forward_kernel,
        out_shape=(
            jax.ShapeDtypeStruct((unit_count, rows, HEAD), jnp.float32),
            jax.ShapeDtypeStruct((unit_count, 1, rows), jnp.float32),
            jax.ShapeDtypeStruct((unit_count, 1, rows), jnp.float32),
        ),
        in_specs=[smem, smem, vmem, vmem],
        out_specs=(vmem, vmem, vmem),
        scratch_shapes=[pltpu.VMEM((length, rows), jnp.float32), pltpu.VMEM((length, rows), jnp.float32)],
        compiler_params=pltpu.CompilerParams(vmem_limit_bytes=VMEM_LIMIT),
        cost_estimate=pl.CostEstimate(
            flops=pairs * 512, bytes_accessed=projected.size * 4, transcendentals=pairs * 8
        ),
        name="attend",
    )(table, prefix, projected, values_t)


def attend_back(table, prefix, projected, keys_t, grads, row_dots, log_totals, pivots):
    unit_count, rows, _ = grads.shape
    length = projected.shape[0]
    smem = pl.BlockSpec(memory_space=pltpu.SMEM)
    vmem = pl.BlockSpec(memory_space=pltpu.VMEM)
    pairs = unit_count * rows * length
    return pl.pallas_call(
        backward_kernel,
        out_shape=jax.ShapeDtypeStruct((length, 4 * LANES), jnp.bfloat16),
        in_specs=[smem, smem] + [vmem] * 6,
        out_specs=vmem,
        scratch_shapes=[
            pltpu.VMEM((length, LANES), jnp.float32),
            pltpu.VMEM((length, LANES), jnp.float32),
            pltpu.VMEM((length, LANES), jnp.float32),
            pltpu.VMEM((2, length, rows), jnp.float32),
        ],
        compiler_params=pltpu.CompilerParams(vmem_limit_bytes=VMEM_LIMIT),
        cost_estimate=pl.CostEstimate(
            flops=pairs * 1280, bytes_accessed=projected.size * 4, transcendentals=pairs * 3
        ),
        name="attend_back",
    )(table, prefix, projected, keys_t, grads, row_dots, log_totals, pivots)


class Grid:
    def __init__(self, count):
        self.deep = 4 if count % 4 == 0 else 1
        self.wide = count // self.deep
        self.count = count

    def index(self, place, across):
        return place * self.wide + across


def hop(values, pairs):
    return lax.ppermute(values, "ctx", pairs)


def line_gather(values, length, pair_of):
    pieces = {0: values}
    ahead = behind = values
    for step in range(1, length):
        ahead = hop(ahead, [p for s in range(step - 1, length - 1) for p in pair_of(s, s + 1)])
        behind = hop(behind, [p for s in range(1, length - step + 1) for p in pair_of(s, s - 1)])
        pieces[-step], pieces[step] = ahead, behind
    return pieces


def gather_ctx(values, grid):
    me = lax.axis_index("ctx")
    place, across = me // grid.wide, me % grid.wide
    rows = values.shape[0]

    def along(s, r):
        return [(grid.index(s, w), grid.index(r, w)) for w in range(grid.wide)]

    deep = line_gather(values, grid.deep, along)
    slots = {}
    for distance, piece in deep.items():
        held = [z for z in range(grid.deep) if 0 <= z + distance < grid.deep]

        def sideways(s, r, held=held):
            return [(grid.index(z, s), grid.index(z, r)) for z in held]

        for shift, part in line_gather(piece, grid.wide, sideways).items():
            slot = (distance % grid.deep, shift % grid.wide)
            slots[slot] = part if slot not in slots else slots[slot] + part
    whole = jnp.zeros((rows * grid.count,) + values.shape[1:], values.dtype)
    for (distance, shift), part in slots.items():
        target = grid.index((place + distance) % grid.deep, (across + shift) % grid.wide)
        whole = lax.dynamic_update_slice_in_dim(whole, part, target * rows, 0)
    return whole


def line_scatter(block, length, place, pair_of):
    ahead = behind = None
    for step in range(length - 1, 0, -1):
        outgoing = block(step) if ahead is None else (block(step) + ahead)
        ahead = hop(
            outgoing.astype(jnp.bfloat16), [p for s in range(length - step) for p in pair_of(s, s + 1)]
        ).astype(jnp.float32)
        outgoing = block(-step) if behind is None else (block(-step) + behind)
        behind = hop(
            outgoing.astype(jnp.bfloat16), [p for s in range(step, length) for p in pair_of(s, s - 1)]
        ).astype(jnp.float32)
    total = block(0)
    return total if ahead is None else total + ahead + behind


def scatter_ctx(values, grid):
    me = lax.axis_index("ctx")
    place, across = me // grid.wide, me % grid.wide
    rows = values.shape[0] // grid.count

    def sideways(s, r):
        return [(grid.index(z, s), grid.index(z, r)) for z in range(grid.deep)]

    def along(s, r):
        return [(grid.index(s, w), grid.index(r, w)) for w in range(grid.wide)]

    lines = {}
    order = sorted(range(grid.deep), key=lambda d: -abs(d - grid.deep / 2 + 0.1))
    for distance in [d for d in order if d] + [0]:
        target = (place + distance) % grid.deep

        def block(shift, target=target):
            which = grid.index(target, (across + shift) % grid.wide)
            return lax.dynamic_slice_in_dim(values, which * rows, rows, 0).astype(jnp.float32)

        lines[distance] = line_scatter(block, grid.wide, across, sideways)
    return line_scatter(lambda d: lines[d % grid.deep], grid.deep, place, along)


def other_core(values):
    return lax.ppermute(values, "tensor", [(0, 1), (1, 0)])


def normalize(values):
    centred = values - jnp.mean(values, axis=-1, keepdims=True)
    scale = lax.rsqrt(jnp.mean(centred * centred, axis=-1, keepdims=True) + norm_epsilon)
    return centred * scale, scale


def normalize_back(grad, hat, scale, gain):
    scaled = grad * gain
    return scale * (
        scaled
        - jnp.mean(scaled, axis=-1, keepdims=True)
        - hat * jnp.mean(scaled * hat, axis=-1, keepdims=True)
    )


def head_plan(ctx_count, head_count, block):
    parts = 1
    while head_count * parts % ctx_count:
        parts += 1
    share = head_count * parts // ctx_count
    rows = block // parts
    lows, tables = [], []
    for device in range(ctx_count):
        pieces = range(share * device, share * (device + 1))
        lows.append(pieces[0] // parts)
        tables.append(
            [
                (piece // parts - lows[-1], at * block + (piece % parts) * rows, at * share + order)
                for order, piece in enumerate(pieces)
                for at in range(ctx_count)
            ]
        )
        assert all(entry[0] in (0, 1) for entry in tables[-1])
    return parts, share, rows, lows, np.asarray(tables, np.int32)


def on_device(
    tokens,
    prefix,
    w_query,
    w_key,
    w_value,
    w_score,
    w_attn_out,
    w_fc,
    w_proj,
    ln1_gain,
    ln1_bias,
    ln2_gain,
    ln2_bias,
    attn_bias,
    fc_bias,
    proj_bias,
    cotangent,
    dp_count,
    ctx_count,
):
    f32, bf16 = jnp.float32, jnp.bfloat16
    micro_count, seq_count, block, width = tokens.shape
    local_heads = w_score.shape[1]
    head_count = 2 * local_heads
    assert micro_count == 2 and seq_count == 1
    core = lax.axis_index("tensor")
    me = lax.axis_index("ctx")
    grid = Grid(ctx_count)
    both = ("dp", "ctx")
    shards = dp_count * ctx_count
    shard_rows = width // shards
    parts, share, rows, lows, tables = head_plan(ctx_count, head_count, block)
    near = ctx_count // 2
    local_low = [low % local_heads for low in lows[:near]]
    local_high = [min(low + 1, local_heads - 1) for low in local_low]

    own_tokens = lax.dynamic_index_in_dim(tokens, core, 0, keepdims=False)[0]
    own_cot = lax.dynamic_index_in_dim(cotangent, core, 0, keepdims=False)[0]
    other_cot = lax.dynamic_index_in_dim(cotangent, 1 - core, 0, keepdims=False)[0]
    own_prefix = lax.dynamic_index_in_dim(prefix, core, 0, keepdims=False)
    table = jnp.asarray(tables)[me]

    all_tokens = gather_ctx(own_tokens, grid)

    vectors = jnp.stack([ln1_gain, ln1_bias, ln2_gain, ln2_bias, attn_bias, proj_bias], axis=1)
    spare = jnp.zeros((shard_rows, LANES - 2 - vectors.shape[1]), bf16)

    def columns(weight, head):
        return weight[:, head * HEAD : (head + 1) * HEAD]

    outgoing = jnp.stack(
        [
            jnp.concatenate(
                [columns(w, h) for w in (w_query, w_key, w_value) for h in (low, high)]
                + [w_score[:, low : low + 1], w_score[:, high : high + 1], vectors, spare],
                axis=1,
            )
            for low, high in zip(local_low, local_high)
        ]
    )
    outgoing = jnp.tile(outgoing, (2 * dp_count, 1, 1))
    head_weights = lax.all_to_all(outgoing, both, 0, 0, tiled=True).reshape(width, 4 * LANES)
    from_half = (me >= near).astype(jnp.int32)
    head_weights = jnp.where(from_half == core, head_weights, other_core(head_weights))
    gains = head_weights[:, 3 * LANES + 2 : 3 * LANES + 8].astype(f32).T
    gain_one, shift_one, gain_two, shift_two, attn_shift, proj_shift = [gains[i : i + 1] for i in range(6)]

    packed = jnp.concatenate([w_fc, w_proj.T, w_attn_out.T], axis=1)
    packed = lax.all_gather(packed, both, axis=0, tiled=True)
    hidden = w_fc.shape[1]
    full_fc, full_proj_t, half_out_t = packed[:, :hidden], packed[:, hidden : 2 * hidden], packed[:, 2 * hidden :]
    other_out_t = other_core(half_out_t)
    out_t = jnp.where(
        core == 0,
        jnp.concatenate([half_out_t, other_out_t], axis=1),
        jnp.concatenate([other_out_t, half_out_t], axis=1),
    )

    hat_one, scale_one = normalize(all_tokens.astype(f32))
    normed = (hat_one * gain_one + shift_one).astype(bf16)
    w_q, w_k, w_v = [head_weights[:, i * LANES : (i + 1) * LANES] for i in range(3)]
    score_columns = head_weights[:, 3 * LANES : 3 * LANES + 2]
    wide_weights = jnp.concatenate(
        [w_q * HEAD**-0.5, w_k, w_v]
        + [jnp.broadcast_to(score_columns[:, i : i + 1], (width, LANES)) for i in range(2)],
        axis=1,
    )
    projected = jnp.dot(normed, wide_weights, preferred_element_type=f32).astype(bf16)
    halver = jnp.where(jnp.arange(5 * LANES) < 3 * LANES, 1.0, 0.5).astype(bf16)
    projected = projected * halver
    turned = lax.dot_general(
        head_weights[:, LANES : 3 * LANES], normed, (((0,), (1,)), ((), ())), preferred_element_type=f32
    ).astype(bf16)
    keys_t, values_t = turned[:LANES], turned[LANES:]

    attended, log_totals, pivots = attend(table, own_prefix, projected, values_t, rows)

    sent = attended.astype(bf16).reshape(ctx_count, share * rows * HEAD // LANES, LANES)
    merged = lax.all_to_all(sent, "ctx", 0, 0, tiled=True)
    merged = merged.reshape(head_count, parts, rows, HEAD).transpose(1, 2, 0, 3).reshape(block, width)

    own_block = own_tokens.astype(f32)
    attn = lax.dot_general(merged, out_t, NT, preferred_element_type=f32)
    middle = own_block + attn + attn_shift
    hat_two, scale_two = normalize(middle)
    normed_two = (hat_two * gain_two + shift_two).astype(bf16)
    normed_two = jnp.concatenate([normed_two, other_core(normed_two)])
    hidden_pre = jnp.dot(normed_two, full_fc, preferred_element_type=f32) + fc_bias.astype(f32)
    active, pull_gelu = jax.vjp(partial(jax.nn.gelu, approximate=True), hidden_pre)
    active = active.astype(bf16)
    mlp = lax.dot_general(active, full_proj_t, NT, preferred_element_type=f32)
    result = middle + mlp[:block] + other_core(mlp[block:].astype(bf16)).astype(f32) + proj_shift
    result = result.astype(bf16)

    both_cot = jnp.concatenate([own_cot, other_cot])
    grad_active = jnp.dot(both_cot, full_proj_t, preferred_element_type=f32)
    grad_pre = pull_gelu(grad_active)[0].astype(bf16)
    grad_two = lax.dot_general(grad_pre, full_fc, NT, preferred_element_type=f32)
    grad_two = grad_two[:block] + other_core(grad_two[block:].astype(bf16)).astype(f32)
    cot = own_cot.astype(f32)
    grad_middle = cot + normalize_back(grad_two, hat_two, scale_two, gain_two)
    grad_middle_low = grad_middle.astype(bf16)
    grad_merged = jnp.dot(grad_middle_low, out_t, preferred_element_type=f32).astype(bf16)

    sent = grad_merged.reshape(parts, rows, head_count, HEAD).transpose(2, 0, 1, 3)
    sent = sent.reshape(ctx_count, share * rows * HEAD // LANES, LANES)
    grad_attended = lax.all_to_all(sent, "ctx", 0, 0, tiled=True).reshape(attended.shape)

    grad_fc = lax.dot_general(normed_two, grad_pre, (((0,), (0,)), ((), ())), preferred_element_type=f32)
    grad_proj_t = lax.dot_general(both_cot, active, (((0,), (0,)), ((), ())), preferred_element_type=f32)
    grad_out_t = lax.dot_general(
        grad_middle_low, merged, (((0,), (0,)), ((), ())), preferred_element_type=f32
    ).astype(bf16)
    half_width = width // 2
    mine, theirs = grad_out_t[:, :half_width], grad_out_t[:, half_width:]
    mine, theirs = jnp.where(core == 0, mine, theirs), jnp.where(core == 0, theirs, mine)
    grad_out_t = (mine.astype(f32) + other_core(theirs).astype(f32)).astype(bf16)
    grad_packed = jnp.concatenate([grad_fc.astype(bf16), grad_proj_t.astype(bf16), grad_out_t], axis=1)
    grad_packed = lax.psum_scatter(grad_packed, both, scatter_dimension=0, tiled=True).astype(f32)
    fc_bias_grad = lax.psum(jnp.sum(grad_pre.astype(f32), axis=0), both)

    row_dots = jnp.sum(attended * grad_attended.astype(f32), axis=-1)[:, None, :]
    doubled = jnp.concatenate([grad_attended, grad_attended], axis=-1)
    grads = attend_back(table, own_prefix, projected, keys_t, doubled, row_dots, log_totals, pivots)

    grad_normed = lax.dot_general(grads, head_weights, NT, preferred_element_type=f32)
    grad_one = scatter_ctx(grad_normed.astype(bf16), grid)
    own_hat, own_scale = normalize(own_block)
    tokens_grad = grad_middle + normalize_back(grad_one, own_hat, own_scale, gain_one)

    grad_vectors = jnp.stack(
        [
            jnp.sum(grad_normed * hat_one, axis=0),
            jnp.sum(grad_normed, axis=0),
            jnp.sum(grad_two * hat_two, axis=0),
            jnp.sum(grad_two, axis=0),
            jnp.sum(grad_middle, axis=0),
            jnp.sum(cot, axis=0),
        ],
        axis=1,
    )
    grad_heads = lax.dot_general(normed, grads, (((0,), (0,)), ((), ())), preferred_element_type=f32)
    grad_heads = jnp.concatenate(
        [grad_heads[:, : 3 * LANES + 2], grad_vectors, jnp.zeros((width, LANES - 8), f32)], axis=1
    )
    grad_heads = grad_heads + other_core(grad_heads.astype(bf16)).astype(f32)
    grad_heads = grad_heads.astype(bf16).reshape(shards, shard_rows, 4 * LANES)
    grad_heads = lax.all_to_all(grad_heads, both, 0, 0, tiled=True)
    grad_heads = grad_heads.reshape(dp_count, ctx_count, shard_rows, 4 * LANES).astype(f32)
    vector_grads = jnp.sum(grad_heads[..., 3 * LANES + 2 : 3 * LANES + 8], axis=(0, 1))
    from_own = lax.dynamic_slice_in_dim(grad_heads, core * near, near, 1)
    from_own = jnp.sum(from_own, axis=0)
    pieces = [[[] for _ in range(local_heads)] for _ in range(4)]
    used = [sorted({entry[0] for entry in tables[device].tolist()}) for device in range(near)]
    for device in range(near):
        for slot in used[device]:
            head = local_low[device] + slot
            for kind in range(3):
                at = kind * LANES + slot * HEAD
                pieces[kind][head].append(from_own[device, :, at : at + HEAD])
            at = 3 * LANES + slot
            pieces[3][head].append(from_own[device, :, at : at + 1])
    grad_query, grad_key, grad_value, grad_score = [
        jnp.concatenate([sum(terms[1:], terms[0]) for terms in kind], axis=1) for kind in pieces
    ]

    def both_micro(own):
        other = other_core(own)
        return jnp.where(core == 0, jnp.stack([own, other]), jnp.stack([other, own]))[:, None]

    return (
        both_micro(result),
        both_micro(tokens_grad),
        grad_query,
        grad_key,
        grad_value,
        grad_score,
        grad_packed[:, 2 * hidden :].T,
        grad_packed[:, :hidden],
        grad_packed[:, hidden : 2 * hidden].T,
        vector_grads[:, 0],
        vector_grads[:, 1],
        vector_grads[:, 2],
        vector_grads[:, 3],
        vector_grads[:, 4],
        fc_bias_grad,
        vector_grads[:, 5],
    )


def solution(mesh):
    rows, columns, vector = P(("dp", "ctx"), "tensor"), P("tensor", ("dp", "ctx")), P(("dp", "ctx"))
    tokens = P(None, "dp", "ctx", None)
    in_specs = (
        (tokens, P(None, "dp"))
        + (rows,) * 4
        + (columns, rows, columns)
        + (vector,) * 5
        + (P("tensor"), vector, tokens)
    )
    out_specs = (
        (tokens, tokens)
        + (rows,) * 4
        + (columns, rows, columns)
        + (vector,) * 5
        + (P("tensor"), vector)
    )
    return jax.shard_map(
        partial(on_device, dp_count=mesh.shape["dp"], ctx_count=mesh.shape["ctx"]),
        mesh=mesh,
        in_specs=in_specs,
        out_specs=out_specs,
        check_vma=False,
    )
```

time: 2780 us -> 551 us (0.20)
  waiting for transfers between devices: 1330 us -> 92.7 us
  other arithmetic: 605 us -> 62.2 us
  blocking collectives: 418 us -> 52.3 us
  matrix products: 265 us -> 30.7 us
  starting transfers between devices: 2.1 us -> 122 us
  Pallas kernels: 0 us -> 115 us
  local copies, waits for them, and re-layouts: 119 us -> 53.1 us
    reduce_scatter x12 -> x1, waiting for transfers between devices: 1010 us -> 0.01 us  [on_device(): lax.psum_scatter(grad_packed, both, scatter_dimension=0, tiled=True)]
    reduce_sum x335 -> x12, other arithmetic: 552 us -> 14.1 us  [the longest x2 4.06 us: normalize(): centred = values - jnp.mean(values, axis=-1, keepdims=True)]
    all_gather x7 -> x0, blocking collectives: 262 us -> none  [the longest x2 63 us: on_device(): lax.all_gather(scores_low.reshape(seq_count, tok_count, -1), 'ctx', axis=...]
    dot_general x126 -> x13, matrix products: 265 us -> 30.7 us  [the longest x1 3.83 us: on_device(): lax.dot_general(grads, head_weights, NT, preferred_element_type=f32)]
    unnamed x2 -> x0, blocking collectives: 156 us -> none
    all_gather x6 -> x1, waiting for transfers between devices: 153 us -> 0.02 us  [on_device(): packed = lax.all_gather(packed, both, axis=0, tiled=True)]
    pallas_call x0 -> x2, Pallas kernels: none -> 115 us  [the longest x1 68.5 us: attend(): pl.pallas_call(forward_kernel, out_shape=(jax.ShapeDtypeStruct((unit_coun...]
    unnamed x24 -> x2, waiting for transfers between devices: 97.9 us -> 0.03 us
  transfers between devices with their start and end apart: 23 -> 49, of which waited for: 20 -> 11; matrix products, arithmetic and copies ran while one was open for 7% -> 20% of each run, Pallas kernels for 0% -> 21%
where the time goes in v1:
time: 551 us; the launch traced here: 543 us
  starting transfers between devices  122 us (22%)
  Pallas kernels  115 us (21%)
  waiting for transfers between devices  92.7 us (17%)
  other arithmetic  62.2 us (11%)
  local copies, waits for them, and re-layouts  53.1 us (10%)
  blocking collectives  52.3 us (9%)
  matrix products  30.7 us (6%)
  between operations  15.5 us (3%)
    ppermute x34, starting transfers between devices, hop(): return lax.ppermute(values, 'ctx', pairs)  74.6 us
    ppermute x34, waiting for transfers between devices, hop(): return lax.ppermute(values, 'ctx', pairs)  69.1 us
    pallas_call x1, Pallas kernels, attend(): pl.pallas_call(forward_kernel, out_shape=(jax.ShapeDtypeStruct((unit_coun...  68.5 us
    psum x1, blocking collectives, on_device(): fc_bias_grad = lax.psum(jnp.sum(grad_pre.astype(f32), axis=0), both)  52.3 us
    pallas_call x1, Pallas kernels, attend_back(): pl.pallas_call(backward_kernel, out_shape=jax.ShapeDtypeStruct((length, 4...  46.5 us
    all_to_all x1, waiting for transfers between devices, on_device(): lax.all_to_all(sent, 'ctx', 0, 0, tiled=True).reshape(attended.shape)  19.7 us
    all_to_all x1, starting transfers between devices, on_device(): merged = lax.all_to_all(sent, 'ctx', 0, 0, tiled=True)  15.2 us
    ppermute x9, starting transfers between devices, other_core(): return lax.ppermute(values, 'tensor', [(0, 1), (1, 0)])  13.2 us
  transfers between devices with their start and end apart: 49, of which 11 were waited for; matrix products, arithmetic and copies ran while one was open for 20% of the time, Pallas kernels for 21%

profile of v1, /device:TPU:0, one launch (start us, length us, event | category | flops | bytes accessed | tf_op | source)
XLA Modules:
  0.0 543.3 jit_solution(6097958577055588170)
XLA Ops:
  7.2 1.7 pad_maximum_fusion.8
  9.0 1.7 convert_reduce_fusion.2
  12.0 5.6 %collective-permute-start.2 = (bf16[256,768]{1,0:T(8,128)(2,1)S(1)}, bf16[256,768]{1,0:T(8,128)(2,1)S(1)}, u32[]{:S(2)}, u32[]{:S(2)}) collective-permute-start(bf16[256,768]{1,0:T(8,128)(2,1)S(1)} %get-tuple-element.56), channel_id=1, source_target_pairs={{0,4},{2,6},{4,8},{6,10},{8,12},{10,14},{1,5},{3,7},{5,9},{7,11},{... | collective-permute-start | bytes 1179656 | tf_op jit(solution)/shard_map/ppermute | solution.py:307
  18.5 6.3 %collective-permute-done.3 = bf16[256,768]{1,0:T(8,128)(2,1)S(1)} collective-permute-done((bf16[256,768]{1,0:T(8,128)(2,1)S(1)}, bf16[256,768]{1,0:T(8,128)(2,1)S(1)}, u32[]{:S(2)}, u32[]{:S(2)}) %collective-permute-start.3) | collective-permute-done | bytes 393248 | tf_op jit(solution)/shard_map/ppermute | solution.py:307
  34.3 7.1 %all-to-all-start = ((bf16[16,48,512]{2,1,0:T(8,128)(2,1)}), bf16[16,48,512]{2,1,0:T(8,128)(2,1)S(1)}, u32[]{:S(2)}, u32[]{:S(2)}) async-start(bf16[16,48,512]{2,1,0:T(8,128)(2,1)} %bitcast.13), calls=%async_computation | async-start | bytes 1572864 | tf_op jit(solution)/shard_map/all_to_all | solution.py:487
  41.4 3.8 collective-permute-start
  51.9 1.9 broadcast_in_dim.24
  55.2 10.1 %collective-permute-done = bf16[256,768]{1,0:T(8,128)(2,1)S(1)} collective-permute-done((bf16[256,768]{1,0:T(8,128)(2,1)S(1)}, bf16[256,768]{1,0:T(8,128)(2,1)S(1)}, u32[]{:S(2)}, u32[]{:S(2)}) %collective-permute-start) | collective-permute-done | bytes 393248 | tf_op jit(solution)/shard_map/ppermute | solution.py:307
  67.4 10.3 %collective-permute-done.5 = bf16[256,768]{1,0:T(8,128)(2,1)S(1)} collective-permute-done((bf16[256,768]{1,0:T(8,128)(2,1)S(1)}, bf16[256,768]{1,0:T(8,128)(2,1)S(1)}, u32[]{:S(2)}, u32[]{:S(2)}) %collective-permute-start.5) | collective-permute-done | bytes 393248 | tf_op jit(solution)/shard_map/ppermute | solution.py:307
  79.1 4.6 collective-permute-start.8
  83.7 1.9 add_dynamic-update-slice_fusion.6
  90.4 9.2 %collective-permute-done.9 = bf16[256,768]{1,0:T(8,128)(2,1)S(1)} collective-permute-done((bf16[256,768]{1,0:T(8,128)(2,1)S(1)}, bf16[256,768]{1,0:T(8,128)(2,1)S(1)}, u32[]{:S(2)}, u32[]{:S(2)}) %collective-permute-start.9) | collective-permute-done | bytes 393248 | tf_op jit(solution)/shard_map/ppermute | solution.py:307
  104.0 1.8 add_dynamic-update-slice_fusion.3
  105.8 11.6 %collective-permute-done.12 = bf16[256,768]{1,0:T(8,128)(2,1)S(1)} collective-permute-done((bf16[256,768]{1,0:T(8,128)(2,1)S(1)}, bf16[256,768]{1,0:T(8,128)(2,1)S(1)}, u32[]{:S(2)}, u32[]{:S(2)}) %collective-permute-start.12) | collective-permute-done | bytes 393248 | tf_op jit(solution)/shard_map/ppermute | solution.py:307
  117.4 4.4 collective-permute-start.18
  124.8 2.2 add_dynamic-update-slice_fusion.2
  127.9 1.9 add_dynamic-update-slice_fusion
  129.8 2.4 convert_reduce_fusion
  132.2 2.9 fusion.7
  137.1 2.7 fusion.5
  141.5 2.8 fusion.15.p_ref
  144.4 68.5 %attend.1 = (f32[24,128,64]{2,1,0:T(8,128)S(1)}, f32[24,1,128]{2,1,0:T(1,128)S(1)}, f32[24,1,128]{2,1,0:T(1,128)S(1)}) custom-call(s32[24,3]{1,0:T(8,128)S(1)} %copy.200.table, s32[1]{0:T(128)} %bitcast.2.prefix_ref, bf16[2048,640]{1,0:T(8,128)(2,1)S(1)} %fusion.15.p_ref, bf16[128,2048]{1,0:T(8,128)(2,1)S(1)} %get-tuple-element.69.vt_ref), custom_call_target="tpu_custom_call" | custom-call | flops 3221225472 | bytes 5242880 | tf_op jit(solution)/shard_map/attend/pallas_call | solution.py:253
  214.1 15.2 %all-to-all-start.1 = ((bf16[8,192,128]{2,1,0:T(8,128)(2,1)}), bf16[8,192,128]{2,1,0:T(8,128)(2,1)}, u32[]{:S(2)}, u32[]{:S(2)}) async-start(bf16[8,192,128]{2,1,0:T(8,128)(2,1)} %reshape.292), calls=%async_computation.1 | async-start | bytes 786432 | tf_op jit(solution)/shard_map/all_to_all | solution.py:524
  229.4 1.9 slice.373
  231.3 4.5 collective-permute-start.21
  235.8 2.9 all-to-all-done.1
  241.4 2.4 fusion.81
  244.9 3.6 collective-permute-start.22
  250.8 3.5 convolution_add_fusion
  254.4 3.8 convert_reduce_fusion.1
  259.7 2.0 fusion.20
  266.8 2.5 convolution_convert_fusion.1
  271.1 11.9 %pad_maximum_fusion = bf16[768,3456]{1,0:T(8,128)(2,1)} fusion(bf16[768,384]{1,0:T(8,128)(2,1)S(1)} %add_convert_fusion.1, bf16[768,1536]{1,0:T(8,128)(2,1)S(1)} %convolution_convert_fusion, bf16[768,1536]{1,0:T(8,128)(2,1)S(1)} %convolution_convert_fusion.1), kind=kLoop, calls=%fused_computation.10 | loop fusion | flops 15925248 | bytes 10616832 | tf_op jit(solution)/shard_map/concatenate | solution.py:563
  284.1 2.9 convolution_convert_fusion.5
  287.0 1.9 copy.202
  288.9 1.9 reshape.295
  290.7 2.1 copy.203
  292.8 2.3 reshape.296
  295.1 4.1 all-to-all-start.2
  299.2 19.7 %all-to-all-done.2 = bf16[8,192,128]{2,1,0:T(8,128)(2,1)} async-done(((bf16[8,192,128]{2,1,0:T(8,128)(2,1)}), bf16[8,192,128]{2,1,0:T(8,128)(2,1)}, u32[]{:S(2)}, u32[]{:S(2)}) %all-to-all-start.2) | async-done | bytes 393248 | tf_op jit(solution)/shard_map/all_to_all | solution.py:552
  318.9 2.2 reshape.297
  321.2 2.0 pad_maximum_fusion.3.do_ref
  324.8 46.5 %attend_back.1 = bf16[2048,512]{1,0:T(8,128)(2,1)S(1)} custom-call(s32[24,3]{1,0:T(8,128)S(1)} %copy.200.table, s32[1]{0:T(128)} %bitcast.2.prefix_ref, bf16[2048,640]{1,0:T(8,128)(2,1)S(1)} %copy-done.3, bf16[128,2048]{1,0:T(8,128)(2,1)S(1)} %get-tuple-element.68.kt_ref, bf16[24,128,128]{2,1,0:T(8,128)(2,1)S(1)} %pad_maximum_fusion.3.do_ref, ...), custom_call_target="tpu_custom_call" | custom-call | flops 8053063680 | bytes 5242880 | tf_op jit(solution)/shard_map/attend_back/pallas_call | solution.py:277
  371.3 3.8 fusion.73
  378.2 4.6 collective-permute-start.32
  384.7 4.6 collective-permute-start.30
  391.7 6.0 %collective-permute-start.28 = (bf16[256,768]{1,0:T(8,128)(2,1)}, bf16[256,768]{1,0:T(8,128)(2,1)}, u32[]{:S(2)}, u32[]{:S(2)}) collective-permute-start(bf16[256,768]{1,0:T(8,128)(2,1)} %get-tuple-element.66), channel_id=1, source_target_pairs={{0,2},{4,6},{8,10},{12,14},{1,3},{5,7},{9,11},{13,15},{16,18},{20,... | collective-permute-start | bytes 1179656 | tf_op jit(solution)/shard_map/ppermute | solution.py:307
  398.7 2.3 collective-permute-start.34
  401.0 2.6 fusion.16
  404.4 4.8 concatenate.99
  409.2 4.0 collective-permute-start.41
  414.7 3.5 collective-permute-start.35
  418.2 14.1 %collective-permute-done.35 = bf16[256,768]{1,0:T(8,128)(2,1)S(1)} collective-permute-done((bf16[256,768]{1,0:T(8,128)(2,1)S(1)}, bf16[256,768]{1,0:T(8,128)(2,1)S(1)}, u32[]{:S(2)}, u32[]{:S(2)}) %collective-permute-start.35) | collective-permute-done | bytes 393248 | tf_op jit(solution)/shard_map/ppermute | solution.py:307
  432.3 2.3 add_convert_fusion.4
  437.5 7.6 %all-to-all-start.3 = ((bf16[16,48,512]{2,1,0:T(8,128)(2,1)}), bf16[16,48,512]{2,1,0:T(8,128)(2,1)S(1)}, u32[]{:S(2)}, u32[]{:S(2)}) async-start(bf16[16,48,512]{2,1,0:T(8,128)(2,1)} %bitcast.27), calls=%async_computation.3 | async-start | bytes 1572864 | tf_op jit(solution)/shard_map/all_to_all | solution.py:593
  445.1 2.2 add_convert_fusion.3
  448.3 52.3 %psum.7 = f32[1536]{0:T(1024)} all-reduce(f32[1536]{0:T(1024)} %get-tuple-element.108), channel_id=1, replica_groups=mesh['dp'=2,'ctx'=8,'tensor'=2] {'dp','ctx'}, use_global_device_ids=true, to_apply=%region_21.22 | all-reduce | flops 1536 | bytes 12288 | tf_op jit(solution)/shard_map/psum | solution.py:565
  501.9 6.1 %collective-permute-start.26 = (bf16[256,768]{1,0:T(8,128)(2,1)}, bf16[256,768]{1,0:T(8,128)(2,1)}, u32[]{:S(2)}, u32[]{:S(2)}) collective-permute-start(bf16[256,768]{1,0:T(8,128)(2,1)} %get-tuple-element.60), channel_id=1, source_target_pairs={{0,2},{4,6},{8,10},{12,14},{1,3},{5,7},{9,11},{13,15},{16,18},{20,... | collective-permute-start | bytes 1179656 | tf_op jit(solution)/shard_map/ppermute | solution.py:307
  508.0 2.1 collective-permute-start.36
  510.1 2.0 add_convert_fusion.2
  513.3 2.2 maximum_select_fusion.2
  515.8 6.2 %collective-permute-done.39 = bf16[256,768]{1,0:T(8,128)(2,1)} collective-permute-done((bf16[256,768]{1,0:T(8,128)(2,1)}, bf16[256,768]{1,0:T(8,128)(2,1)}, u32[]{:S(2)}, u32[]{:S(2)}) %collective-permute-start.39) | collective-permute-done | bytes 393248 | tf_op jit(solution)/shard_map/ppermute | solution.py:307
  522.0 2.0 fusion.74
  529.5 2.7 maximum_select_fusion
  (225 shorter events, 84.9 us)
Async XLA Ops:
  7.2 43.5 %copy-start = (s32[2,1]{0,1:T(1,128)S(1)}, s32[2,1]{0,1:T(1,128)}, u32[]{:S(2)}) copy-start(s32[2,1]{0,1:T(1,128)} %param.19) | copy-start | bytes 28
  7.2 222.2 %all-gather.2.cloned.1.call-start = ((), (), s32[]{:S(2)}) async-start(), calls=%async_computation.5 | async-start | bytes 5640192 | tf_op jit(solution)/shard_map/all_gather | solution.py:494
  10.7 14.0 %collective-permute-start.3 = (bf16[256,768]{1,0:T(8,128)(2,1)S(1)}, bf16[256,768]{1,0:T(8,128)(2,1)S(1)}, u32[]{:S(2)}, u32[]{:S(2)}) collective-permute-start(bf16[256,768]{1,0:T(8,128)(2,1)S(1)} %get-tuple-element.56), channel_id=1, source_target_pairs={{4,0},{6,2},{8,4},{10,6},{12,8},{14,10},{5,1},{7,3},{9,5},{11,7},{... | collective-permute-start | bytes 1179656 | tf_op jit(solution)/shard_map/ppermute | solution.py:307
  12.0 33.2 %collective-permute-start.2 = (bf16[256,768]{1,0:T(8,128)(2,1)S(1)}, bf16[256,768]{1,0:T(8,128)(2,1)S(1)}, u32[]{:S(2)}, u32[]{:S(2)}) collective-permute-start(bf16[256,768]{1,0:T(8,128)(2,1)S(1)} %get-tuple-element.56), channel_id=1, source_target_pairs={{0,4},{2,6},{4,8},{6,10},{8,12},{10,14},{1,5},{3,7},{5,9},{7,11},{... | collective-permute-start | bytes 1179656 | tf_op jit(solution)/shard_map/ppermute | solution.py:307
  24.7 21.2 %collective-permute-start.4 = (bf16[256,768]{1,0:T(8,128)(2,1)S(1)}, bf16[256,768]{1,0:T(8,128)(2,1)S(1)}, u32[]{:S(2)}, u32[]{:S(2)}) collective-permute-start(bf16[256,768]{1,0:T(8,128)(2,1)S(1)} %collective-permute-done.3), channel_id=1, source_target_pairs={{4,0},{6,2},{8,4},{10,6},{5,1},{7,3},{9,5},{11,7},{20,16},{22,18},... | collective-permute-start | bytes 1179656 | tf_op jit(solution)/shard_map/ppermute | solution.py:307
  34.3 90.5 %all-to-all-start = ((bf16[16,48,512]{2,1,0:T(8,128)(2,1)}), bf16[16,48,512]{2,1,0:T(8,128)(2,1)S(1)}, u32[]{:S(2)}, u32[]{:S(2)}) async-start(bf16[16,48,512]{2,1,0:T(8,128)(2,1)} %bitcast.13), calls=%async_computation | async-start | bytes 1572864 | tf_op jit(solution)/shard_map/all_to_all | solution.py:487
  41.4 23.9 %collective-permute-start = (bf16[256,768]{1,0:T(8,128)(2,1)S(1)}, bf16[256,768]{1,0:T(8,128)(2,1)S(1)}, u32[]{:S(2)}, u32[]{:S(2)}) collective-permute-start(bf16[256,768]{1,0:T(8,128)(2,1)S(1)} %get-tuple-element.56), channel_id=1, source_target_pairs={{0,2},{4,6},{8,10},{12,14},{1,3},{5,7},{9,11},{13,15},{16,18},{20,... | collective-permute-start | bytes 1179656 | tf_op jit(solution)/shard_map/ppermute | solution.py:307
  45.2 20.7 %collective-permute-start.10 = (bf16[256,768]{1,0:T(8,128)(2,1)S(1)}, bf16[256,768]{1,0:T(8,128)(2,1)S(1)}, u32[]{:S(2)}, u32[]{:S(2)}) collective-permute-start(bf16[256,768]{1,0:T(8,128)(2,1)S(1)} %collective-permute-done.2), channel_id=1, source_target_pairs={{4,8},{6,10},{8,12},{10,14},{5,9},{7,11},{9,13},{11,15},{20,24},{2... | collective-permute-start | bytes 1179656 | tf_op jit(solution)/shard_map/ppermute | solution.py:307
  45.9 31.8 %collective-permute-start.5 = (bf16[256,768]{1,0:T(8,128)(2,1)S(1)}, bf16[256,768]{1,0:T(8,128)(2,1)S(1)}, u32[]{:S(2)}, u32[]{:S(2)}) collective-permute-start(bf16[256,768]{1,0:T(8,128)(2,1)S(1)} %collective-permute-done.4), channel_id=1, source_target_pairs={{4,0},{6,2},{5,1},{7,3},{20,16},{22,18},{21,17},{23,19}} | collective-permute-start | bytes 1179656 | tf_op jit(solution)/shard_map/ppermute | solution.py:307
  47.2 31.8 %collective-permute-start.1 = (bf16[256,768]{1,0:T(8,128)(2,1)S(1)}, bf16[256,768]{1,0:T(8,128)(2,1)}, u32[]{:S(2)}, u32[]{:S(2)}) collective-permute-start(bf16[256,768]{1,0:T(8,128)(2,1)S(1)} %get-tuple-element.56), channel_id=1, source_target_pairs={{2,0},{6,4},{10,8},{14,12},{3,1},{7,5},{11,9},{15,13},{18,16},{22,... | collective-permute-start | bytes 1179656 | tf_op jit(solution)/shard_map/ppermute | solution.py:307
  54.5 31.8 %collective-permute-start.6 = (bf16[256,768]{1,0:T(8,128)(2,1)S(1)}, bf16[256,768]{1,0:T(8,128)(2,1)S(1)}, u32[]{:S(2)}, u32[]{:S(2)}) collective-permute-start(bf16[256,768]{1,0:T(8,128)(2,1)S(1)} %collective-permute-done.2), channel_id=1, source_target_pairs={{4,6},{8,10},{12,14},{5,7},{9,11},{13,15},{20,22},{24,26},{28,30},... | collective-permute-start | bytes 1179656 | tf_op jit(solution)/shard_map/ppermute | solution.py:307
  65.3 22.5 %collective-permute-start.7 = (bf16[256,768]{1,0:T(8,128)(2,1)S(1)}, bf16[256,768]{1,0:T(8,128)(2,1)S(1)}, u32[]{:S(2)}, u32[]{:S(2)}) collective-permute-start(bf16[256,768]{1,0:T(8,128)(2,1)S(1)} %collective-permute-done.2), channel_id=1, source_target_pairs={{6,4},{10,8},{14,12},{7,5},{11,9},{15,13},{22,20},{26,24},{30,28},... | collective-permute-start | bytes 1179656 | tf_op jit(solution)/shard_map/ppermute | solution.py:307
  66.0 23.1 %collective-permute-start.11 = (bf16[256,768]{1,0:T(8,128)(2,1)S(1)}, bf16[256,768]{1,0:T(8,128)(2,1)}, u32[]{:S(2)}, u32[]{:S(2)}) collective-permute-start(bf16[256,768]{1,0:T(8,128)(2,1)S(1)} %collective-permute-done.10), channel_id=1, source_target_pairs={{8,12},{10,14},{9,13},{11,15},{24,28},{26,30},{25,29},{27,31}} | collective-permute-start | bytes 1179656 | tf_op jit(solution)/shard_map/ppermute | solution.py:307
  77.8 21.9 %collective-permute-start.9 = (bf16[256,768]{1,0:T(8,128)(2,1)S(1)}, bf16[256,768]{1,0:T(8,128)(2,1)S(1)}, u32[]{:S(2)}, u32[]{:S(2)}) collective-permute-start(bf16[256,768]{1,0:T(8,128)(2,1)S(1)} %collective-permute-done.5), channel_id=1, source_target_pairs={{2,0},{3,1},{18,16},{19,17}} | collective-permute-start | bytes 1179656 | tf_op jit(solution)/shard_map/ppermute | solution.py:307
  79.1 22.4 %collective-permute-start.8 = (bf16[256,768]{1,0:T(8,128)(2,1)S(1)}, bf16[256,768]{1,0:T(8,128)(2,1)S(1)}, u32[]{:S(2)}, u32[]{:S(2)}) collective-permute-start(bf16[256,768]{1,0:T(8,128)(2,1)S(1)} %collective-permute-done.5), channel_id=1, source_target_pairs={{0,2},{1,3},{16,18},{17,19}} | collective-permute-start | bytes 1179656 | tf_op jit(solution)/shard_map/ppermute | solution.py:307
  86.4 31.1 %collective-permute-start.12 = (bf16[256,768]{1,0:T(8,128)(2,1)S(1)}, bf16[256,768]{1,0:T(8,128)(2,1)S(1)}, u32[]{:S(2)}, u32[]{:S(2)}) collective-permute-start(bf16[256,768]{1,0:T(8,128)(2,1)S(1)} %collective-permute-done.3), channel_id=1, source_target_pairs={{0,2},{4,6},{8,10},{1,3},{5,7},{9,11},{16,18},{20,22},{24,26},{17,... | collective-permute-start | bytes 1179656 | tf_op jit(solution)/shard_map/ppermute | solution.py:307
  87.8 34.0 %collective-permute-start.13 = (bf16[256,768]{1,0:T(8,128)(2,1)S(1)}, bf16[256,768]{1,0:T(8,128)(2,1)S(1)}, u32[]{:S(2)}, u32[]{:S(2)}) collective-permute-start(bf16[256,768]{1,0:T(8,128)(2,1)S(1)} %collective-permute-done.3), channel_id=1, source_target_pairs={{2,0},{6,4},{10,8},{3,1},{7,5},{11,9},{18,16},{22,20},{26,24},{19,... | collective-permute-start | bytes 1179656 | tf_op jit(solution)/shard_map/ppermute | solution.py:307
  89.1 38.7 %collective-permute-start.19 = (bf16[256,768]{1,0:T(8,128)(2,1)S(1)}, bf16[256,768]{1,0:T(8,128)(2,1)S(1)}, u32[]{:S(2)}, u32[]{:S(2)}) collective-permute-start(bf16[256,768]{1,0:T(8,128)(2,1)S(1)} %collective-permute-done.4), channel_id=1, source_target_pairs={{2,0},{6,4},{3,1},{7,5},{18,16},{22,20},{19,17},{23,21}} | collective-permute-start | bytes 1179656 | tf_op jit(solution)/shard_map/ppermute | solution.py:307
  99.6 22.9 %collective-permute-start.15 = (bf16[256,768]{1,0:T(8,128)(2,1)}, bf16[256,768]{1,0:T(8,128)(2,1)S(1)}, u32[]{:S(2)}, u32[]{:S(2)}) collective-permute-start(bf16[256,768]{1,0:T(8,128)(2,1)} %collective-permute-done.11), channel_id=1, source_target_pairs={{14,12},{15,13},{30,28},{31,29}} | collective-permute-start | bytes 1179656 | tf_op jit(solution)/shard_map/ppermute | solution.py:307
  101.5 23.2 %collective-permute-start.14 = (bf16[256,768]{1,0:T(8,128)(2,1)}, bf16[256,768]{1,0:T(8,128)(2,1)}, u32[]{:S(2)}, u32[]{:S(2)}) collective-permute-start(bf16[256,768]{1,0:T(8,128)(2,1)} %collective-permute-done.11), channel_id=1, source_target_pairs={{12,14},{13,15},{28,30},{29,31}} | collective-permute-start | bytes 1179656 | tf_op jit(solution)/shard_map/ppermute | solution.py:307
  117.4 10.4 %collective-permute-start.18 = (bf16[256,768]{1,0:T(8,128)(2,1)S(1)}, bf16[256,768]{1,0:T(8,128)(2,1)S(1)}, u32[]{:S(2)}, u32[]{:S(2)}) collective-permute-start(bf16[256,768]{1,0:T(8,128)(2,1)S(1)} %collective-permute-done.4), channel_id=1, source_target_pairs={{0,2},{4,6},{1,3},{5,7},{16,18},{20,22},{17,19},{21,23}} | collective-permute-start | bytes 1179656 | tf_op jit(solution)/shard_map/ppermute | solution.py:307
  121.8 6.0 %collective-permute-start.16 = (bf16[256,768]{1,0:T(8,128)(2,1)S(1)}, bf16[256,768]{1,0:T(8,128)(2,1)S(1)}, u32[]{:S(2)}, u32[]{:S(2)}) collective-permute-start(bf16[256,768]{1,0:T(8,128)(2,1)S(1)} %collective-permute-done.10), channel_id=1, source_target_pairs={{8,10},{12,14},{9,11},{13,15},{24,26},{28,30},{25,27},{29,31}} | collective-permute-start | bytes 1179656 | tf_op jit(solution)/shard_map/ppermute | solution.py:307
  123.3 4.6 collective-permute-start.17
  124.8 10.4 %collective-permute-start.20 = (bf16[768,512]{1,0:T(8,128)(2,1)S(1)}, bf16[768,512]{1,0:T(8,128)(2,1)S(1)}, u32[]{:S(2)}, u32[]{:S(2)}) collective-permute-start(bf16[768,512]{1,0:T(8,128)(2,1)S(1)} %bitcast.108), channel_id=1, source_target_pairs={{0,1},{1,0},{2,3},{3,2},{4,5},{5,4},{6,7},{7,6},{8,9},{9,8},{10,11... | collective-permute-start | bytes 2359304 | tf_op jit(solution)/shard_map/ppermute | solution.py:386
  144.3 68.5 %copy-start.2 = (bf16[2048,640]{1,0:T(8,128)(2,1)}, bf16[2048,640]{1,0:T(8,128)(2,1)S(1)}, u32[]{:S(2)}) copy-start(bf16[2048,640]{1,0:T(8,128)(2,1)S(1)} %fusion.15.p_ref) | copy-start | bytes 7864324
  214.1 24.6 %all-to-all-start.1 = ((bf16[8,192,128]{2,1,0:T(8,128)(2,1)}), bf16[8,192,128]{2,1,0:T(8,128)(2,1)}, u32[]{:S(2)}, u32[]{:S(2)}) async-start(bf16[8,192,128]{2,1,0:T(8,128)(2,1)} %reshape.292), calls=%async_computation.1 | async-start | bytes 786432 | tf_op jit(solution)/shard_map/all_to_all | solution.py:524
  229.3 302.9 %reduce-scatter.2.cloned.1.call-start = ((), (), s32[]{:S(2)}) async-start(), calls=%async_computation.6 | async-start | bytes 5640192 | tf_op jit(solution)/shard_map/reduce_scatter | solution.py:564
  231.3 10.1 %collective-permute-start.21 = (bf16[768,384]{1,0:T(8,128)(2,1)}, bf16[768,384]{1,0:T(8,128)(2,1)}, u32[]{:S(2)}, u32[]{:S(2)}) collective-permute-start(bf16[768,384]{1,0:T(8,128)(2,1)} %slice.373), channel_id=1, source_target_pairs={{0,1},{1,0},{2,3},{3,2},{4,5},{5,4},{6,7},{7,6},{8,9},{9,8},{10,11... | collective-permute-start | bytes 1769480 | tf_op jit(solution)/shard_map/ppermute | solution.py:386
  241.4 7.2 %copy-start.23 = (bf16[1536]{0:T(1024)(128)(2,1)S(1)}, bf16[1536]{0:T(1024)(128)(2,1)}, u32[]{:S(2)}) copy-start(bf16[1536]{0:T(1024)(128)(2,1)} %param.32) | copy-start | bytes 9220
  244.9 5.9 %collective-permute-start.22 = (bf16[256,768]{1,0:T(8,128)(2,1)}, bf16[256,768]{1,0:T(8,128)(2,1)}, u32[]{:S(2)}, u32[]{:S(2)}) collective-permute-start(bf16[256,768]{1,0:T(8,128)(2,1)} %add_convert_fusion.6), channel_id=1, source_target_pairs={{0,1},{1,0},{2,3},{3,2},{4,5},{5,4},{6,7},{7,6},{8,9},{9,8},{10,11... | collective-permute-start | bytes 1179656 | tf_op jit(solution)/shard_map/ppermute | solution.py:386
  259.6 2.7 collective-permute-start.25
  261.7 1.9 collective-permute-start.23
  266.3 4.5 collective-permute-start.42
  295.1 23.9 %all-to-all-start.2 = ((bf16[8,192,128]{2,1,0:T(8,128)(2,1)}), bf16[8,192,128]{2,1,0:T(8,128)(2,1)}, u32[]{:S(2)}, u32[]{:S(2)}) async-start(bf16[8,192,128]{2,1,0:T(8,128)(2,1)} %reshape.296), calls=%async_computation.2 | async-start | bytes 786432 | tf_op jit(solution)/shard_map/all_to_all | solution.py:552
  324.8 46.5 %copy-start.8 = (bf16[768,512]{1,0:T(8,128)(2,1)S(1)}, bf16[768,512]{1,0:T(8,128)(2,1)}, u32[]{:S(2)}) copy-start(bf16[768,512]{1,0:T(8,128)(2,1)} %copy-done.7) | copy-start | bytes 2359300
  375.2 22.6 %copy-start.4 = (bf16[2048,768]{1,0:T(8,128)(2,1)}, bf16[2048,768]{1,0:T(8,128)(2,1)S(1)}, u32[]{:S(2)}) copy-start(bf16[2048,768]{1,0:T(8,128)(2,1)S(1)} %get-tuple-element.57) | copy-start | bytes 9437188
  375.2 25.8 %copy-start.10 = (bf16[2048,768]{1,0:T(8,128)(2,1)S(1)}, bf16[2048,768]{1,0:T(8,128)(2,1)}, u32[]{:S(2)}) copy-start(bf16[2048,768]{1,0:T(8,128)(2,1)} %copy-done.9) | copy-start | bytes 9437188
  376.6 15.1 %collective-permute-start.33 = (bf16[256,768]{1,0:T(8,128)(2,1)S(1)}, bf16[256,768]{1,0:T(8,128)(2,1)S(1)}, u32[]{:S(2)}, u32[]{:S(2)}) collective-permute-start(bf16[256,768]{1,0:T(8,128)(2,1)S(1)} %get-tuple-element.61), channel_id=1, source_target_pairs={{2,0},{6,4},{10,8},{14,12},{3,1},{7,5},{11,9},{15,13},{18,16},{22,... | collective-permute-start | bytes 1179656 | tf_op jit(solution)/shard_map/ppermute | solution.py:307
  378.2 19.6 %collective-permute-start.32 = (bf16[256,768]{1,0:T(8,128)(2,1)S(1)}, bf16[256,768]{1,0:T(8,128)(2,1)S(1)}, u32[]{:S(2)}, u32[]{:S(2)}) collective-permute-start(bf16[256,768]{1,0:T(8,128)(2,1)S(1)} %get-tuple-element.62), channel_id=1, source_target_pairs={{0,2},{4,6},{8,10},{12,14},{1,3},{5,7},{9,11},{13,15},{16,18},{20,... | collective-permute-start | bytes 1179656 | tf_op jit(solution)/shard_map/ppermute | solution.py:307
  383.4 25.8 %collective-permute-start.31 = (bf16[256,768]{1,0:T(8,128)(2,1)}, bf16[256,768]{1,0:T(8,128)(2,1)S(1)}, u32[]{:S(2)}, u32[]{:S(2)}) collective-permute-start(bf16[256,768]{1,0:T(8,128)(2,1)} %get-tuple-element.63), channel_id=1, source_target_pairs={{2,0},{6,4},{10,8},{14,12},{3,1},{7,5},{11,9},{15,13},{18,16},{22,... | collective-permute-start | bytes 1179656 | tf_op jit(solution)/shard_map/ppermute | solution.py:307
  384.7 28.6 %collective-permute-start.30 = (bf16[256,768]{1,0:T(8,128)(2,1)}, bf16[256,768]{1,0:T(8,128)(2,1)S(1)}, u32[]{:S(2)}, u32[]{:S(2)}) collective-permute-start(bf16[256,768]{1,0:T(8,128)(2,1)} %get-tuple-element.64), channel_id=1, source_target_pairs={{0,2},{4,6},{8,10},{12,14},{1,3},{5,7},{9,11},{13,15},{16,18},{20,... | collective-permute-start | bytes 1179656 | tf_op jit(solution)/shard_map/ppermute | solution.py:307
  389.3 29.0 %collective-permute-start.29 = (bf16[256,768]{1,0:T(8,128)(2,1)}, bf16[256,768]{1,0:T(8,128)(2,1)}, u32[]{:S(2)}, u32[]{:S(2)}) collective-permute-start(bf16[256,768]{1,0:T(8,128)(2,1)} %get-tuple-element.65), channel_id=1, source_target_pairs={{2,0},{6,4},{10,8},{14,12},{3,1},{7,5},{11,9},{15,13},{18,16},{22,... | collective-permute-start | bytes 1179656 | tf_op jit(solution)/shard_map/ppermute | solution.py:307
  391.7 11.8 %copy-start.13 = (bf16[256,768]{1,0:T(8,128)(2,1)}, bf16[256,768]{1,0:T(8,128)(2,1)S(1)}, u32[]{:S(2)}) copy-start(bf16[256,768]{1,0:T(8,128)(2,1)S(1)} %collective-permute-done.33) | copy-start | bytes 1179652
  391.7 26.5 %collective-permute-start.28 = (bf16[256,768]{1,0:T(8,128)(2,1)}, bf16[256,768]{1,0:T(8,128)(2,1)}, u32[]{:S(2)}, u32[]{:S(2)}) collective-permute-start(bf16[256,768]{1,0:T(8,128)(2,1)} %get-tuple-element.66), channel_id=1, source_target_pairs={{0,2},{4,6},{8,10},{12,14},{1,3},{5,7},{9,11},{13,15},{16,18},{20,... | collective-permute-start | bytes 1179656 | tf_op jit(solution)/shard_map/ppermute | solution.py:307
  398.7 14.5 %collective-permute-start.34 = (bf16[256,768]{1,0:T(8,128)(2,1)}, bf16[256,768]{1,0:T(8,128)(2,1)}, u32[]{:S(2)}, u32[]{:S(2)}) collective-permute-start(bf16[256,768]{1,0:T(8,128)(2,1)} %fusion.48), channel_id=1, source_target_pairs={{0,4},{2,6},{1,5},{3,7},{16,20},{18,22},{17,21},{19,23}} | collective-permute-start | bytes 1179656 | tf_op jit(solution)/shard_map/ppermute | solution.py:307
  409.2 26.8 %copy-start.17 = (bf16[256,768]{1,0:T(8,128)(2,1)}, bf16[256,768]{1,0:T(8,128)(2,1)S(1)}, u32[]{:S(2)}) copy-start(bf16[256,768]{1,0:T(8,128)(2,1)S(1)} %collective-permute-done.31) | copy-start | bytes 1179652
  409.2 26.8 %collective-permute-start.41 = (bf16[768,512]{0,1:T(8,128)(2,1)S(1)}, bf16[768,512]{0,1:T(8,128)(2,1)S(1)}, u32[]{:S(2)}, u32[]{:S(2)}) collective-permute-start(bf16[768,512]{0,1:T(8,128)(2,1)S(1)} %convert_element_type.238), channel_id=1, source_target_pairs={{0,1},{1,0},{2,3},{3,2},{4,5},{5,4},{6,7},{7,6},{8,9},{9,8},{10,11... | collective-permute-start | bytes 2359304 | tf_op jit(solution)/shard_map/ppermute | solution.py:386
  413.2 22.8 %copy-start.19 = (bf16[256,768]{1,0:T(8,128)(2,1)}, bf16[256,768]{1,0:T(8,128)(2,1)S(1)}, u32[]{:S(2)}) copy-start(bf16[256,768]{1,0:T(8,128)(2,1)S(1)} %collective-permute-done.30) | copy-start | bytes 1179652
  414.7 17.6 %collective-permute-start.35 = (bf16[256,768]{1,0:T(8,128)(2,1)S(1)}, bf16[256,768]{1,0:T(8,128)(2,1)S(1)}, u32[]{:S(2)}, u32[]{:S(2)}) collective-permute-start(bf16[256,768]{1,0:T(8,128)(2,1)S(1)} %add_convert_fusion.5), channel_id=1, source_target_pairs={{0,4},{2,6},{4,8},{6,10},{1,5},{3,7},{5,9},{7,11},{16,20},{18,22},... | collective-permute-start | bytes 1179656 | tf_op jit(solution)/shard_map/ppermute | solution.py:307
  434.7 10.4 %collective-permute-start.37 = (bf16[256,768]{1,0:T(8,128)(2,1)}, bf16[256,768]{1,0:T(8,128)(2,1)}, u32[]{:S(2)}, u32[]{:S(2)}) collective-permute-start(bf16[256,768]{1,0:T(8,128)(2,1)} %get-tuple-element.59), channel_id=1, source_target_pairs={{12,8},{14,10},{13,9},{15,11},{28,24},{30,26},{29,25},{31,27}} | collective-permute-start | bytes 1179656 | tf_op jit(solution)/shard_map/ppermute | solution.py:307
  436.3 8.8 %copy-start.18 = (bf16[256,768]{1,0:T(8,128)(2,1)S(1)}, bf16[256,768]{1,0:T(8,128)(2,1)}, u32[]{:S(2)}) copy-start(bf16[256,768]{1,0:T(8,128)(2,1)} %copy-done.17) | copy-start | bytes 1179652
  436.3 11.7 %copy-start.22 = (f32[256]{0:T(256)S(1)}, f32[256]{0:T(256)}, u32[]{:S(2)}) copy-start(f32[256]{0:T(256)} %get-tuple-element.55) | copy-start | bytes 3076
  436.3 11.9 %copy-start.11 = (bf16[256,768]{1,0:T(8,128)(2,1)S(1)}, bf16[256,768]{1,0:T(8,128)(2,1)}, u32[]{:S(2)}) copy-start(bf16[256,768]{1,0:T(8,128)(2,1)} %get-tuple-element.70) | copy-start | bytes 1179652
  436.3 73.8 %copy-start.14 = (bf16[256,768]{1,0:T(8,128)(2,1)S(1)}, bf16[256,768]{1,0:T(8,128)(2,1)}, u32[]{:S(2)}) copy-start(bf16[256,768]{1,0:T(8,128)(2,1)} %copy-done.13) | copy-start | bytes 1179652
  436.3 73.8 %copy-start.16 = (bf16[256,768]{1,0:T(8,128)(2,1)S(1)}, bf16[256,768]{1,0:T(8,128)(2,1)}, u32[]{:S(2)}) copy-start(bf16[256,768]{1,0:T(8,128)(2,1)} %copy-done.15) | copy-start | bytes 1179652
  437.5 78.0 %all-to-all-start.3 = ((bf16[16,48,512]{2,1,0:T(8,128)(2,1)}), bf16[16,48,512]{2,1,0:T(8,128)(2,1)S(1)}, u32[]{:S(2)}, u32[]{:S(2)}) async-start(bf16[16,48,512]{2,1,0:T(8,128)(2,1)} %bitcast.27), calls=%async_computation.3 | async-start | bytes 1572864 | tf_op jit(solution)/shard_map/all_to_all | solution.py:593
  447.3 62.8 %collective-permute-start.38 = (bf16[256,768]{1,0:T(8,128)(2,1)}, bf16[256,768]{1,0:T(8,128)(2,1)S(1)}, u32[]{:S(2)}, u32[]{:S(2)}) collective-permute-start(bf16[256,768]{1,0:T(8,128)(2,1)} %add_convert_fusion.3), channel_id=1, source_target_pairs={{8,4},{10,6},{12,8},{14,10},{9,5},{11,7},{13,9},{15,11},{24,20},{2... | collective-permute-start | bytes 1179656 | tf_op jit(solution)/shard_map/ppermute | solution.py:307
  448.2 65.1 %collective-permute-start.24 = (bf16[256,768]{1,0:T(8,128)(2,1)S(1)}, bf16[256,768]{1,0:T(8,128)(2,1)}, u32[]{:S(2)}, u32[]{:S(2)}) collective-permute-start(bf16[256,768]{1,0:T(8,128)(2,1)S(1)} %copy-done.11), channel_id=1, source_target_pairs={{0,1},{1,0},{2,3},{3,2},{4,5},{5,4},{6,7},{7,6},{8,9},{9,8},{10,11... | collective-permute-start | bytes 1179656 | tf_op jit(solution)/shard_map/ppermute | solution.py:386
  500.6 15.2 %collective-permute-start.27 = (bf16[256,768]{1,0:T(8,128)(2,1)}, bf16[256,768]{1,0:T(8,128)(2,1)}, u32[]{:S(2)}, u32[]{:S(2)}) collective-permute-start(bf16[256,768]{1,0:T(8,128)(2,1)} %get-tuple-element.67), channel_id=1, source_target_pairs={{2,0},{6,4},{10,8},{14,12},{3,1},{7,5},{11,9},{15,13},{18,16},{22,... | collective-permute-start | bytes 1179656 | tf_op jit(solution)/shard_map/ppermute | solution.py:307
  501.9 13.9 %collective-permute-start.26 = (bf16[256,768]{1,0:T(8,128)(2,1)}, bf16[256,768]{1,0:T(8,128)(2,1)}, u32[]{:S(2)}, u32[]{:S(2)}) collective-permute-start(bf16[256,768]{1,0:T(8,128)(2,1)} %get-tuple-element.60), channel_id=1, source_target_pairs={{0,2},{4,6},{8,10},{12,14},{1,3},{5,7},{9,11},{13,15},{16,18},{20,... | collective-permute-start | bytes 1179656 | tf_op jit(solution)/shard_map/ppermute | solution.py:307
  508.0 7.8 %collective-permute-start.36 = (bf16[256,768]{1,0:T(8,128)(2,1)}, bf16[256,768]{1,0:T(8,128)(2,1)}, u32[]{:S(2)}, u32[]{:S(2)}) collective-permute-start(bf16[256,768]{1,0:T(8,128)(2,1)} %get-tuple-element.58), channel_id=1, source_target_pairs={{0,4},{2,6},{4,8},{6,10},{8,12},{10,14},{1,5},{3,7},{5,9},{7,11},{... | collective-permute-start | bytes 1179656 | tf_op jit(solution)/shard_map/ppermute | solution.py:307
  512.0 10.0 %collective-permute-start.39 = (bf16[256,768]{1,0:T(8,128)(2,1)}, bf16[256,768]{1,0:T(8,128)(2,1)}, u32[]{:S(2)}, u32[]{:S(2)}) collective-permute-start(bf16[256,768]{1,0:T(8,128)(2,1)} %add_convert_fusion.2), channel_id=1, source_target_pairs={{4,0},{6,2},{8,4},{10,6},{12,8},{14,10},{5,1},{7,3},{9,5},{11,7},{... | collective-permute-start | bytes 1179656 | tf_op jit(solution)/shard_map/ppermute | solution.py:307
  525.2 4.2 collective-permute-start.40
  526.9 9.3 %copy-start.1 = (s32[2,1]{0,1:T(1,128)S(1)}, s32[2,1]{0,1:T(1,128)}, u32[]{:S(2)}) copy-start(s32[2,1]{0,1:T(1,128)} %param.19) | copy-start | bytes 28
  (12 other events, 33.0 us)
Sparse Core Ops, SparseCore 0:
  10.8 121.4 all-gather.1
  283.1 147.6 reduce-scatter.1

commit v2 on v1

v2 whole, which is shorter than its diff:
```python
from functools import partial

import jax
import jax.numpy as jnp
import numpy as np
from jax import lax
from jax.experimental import pallas as pl
from jax.experimental.pallas import tpu as pltpu
from jax.sharding import PartitionSpec as P

WIN = 64
TOPK = 64
HEAD = 64
LANES = 128

norm_epsilon = 1e-05
search_steps = 24
search_bound = 64.0

CHUNK = 256
FAR = 1e9
OPEN_PIVOT = -1e6
NEWTON_TOLERANCE = 3e-3
SCORE_ROWS = 16
NT = (((1,), (1,)), ((), ()))


def over_chunks(first, last, prefix, body, carry):
    below = lax.div(jnp.maximum(first - (WIN - 1), 0), CHUNK)
    total = lax.div(jnp.maximum(last + 1, prefix) + CHUNK - 1, CHUNK)
    above = jnp.minimum(lax.div(last + WIN + CHUNK - 1, CHUNK), total)
    whole = jnp.maximum(lax.div(prefix, CHUNK), above)
    carry = lax.fori_loop(0, below, body(False), carry)
    carry = lax.fori_loop(below, above, body(True), carry)
    carry = lax.fori_loop(above, whole, body(False), carry)
    return lax.fori_loop(whole, total, body(True), carry)


def fold(values, how):
    while values.shape[0] > 8:
        half = values.shape[0] // 2
        values = how(values[:half], values[half:])
    return values


def own_head(values, slot):
    lane = lax.broadcasted_iota(jnp.int32, values.shape, 1)
    kept = jnp.where(lax.div(lane, HEAD) == slot, values.astype(jnp.float32), 0.0)
    return kept


def rows_of(first, shape, rows, block):
    lane = lax.broadcasted_iota(jnp.int32, shape, 1)
    return first + lax.div(lane, rows) * block + lax.rem(lane, rows)


def masks(start, first, prefix, rows, block, together):
    shape = (CHUNK, rows * together)
    key = lax.broadcasted_iota(jnp.int32, shape, 0)
    behind = rows_of(first - start, shape, rows, block) - key
    allowed = (behind >= 0) | (key < prefix - start)
    return allowed, allowed & (jnp.abs(behind) < WIN)


def spread_lanes(values, lanes):
    values = values.astype(jnp.float32)
    return jnp.concatenate([values] * (lanes // LANES), axis=1)


def turn(source_ref, lanes, target_ref):
    def run(chunk, _):
        here = pl.ds(pl.multiple_of(chunk * CHUNK, CHUNK), CHUNK)
        flipped = source_ref[here, lanes : lanes + LANES].astype(jnp.float32).T
        target_ref[:, here] = flipped.astype(jnp.bfloat16)
        return 0

    lax.fori_loop(0, source_ref.shape[0] // CHUNK, run, 0)


def forward_kernel(
    block, table, prefix_ref, p_ref, o_ref, low_ref, lse_ref, pivot_ref, sm_ref, st_ref, vt_ref
):
    unit_count, _, lanes = o_ref.shape
    rows = low_ref.shape[2]
    together = lanes // rows
    prefix = prefix_ref[0]
    turn(p_ref, 2 * LANES, vt_ref)

    def unit(step, guess):
        slot, first = table[step, 0], table[step, 1]
        last = first + (together - 1) * block + rows - 1
        query = jnp.concatenate(
            [
                p_ref[pl.ds(pl.multiple_of(first + at * block, rows), rows), 0:LANES]
                for at in range(together)
            ],
            axis=0,
        )
        query_t = own_head(query, slot).T.astype(jnp.bfloat16)
        score_lane = pl.multiple_of((3 + slot) * LANES, LANES)

        def build(masked):
            def run(chunk, top):
                start = pl.multiple_of(chunk * CHUNK, CHUNK)
                here = pl.ds(start, CHUNK)
                logits = jnp.dot(
                    p_ref[here, LANES : 2 * LANES], query_t, preferred_element_type=jnp.float32
                )
                score = spread_lanes(p_ref[here, pl.ds(score_lane, LANES)], lanes)
                if masked:
                    allowed, local = masks(start, first, prefix, rows, block, together)
                    logits = jnp.where(allowed, logits, -1e30)
                    score = jnp.where(local, FAR, jnp.where(allowed, score, -FAR))
                    top = jnp.maximum(top, fold(jnp.where(local, logits, -1e30), jnp.maximum))
                st_ref[here, :] = logits
                sm_ref[here, :] = score
                return top

            return run

        top = over_chunks(first, last, prefix, build, jnp.full((8, lanes), -1e30, jnp.float32))
        top = jnp.max(top, axis=0, keepdims=True)

        row = rows_of(first, (1, lanes), rows, block)
        local_count = (
            jnp.minimum(row, WIN - 1) + 1 + jnp.clip(prefix - 1 - row, 0, WIN - 1)
        ).astype(jnp.float32)
        candidates = jnp.maximum(row + 1, prefix).astype(jnp.float32) - local_count
        chunks = lax.div(jnp.maximum(last + 1, prefix) + CHUNK - 1, CHUNK)
        entries = (chunks * CHUNK).astype(jnp.float32)
        searched = candidates > TOPK
        count = jnp.maximum(candidates, TOPK + 1.0)
        goal = jnp.log(TOPK / (count - TOPK))

        def measure(half):
            def run(chunk, sums):
                bent = jnp.tanh(sm_ref[pl.ds(pl.multiple_of(chunk * CHUNK, CHUNK), CHUNK), :] - half)
                return sums[0] + fold(bent, jnp.add), sums[1] + fold(bent * bent, jnp.add)

            zero = jnp.zeros((8, lanes), jnp.float32)
            first_sum, second_sum = lax.fori_loop(0, chunks, run, (zero, zero))
            filled = 0.5 * (entries + jnp.sum(first_sum, axis=0, keepdims=True)) - local_count
            slope = 0.25 * (entries - jnp.sum(second_sum, axis=0, keepdims=True))
            return filled, slope

        def improve(state):
            turn, _, half, lower, upper, done = state
            filled, slope = measure(half)
            above = filled > TOPK
            lower = jnp.where(above, half, lower)
            upper = jnp.where(above, upper, half)
            newton = (filled - TOPK) / slope
            held = jnp.clip(filled, 1e-3, count - 1e-3)
            bent = (jnp.log(held / (count - held)) - goal) * (held * (count - held) / (count * slope))
            close = jnp.abs(newton) <= NEWTON_TOLERANCE
            following = half + 0.5 * jnp.where(close, newton, bent)
            inside = (following > lower) & (following < upper)
            halve = (turn >= 12) & (lax.rem(turn, 2) == 1)
            middle = 0.5 * (lower + upper)
            following = jnp.where(close | (inside & jnp.logical_not(halve)), following, middle)
            half = jnp.where(done > 0.0, half, following)
            done = jnp.where(close, 1.0, done)
            return turn + 1, jnp.min(done), half, lower, upper, done

        start_done = jnp.where(searched, 0.0, 1.0)
        bound = jnp.full((1, lanes), 0.5 * search_bound, jnp.float32)
        _, _, half, lower, upper, done = lax.while_loop(
            lambda state: (state[0] < 12 + 2 * search_steps) & (state[1] < 0.5),
            improve,
            (0, jnp.min(start_done), guess, -bound, bound, start_done),
        )
        half = jnp.where(done > 0.0, half, 0.5 * (lower + upper))
        pivot = jnp.where(searched, half, OPEN_PIVOT)

        def weigh(chunk, sums):
            here = pl.ds(pl.multiple_of(chunk * CHUNK, CHUNK), CHUNK)
            raised = jnp.exp(st_ref[here, :] - top)
            weight = raised / (1.0 + jnp.exp(2.0 * (pivot - sm_ref[here, :])))
            merged = sums[1] + jnp.dot(
                vt_ref[:, here], weight.astype(jnp.bfloat16), preferred_element_type=jnp.float32
            )
            return sums[0] + fold(weight, jnp.add), merged

        total, merged = lax.fori_loop(
            0,
            chunks,
            weigh,
            (jnp.zeros((8, lanes), jnp.float32), jnp.zeros((LANES, lanes), jnp.float32)),
        )
        total = jnp.sum(total, axis=0, keepdims=True)
        merged = merged / total
        own = jnp.where(slot == 0, merged[:HEAD], merged[HEAD:])
        o_ref[step] = own
        for at in range(together):
            low_ref[table[step, 2 + at]] = own[:, at * rows : (at + 1) * rows].astype(jnp.bfloat16)
        lse_ref[step] = top + jnp.log(total)
        pivot_ref[step] = pivot
        return jnp.where(searched, half, guess)

    lax.fori_loop(0, unit_count, unit, jnp.zeros((1, lanes), jnp.float32))


def backward_kernel(
    block,
    table,
    prefix_ref,
    p_ref,
    do_ref,
    o_ref,
    lse_ref,
    pivot_ref,
    message_ref,
    d_ref,
    score_ref,
    dq_ref,
    dk_ref,
    dv_ref,
    ds_ref,
    kt_ref,
):
    unit_count, _, lanes = o_ref.shape
    rows = do_ref.shape[2]
    together = lanes // rows
    length = p_ref.shape[0]
    prefix = prefix_ref[0]
    turn(p_ref, LANES, kt_ref)

    def clear(chunk, _):
        here = pl.ds(pl.multiple_of(chunk * CHUNK, CHUNK), CHUNK)
        for ref in (dq_ref, dk_ref, dv_ref):
            ref[here, :] = jnp.zeros((CHUNK, LANES), jnp.float32)
        for slot in range(2):
            ds_ref[slot, here, :] = jnp.zeros((CHUNK, lanes), jnp.float32)
        return 0

    lax.fori_loop(0, length // CHUNK, clear, 0)

    def unit(step, _):
        slot, first = table[step, 0], table[step, 1]
        last = first + (together - 1) * block + rows - 1
        whose = [pl.ds(pl.multiple_of(first + at * block, rows), rows) for at in range(together)]
        query = own_head(jnp.concatenate([p_ref[here, 0:LANES] for here in whose], axis=0), slot)
        query_t = query.T.astype(jnp.bfloat16)
        query = query.astype(jnp.bfloat16)
        grad = jnp.concatenate([do_ref[table[step, 2 + at]] for at in range(together)], axis=1)
        grad = grad.astype(jnp.float32)
        row_dot = jnp.sum(grad * o_ref[step], axis=0, keepdims=True)
        empty = jnp.zeros_like(grad)
        grad = jnp.where(
            slot == 0,
            jnp.concatenate([grad, empty], axis=0),
            jnp.concatenate([empty, grad], axis=0),
        )
        grad_t = grad.T.astype(jnp.bfloat16)
        grad = grad.astype(jnp.bfloat16)
        lse, pivot = lse_ref[step], pivot_ref[step]
        score_lane = pl.multiple_of((3 + slot) * LANES, LANES)

        def body(masked):
            def run(chunk, grad_query):
                start = pl.multiple_of(chunk * CHUNK, CHUNK)
                here = pl.ds(start, CHUNK)
                logits = jnp.dot(
                    p_ref[here, LANES : 2 * LANES], query_t, preferred_element_type=jnp.float32
                )
                grad_probs = jnp.dot(
                    p_ref[here, 2 * LANES : 3 * LANES], grad, preferred_element_type=jnp.float32
                )
                score = spread_lanes(p_ref[here, pl.ds(score_lane, LANES)], lanes)
                if masked:
                    allowed, local = masks(start, first, prefix, rows, block, together)
                    logits = jnp.where(allowed, logits, -1e30)
                    score = jnp.where(local, FAR, jnp.where(allowed, score, -FAR))
                unit_probs = jnp.exp(logits - lse)
                gate = 1.0 / (1.0 + jnp.exp(2.0 * (pivot - score)))
                probs = gate * unit_probs
                grad_logits = probs * (grad_probs - row_dot)
                ds_ref[slot, here, :] += grad_logits * (1.0 - gate)
                low = grad_logits.astype(jnp.bfloat16)
                dk_ref[here, :] += jnp.dot(low, query, preferred_element_type=jnp.float32)
                dv_ref[here, :] += jnp.dot(
                    probs.astype(jnp.bfloat16), grad_t, preferred_element_type=jnp.float32
                )
                return grad_query + jnp.dot(
                    kt_ref[:, here], low, preferred_element_type=jnp.float32
                )

            return run

        grad_query = over_chunks(
            first, last, prefix, body, jnp.zeros((LANES, lanes), jnp.float32)
        ).T
        lane = lax.broadcasted_iota(jnp.int32, grad_query.shape, 1)
        grad_query = jnp.where(lax.div(lane, HEAD) == slot, grad_query, 0.0)
        for at, here in enumerate(whose):
            dq_ref[here, :] += grad_query[at * rows : (at + 1) * rows]
        return 0

    lax.fori_loop(0, unit_count, unit, 0)

    def finish(chunk, _):
        here = pl.ds(pl.multiple_of(chunk * CHUNK, CHUNK), CHUNK)
        lane = lax.broadcasted_iota(jnp.int32, (CHUNK, LANES), 1)
        columns = [jnp.sum(ds_ref[slot, here, :], axis=1, keepdims=True) for slot in range(2)]
        grad_score = jnp.where(lane == 0, columns[0], jnp.where(lane == 1, columns[1], 0.0))
        grad_score = grad_score.T[:SCORE_ROWS].astype(jnp.bfloat16)
        score_ref[:, here] = grad_score
        message_ref[chunk, CHUNK:, 0:CHUNK] = grad_score
        message_ref[chunk, CHUNK:, CHUNK:] = jnp.zeros_like(message_ref[chunk, CHUNK:, CHUNK:])
        grads = (dq_ref[here, :] * HEAD**-0.5, dk_ref[here, :], dv_ref[here, :])
        for kind, grad in enumerate(grads):
            low = grad.astype(jnp.bfloat16)
            d_ref[here, kind * LANES : (kind + 1) * LANES] = low
            message_ref[chunk, 0:CHUNK, kind * LANES : (kind + 1) * LANES] = low
        return 0

    lax.fori_loop(0, length // CHUNK, finish, 0)


VMEM_LIMIT = 48 * 1024 * 1024


def kernel_params():
    return pltpu.CompilerParams(vmem_limit_bytes=VMEM_LIMIT)


def in_vmem():
    return pl.BlockSpec(memory_space=pltpu.VMEM)


def in_smem():
    return pl.BlockSpec(memory_space=pltpu.SMEM)


def attend(table, prefix, projected, rows, block):
    unit_count = table.shape[0]
    together = table.shape[1] - 2
    lanes = rows * together
    length = projected.shape[0]
    pairs = unit_count * lanes * length
    return pl.pallas_call(
        partial(forward_kernel, block),
        out_shape=(
            jax.ShapeDtypeStruct((unit_count, HEAD, lanes), jnp.float32),
            jax.ShapeDtypeStruct((unit_count * together, HEAD, rows), jnp.bfloat16),
            jax.ShapeDtypeStruct((unit_count, 1, lanes), jnp.float32),
            jax.ShapeDtypeStruct((unit_count, 1, lanes), jnp.float32),
        ),
        in_specs=[in_smem(), in_smem(), in_vmem()],
        out_specs=(in_vmem(),) * 4,
        scratch_shapes=[
            pltpu.VMEM((length, lanes), jnp.float32),
            pltpu.VMEM((length, lanes), jnp.float32),
            pltpu.VMEM((LANES, length), jnp.bfloat16),
        ],
        compiler_params=kernel_params(),
        cost_estimate=pl.CostEstimate(
            flops=pairs * 12000, bytes_accessed=projected.size * 4, transcendentals=pairs * 8
        ),
        name="attend",
    )(table, prefix, projected)


def attend_back(table, prefix, projected, grads, attended, log_totals, pivots, block):
    unit_count, _, lanes = attended.shape
    length = projected.shape[0]
    pairs = unit_count * lanes * length
    return pl.pallas_call(
        partial(backward_kernel, block),
        out_shape=(
            jax.ShapeDtypeStruct((length // CHUNK, CHUNK + SCORE_ROWS, 3 * LANES), jnp.bfloat16),
            jax.ShapeDtypeStruct((length, 3 * LANES), jnp.bfloat16),
            jax.ShapeDtypeStruct((SCORE_ROWS, length), jnp.bfloat16),
        ),
        in_specs=[in_smem(), in_smem()] + [in_vmem()] * 5,
        out_specs=(in_vmem(),) * 3,
        scratch_shapes=[
            pltpu.VMEM((length, LANES), jnp.float32),
            pltpu.VMEM((length, LANES), jnp.float32),
            pltpu.VMEM((length, LANES), jnp.float32),
            pltpu.VMEM((2, length, lanes), jnp.float32),
            pltpu.VMEM((LANES, length), jnp.bfloat16),
        ],
        compiler_params=kernel_params(),
        cost_estimate=pl.CostEstimate(
            flops=pairs * 9000, bytes_accessed=projected.size * 4, transcendentals=pairs * 3
        ),
        name="attend_back",
    )(table, prefix, projected, grads, attended, log_totals, pivots)


def project_kernel(count, offset, *refs):
    tokens, (gain_ref, shift_ref, weight_ref, _, __, normed_ref, projected_ref) = refs[:count], refs[count:]
    for step, tokens_ref in enumerate(tokens):

        @pl.when(pl.program_id(0) == step)
        def _(tokens_ref=tokens_ref):
            hat, _ = normalize(tokens_ref[...].astype(jnp.float32))
            normed = (hat * gain_ref[...] + shift_ref[...]).astype(jnp.bfloat16)
            normed_ref[...] = normed
            low = jnp.dot(normed, weight_ref[...], preferred_element_type=jnp.float32)
            low = low.astype(jnp.bfloat16).astype(jnp.float32)
            lane = lax.broadcasted_iota(jnp.int32, low.shape, 1)
            projected_ref[...] = jnp.where(lane < 3 * LANES, low, 0.5 * low).astype(jnp.bfloat16)


def project(places, tokens, gain, shift, weight, normed, projected):
    count = len(tokens)
    rows, width = tokens[0].shape
    columns = weight.shape[1]

    def whole(shape):
        return pl.BlockSpec(shape, lambda i, at: (0, 0))

    anywhere = pl.BlockSpec(memory_space=pl.ANY)
    return pl.pallas_call(
        partial(project_kernel, count),
        grid_spec=pltpu.PrefetchScalarGridSpec(
            num_scalar_prefetch=1,
            grid=(count,),
            in_specs=[whole((rows, width))] * count
            + [whole((1, width)), whole((1, width)), whole((width, columns)), anywhere, anywhere],
            out_specs=(
                pl.BlockSpec((rows, width), lambda i, at: (at[i], 0)),
                pl.BlockSpec((rows, columns), lambda i, at: (at[i], 0)),
            ),
        ),
        out_shape=(
            jax.ShapeDtypeStruct(normed.shape, normed.dtype),
            jax.ShapeDtypeStruct(projected.shape, projected.dtype),
        ),
        input_output_aliases={count + 4: 0, count + 5: 1},
        compiler_params=kernel_params(),
        cost_estimate=pl.CostEstimate(
            flops=2 * count * rows * width * columns * 20,
            bytes_accessed=rows * width * 12,
            transcendentals=0,
        ),
        name="project",
    )(jnp.stack(places).astype(jnp.int32), *tokens, gain, shift, weight, normed, projected)


def pack_kernel(pairs, vector_ref, query_ref, key_ref, value_ref, score_ref, out_ref):
    rows = query_ref.shape[0]
    spare = vector_ref[...].astype(jnp.float32).T[:rows]
    lane = lax.broadcasted_iota(jnp.int32, spare.shape, 1)
    for pattern, heads in enumerate(pairs):
        tail = spare
        for slot, head in enumerate(heads):
            score = score_ref[:, head : head + 1].astype(jnp.float32)
            tail = jnp.where(lane == slot, score, tail)
        for kind, ref in enumerate((query_ref, key_ref, value_ref)):
            pair = jnp.concatenate([ref[:, h * HEAD : (h + 1) * HEAD] for h in heads], axis=1)
            for copy in range(pattern, out_ref.shape[0], len(pairs)):
                out_ref[copy, :, kind * LANES : (kind + 1) * LANES] = pair
        for copy in range(pattern, out_ref.shape[0], len(pairs)):
            out_ref[copy, :, 3 * LANES :] = tail.astype(jnp.bfloat16)


def pack_heads(copies, pairs, vectors, query, key, value, score):
    return pl.pallas_call(
        partial(pack_kernel, pairs),
        out_shape=jax.ShapeDtypeStruct((copies, query.shape[0], 4 * LANES), jnp.bfloat16),
        in_specs=[in_vmem()] * 5,
        out_specs=in_vmem(),
        compiler_params=kernel_params(),
        name="pack_heads",
    )(jnp.pad(vectors, ((2, LANES - 2 - vectors.shape[0]), (0, LANES - vectors.shape[1]))), query, key, value, score)


def unpack_kernel(
    near, owners, first, arrived_ref, query_ref, key_ref, value_ref, score_ref, vector_ref, bias_ref
):
    rows = query_ref.shape[0]
    kinds = (query_ref, key_ref, value_ref)
    sources = [arrived_ref[first[0] + device].astype(jnp.float32) for device in range(near)]
    lane = lax.broadcasted_iota(jnp.int32, (rows, LANES), 1)
    scores = jnp.zeros((rows, LANES), jnp.float32)
    for head, terms in enumerate(owners):
        for kind, ref in enumerate(kinds):
            at = [kind * LANES + slot * HEAD for _, slot in terms]
            parts = [sources[d][:rows, a : a + HEAD] for (d, _), a in zip(terms, at)]
            ref[:, head * HEAD : (head + 1) * HEAD] = sum(parts[1:], parts[0])
        parts = [sources[d][:rows, 3 * LANES + slot : 3 * LANES + slot + 1] for d, slot in terms]
        scores = jnp.where(lane == head, sum(parts[1:], parts[0]), scores)
    score_ref[...] = scores[:, : score_ref.shape[1]]
    total = arrived_ref[0].astype(jnp.float32)
    for device in range(1, arrived_ref.shape[0]):
        total = total + arrived_ref[device].astype(jnp.float32)
    tail = jnp.concatenate([total[:rows, 3 * LANES :], jnp.zeros((LANES - rows, LANES), jnp.float32)], axis=0)
    vector_ref[...] = tail.T[:8, :rows]
    bias_ref[...] = total[rows:]


def unpack_heads(near, owners, first, arrived, heads, hidden):
    sources, rows, lanes = arrived.shape
    rows = rows - SCORE_ROWS
    shapes = [(rows, heads * HEAD)] * 3 + [(rows, heads), (8, rows), (SCORE_ROWS, lanes)]
    return pl.pallas_call(
        partial(unpack_kernel, near, owners),
        out_shape=[jax.ShapeDtypeStruct(shape, jnp.float32) for shape in shapes],
        in_specs=[in_smem(), in_vmem()],
        out_specs=[in_vmem()] * 6,
        compiler_params=kernel_params(),
        name="unpack_heads",
    )(first, arrived)


def finish_kernel(pairs, arrived_ref, halves_ref, tokens_ref, middle_ref, gain_ref, out_ref):
    rows, width = tokens_ref.shape
    near = len(pairs)
    half = width // 2
    total = jnp.zeros((rows, width), jnp.float32)
    for device in range(arrived_ref.shape[0]):
        heads = pairs[device % near]
        side = device // near
        weight = jnp.concatenate(
            [
                halves_ref[side, :, kind * half + head * HEAD : kind * half + (head + 1) * HEAD]
                for kind in range(3)
                for head in heads
            ],
            axis=1,
        )
        total += lax.dot_general(
            arrived_ref[device, :rows], weight, NT, preferred_element_type=jnp.float32
        )
        at = 3 * half
        lane = lax.broadcasted_iota(jnp.int32, (width, SCORE_ROWS), 1)
        columns = [halves_ref[side, :, at + head : at + head + 1].astype(jnp.float32) for head in heads]
        weight = jnp.where(lane == 0, columns[0], jnp.where(lane == 1, columns[1], 0.0))
        grads = arrived_ref[device, rows:, :rows].astype(jnp.float32).T
        total += lax.dot_general(
            grads.astype(jnp.bfloat16), weight.astype(jnp.bfloat16), NT, preferred_element_type=jnp.float32
        )
    hat, scale = normalize(tokens_ref[...].astype(jnp.float32))
    out_ref[...] = middle_ref[...] + normalize_back(total, hat, scale, gain_ref[...])


def finish_tokens(pairs, arrived, halves, tokens, grad_middle, gain):
    return pl.pallas_call(
        partial(finish_kernel, pairs),
        out_shape=jax.ShapeDtypeStruct(grad_middle.shape, jnp.float32),
        in_specs=[in_vmem()] * 5,
        out_specs=in_vmem(),
        compiler_params=kernel_params(),
        name="finish_tokens",
    )(arrived, halves, tokens, grad_middle, gain)


def ring_order(count):
    deep = 4 if count % 4 == 0 else 1
    wide = count // deep
    if deep == 1 or wide == 1:
        return list(range(count))
    walk = []
    for place in range(deep):
        across = range(1, wide) if place % 2 == 0 else range(wide - 1, 0, -1)
        walk += [place * wide + at for at in across]
    return walk + [place * wide for place in reversed(range(deep))]


def ring_gather(values, order):
    count = len(order)
    spot = jnp.asarray(np.argsort(order), jnp.int32)[lax.axis_index("ctx")]
    forward = [(order[i], order[(i + 1) % count]) for i in range(count)]
    backward = [(receiver, sender) for sender, receiver in forward]
    held = {0: values}
    for step in range(1, count // 2 + 1):
        held[-step] = lax.ppermute(held[1 - step], "ctx", forward)
        if step < count - step:
            held[step] = lax.ppermute(held[step - 1], "ctx", backward)
    walk = jnp.asarray(order, jnp.int32)
    return {distance: (walk[(spot + distance) % count], block) for distance, block in held.items()}


def other_core(values):
    return lax.ppermute(values, "tensor", [(0, 1), (1, 0)])


def normalize(values):
    centred = values - jnp.mean(values, axis=-1, keepdims=True)
    scale = lax.rsqrt(jnp.mean(centred * centred, axis=-1, keepdims=True) + norm_epsilon)
    return centred * scale, scale


def normalize_back(grad, hat, scale, gain):
    scaled = grad * gain
    return scale * (
        scaled
        - jnp.mean(scaled, axis=-1, keepdims=True)
        - hat * jnp.mean(scaled * hat, axis=-1, keepdims=True)
    )


def head_plan(ctx_count, head_count, block):
    parts = 1
    while head_count * parts % ctx_count:
        parts += 1
    share = head_count * parts // ctx_count
    rows = block // parts
    lows, tables = [], []
    for device in range(ctx_count):
        pieces = range(share * device, share * (device + 1))
        lows.append(pieces[0] // parts)
        tables.append(
            [
                (piece // parts - lows[-1], at * block + (piece % parts) * rows)
                + tuple((at + more) * share + order for more in range(parts))
                for order, piece in enumerate(pieces)
                for at in range(0, ctx_count, parts)
            ]
        )
        assert all(entry[0] in (0, 1) for entry in tables[-1])
    assert ctx_count % parts == 0
    return parts, share, rows, lows, np.asarray(tables, np.int32)


def on_device(
    tokens,
    prefix,
    w_query,
    w_key,
    w_value,
    w_score,
    w_attn_out,
    w_fc,
    w_proj,
    ln1_gain,
    ln1_bias,
    ln2_gain,
    ln2_bias,
    attn_bias,
    fc_bias,
    proj_bias,
    cotangent,
    dp_count,
    ctx_count,
):
    f32, bf16 = jnp.float32, jnp.bfloat16
    micro_count, seq_count, block, width = tokens.shape
    local_heads = w_score.shape[1]
    head_count = 2 * local_heads
    assert micro_count == 2 and seq_count == 1
    core = lax.axis_index("tensor")
    me = lax.axis_index("ctx")
    both = ("dp", "ctx")
    shards = dp_count * ctx_count
    shard_rows = width // shards
    parts, share, rows, lows, tables = head_plan(ctx_count, head_count, block)
    near = ctx_count // 2
    local_low = [low % local_heads for low in lows[:near]]
    local_high = [min(low + 1, local_heads - 1) for low in local_low]

    own_tokens = lax.dynamic_index_in_dim(tokens, core, 0, keepdims=False)[0]
    own_cot = lax.dynamic_index_in_dim(cotangent, core, 0, keepdims=False)[0]
    other_cot = lax.dynamic_index_in_dim(cotangent, 1 - core, 0, keepdims=False)[0]
    own_prefix = lax.dynamic_index_in_dim(prefix, core, 0, keepdims=False)
    table = jnp.asarray(tables)[me]

    blocks = ring_gather(own_tokens, ring_order(ctx_count))

    def columns(weight, head):
        return weight[:, head * HEAD : (head + 1) * HEAD]

    vectors = jnp.stack([ln1_gain, ln1_bias, ln2_gain, ln2_bias, attn_bias, proj_bias])
    pairs = tuple(zip(local_low, local_high))
    outgoing = pack_heads(shards, pairs, vectors, w_query, w_key, w_value, w_score)
    if ctx_count >= 6:
        outgoing, *_ = lax.optimization_barrier((outgoing, blocks[-1][1], blocks[1][1]))
    head_weights = lax.all_to_all(outgoing, both, 0, 0, tiled=True).reshape(width, 4 * LANES)
    if ctx_count >= 6:
        head_weights, *_ = lax.optimization_barrier((head_weights, blocks[-2][1], blocks[2][1]))
    from_half = (me >= near).astype(jnp.int32)
    head_weights = jnp.where(from_half == core, head_weights, other_core(head_weights))
    gains = head_weights[:, 3 * LANES + 2 : 3 * LANES + 8].astype(f32).T
    gain_one, shift_one, gain_two, shift_two, attn_shift, proj_shift = [gains[i : i + 1] for i in range(6)]

    score_columns = head_weights[:, 3 * LANES : 3 * LANES + 2]
    wide_weights = jnp.concatenate(
        [head_weights[:, :LANES] * HEAD**-0.5, head_weights[:, LANES : 3 * LANES]]
        + [jnp.broadcast_to(score_columns[:, i : i + 1], (width, LANES)) for i in range(2)],
        axis=1,
    )
    length = ctx_count * block
    normed = jnp.zeros((length, width), bf16)
    projected = jnp.zeros((length, 5 * LANES), bf16)
    near_first = sorted(blocks, key=lambda distance: (abs(distance), distance))
    batches = [near_first[: ctx_count - 3], near_first[ctx_count - 3 :]]
    for batch in batches:
        normed, projected = project(
            [blocks[d][0] for d in batch],
            [blocks[d][1] for d in batch],
            gain_one,
            shift_one,
            wide_weights,
            normed,
            projected,
        )

    packed = jnp.concatenate(
        [w_fc, w_proj.T, w_attn_out.T, w_query, w_key, w_value, w_score, jnp.zeros((shard_rows, LANES - local_heads), bf16)],
        axis=1,
    )
    packed, projected = lax.optimization_barrier((packed, projected))
    packed = lax.all_gather(packed, both, axis=0, tiled=True)
    attended, attended_low, log_totals, pivots = attend(table, own_prefix, projected, rows, block)
    packed, _ = lax.optimization_barrier((packed, log_totals))
    hidden = w_fc.shape[1]
    full_fc, full_proj_t = packed[:, :hidden], packed[:, hidden : 2 * hidden]
    half_out_t = packed[:, 2 * hidden : 2 * hidden + width // 2]
    half_heads = packed[:, 2 * hidden + width // 2 :]
    other_out_t, other_heads = other_core(half_out_t), other_core(half_heads)
    out_t = jnp.where(
        core == 0,
        jnp.concatenate([half_out_t, other_out_t], axis=1),
        jnp.concatenate([other_out_t, half_out_t], axis=1),
    )

    sent = attended_low.reshape(ctx_count, share * HEAD, rows)
    merged = lax.all_to_all(sent, "ctx", 0, 0, tiled=True)
    merged = merged.reshape(head_count, parts, HEAD, rows).transpose(0, 2, 1, 3).reshape(width, block)

    own_block = own_tokens.astype(f32)
    attn = lax.dot_general(merged, out_t, (((0,), (1,)), ((), ())), preferred_element_type=f32)
    middle = own_block + attn + attn_shift
    hat_two, scale_two = normalize(middle)
    normed_two = (hat_two * gain_two + shift_two).astype(bf16)
    normed_two = jnp.concatenate([normed_two, other_core(normed_two)])
    hidden_pre = jnp.dot(normed_two, full_fc, preferred_element_type=f32) + fc_bias.astype(f32)
    active, pull_gelu = jax.vjp(partial(jax.nn.gelu, approximate=True), hidden_pre)
    active = active.astype(bf16)
    mlp = lax.dot_general(active, full_proj_t, NT, preferred_element_type=f32)
    result = middle + mlp[:block] + other_core(mlp[block:].astype(bf16)).astype(f32) + proj_shift
    result = result.astype(bf16)

    both_cot = jnp.concatenate([own_cot, other_cot])
    grad_active = jnp.dot(both_cot, full_proj_t, preferred_element_type=f32)
    grad_pre = pull_gelu(grad_active)[0].astype(bf16)
    grad_two = lax.dot_general(grad_pre, full_fc, NT, preferred_element_type=f32)
    grad_two = grad_two[:block] + other_core(grad_two[block:].astype(bf16)).astype(f32)
    cot = own_cot.astype(f32)
    grad_middle = cot + normalize_back(grad_two, hat_two, scale_two, gain_two)
    grad_middle_low = grad_middle.astype(bf16)
    grad_merged = lax.dot_general(
        out_t, grad_middle_low, (((0,), (1,)), ((), ())), preferred_element_type=f32
    ).astype(bf16)
    sent = grad_merged.reshape(head_count, HEAD, parts, rows).transpose(0, 2, 1, 3)
    sent = sent.reshape(ctx_count, share * HEAD, rows)
    grad_attended = lax.all_to_all(sent, "ctx", 0, 0, tiled=True).reshape(attended_low.shape)

    grad_fc = lax.dot_general(normed_two, grad_pre, (((0,), (0,)), ((), ())), preferred_element_type=f32)
    grad_proj_t = lax.dot_general(both_cot, active, (((0,), (0,)), ((), ())), preferred_element_type=f32)
    grad_out_t = lax.dot_general(
        grad_middle_low, merged, (((0,), (1,)), ((), ())), preferred_element_type=f32
    ).astype(bf16)
    half_width = width // 2
    mine, theirs = grad_out_t[:, :half_width], grad_out_t[:, half_width:]
    mine, theirs = jnp.where(core == 0, mine, theirs), jnp.where(core == 0, theirs, mine)
    grad_out_t = (mine.astype(f32) + other_core(theirs).astype(f32)).astype(bf16)
    grad_packed = jnp.concatenate([grad_fc.astype(bf16), grad_proj_t.astype(bf16), grad_out_t], axis=1)
    grad_packed = lax.psum_scatter(grad_packed, both, scatter_dimension=0, tiled=True).astype(f32)

    message, grads, grad_scores = attend_back(
        table, own_prefix, projected, grad_attended, attended, log_totals, pivots, block
    )

    arrived = lax.all_to_all(message, "ctx", 0, 0, tiled=True)
    half_heads, other_heads, grads = lax.optimization_barrier((half_heads, other_heads, grads))
    halves = jnp.where(
        core == 0, jnp.stack([half_heads, other_heads]), jnp.stack([other_heads, half_heads])
    )
    tokens_grad = finish_tokens(pairs, arrived, halves, own_tokens, grad_middle, gain_one)

    grad_normed = lax.dot_general(grads, head_weights[:, : 3 * LANES], NT, preferred_element_type=f32)
    grad_normed = grad_normed + lax.dot_general(
        grad_scores[:2], score_columns, (((0,), (1,)), ((), ())), preferred_element_type=f32
    )
    hat_one = (normed.astype(f32) - shift_one) / gain_one

    grad_vectors = jnp.stack(
        [
            jnp.sum(grad_normed * hat_one, axis=0),
            jnp.sum(grad_normed, axis=0),
            jnp.sum(grad_two * hat_two, axis=0),
            jnp.sum(grad_two, axis=0),
            jnp.sum(grad_middle, axis=0),
            jnp.sum(cot, axis=0),
        ],
        axis=1,
    )
    over_rows = (((0,), (0,)), ((), ()))
    grad_heads = lax.dot_general(normed, grads, over_rows, preferred_element_type=f32)
    grad_columns = lax.dot_general(normed, grad_scores[:2], (((0,), (1,)), ((), ())), preferred_element_type=f32)
    spare = jnp.zeros((width, LANES - 8), f32)
    grad_heads = jnp.concatenate([grad_heads, grad_columns, grad_vectors, spare], axis=1)
    grad_heads = grad_heads + other_core(grad_heads.astype(bf16)).astype(f32)
    bias = jnp.sum(grad_pre.astype(f32), axis=0).reshape(hidden // (4 * LANES), 4 * LANES)
    bias = jnp.pad(bias, ((0, SCORE_ROWS - bias.shape[0]), (0, 0)))
    grad_heads = jnp.concatenate(
        [
            grad_heads.reshape(dp_count, ctx_count, shard_rows, 4 * LANES),
            jnp.broadcast_to(bias, (dp_count, ctx_count) + bias.shape),
        ],
        axis=2,
    ).astype(bf16)
    where = lax.axis_index("dp")
    summed = lax.dynamic_index_in_dim(grad_heads, where, 0, keepdims=False).astype(f32)
    for shift in range(1, dp_count):
        sent = lax.dynamic_index_in_dim(grad_heads, (where + shift) % dp_count, 0, keepdims=False)
        summed = summed + lax.ppermute(
            sent, "dp", [(i, (i + shift) % dp_count) for i in range(dp_count)]
        ).astype(f32)
    arrived = lax.all_to_all(summed.astype(bf16), "ctx", 0, 0, tiled=True)
    owners = [[] for _ in range(local_heads)]
    for device in range(near):
        for slot in sorted({entry[0] for entry in tables[device].tolist()}):
            owners[local_low[device] + slot].append((device, slot))
    grad_query, grad_key, grad_value, grad_score, vector_grads, fc_bias_grad = unpack_heads(
        near, owners, (core * near).astype(jnp.int32)[None], arrived, local_heads, hidden
    )
    vector_grads = vector_grads[2:].T
    fc_bias_grad = fc_bias_grad[: hidden // (4 * LANES)].reshape(hidden)

    def both_micro(own):
        other = other_core(own)
        return jnp.where(core == 0, jnp.stack([own, other]), jnp.stack([other, own]))[:, None]

    return (
        both_micro(result),
        both_micro(tokens_grad),
        grad_query,
        grad_key,
        grad_value,
        grad_score,
        grad_packed[:, 2 * hidden :].T,
        grad_packed[:, :hidden],
        grad_packed[:, hidden : 2 * hidden].T,
        vector_grads[:, 0],
        vector_grads[:, 1],
        vector_grads[:, 2],
        vector_grads[:, 3],
        vector_grads[:, 4],
        fc_bias_grad,
        vector_grads[:, 5],
    )


def solution(mesh):
    rows, columns, vector = P(("dp", "ctx"), "tensor"), P("tensor", ("dp", "ctx")), P(("dp", "ctx"))
    tokens = P(None, "dp", "ctx", None)
    in_specs = (
        (tokens, P(None, "dp"))
        + (rows,) * 4
        + (columns, rows, columns)
        + (vector,) * 5
        + (P("tensor"), vector, tokens)
    )
    out_specs = (
        (tokens, tokens)
        + (rows,) * 4
        + (columns, rows, columns)
        + (vector,) * 5
        + (P("tensor"), vector)
    )
    return jax.shard_map(
        partial(on_device, dp_count=mesh.shape["dp"], ctx_count=mesh.shape["ctx"]),
        mesh=mesh,
        in_specs=in_specs,
        out_specs=out_specs,
        check_vma=False,
    )
```

time: 551 us -> 411 us (0.75); the launches traced: 543 us -> 410 us
  starting transfers between devices: 122 us -> 37.7 us
  waiting for transfers between devices: 92.7 us -> 149 us
  blocking collectives: 52.3 us -> 0 us
  other arithmetic: 62.2 us -> 28.8 us
  local copies, waits for them, and re-layouts: 53.1 us -> 42.8 us
  Pallas kernels: 115 us -> 106 us
  matrix products: 30.7 us -> 23.8 us
  between operations: 15.5 us -> 21.4 us
    ppermute x34 -> x8, starting transfers between devices: 74.6 us -> 12.6 us  [the longest x4 7.78 us: ring_gather(): held[-step] = lax.ppermute(held[1 - step], 'ctx', forward)]
    psum x1 -> x0, blocking collectives: 52.3 us -> none  [on_device(): fc_bias_grad = lax.psum(jnp.sum(grad_pre.astype(f32), axis=0), both)]
    all_gather x1, waiting for transfers between devices: 0.02 us -> 50.3 us  [on_device(): packed = lax.all_gather(packed, both, axis=0, tiled=True)]
    reduce_scatter x1, waiting for transfers between devices: 0.01 us -> 46.7 us  [on_device(): lax.psum_scatter(grad_packed, both, scatter_dimension=0, tiled=True)]
    ppermute x34 -> x8, waiting for transfers between devices: 69.1 us -> 41.8 us  [the longest x4 24.2 us: ring_gather(): held[-step] = lax.ppermute(held[1 - step], 'ctx', forward)]
    all_to_all x2 -> x3, waiting for transfers between devices: 19.7 us -> 6.5 us  [the longest x1 6.43 us: on_device(): lax.all_to_all(sent, 'ctx', 0, 0, tiled=True).reshape(attended_low.shape)]
    ppermute x9 -> x10, starting transfers between devices: 13.2 us -> 1.64 us  [other_core(): return lax.ppermute(values, 'tensor', [(0, 1), (1, 0)])]
    all_to_all x1, starting transfers between devices: 15.2 us -> 3.77 us  [on_device(): merged = lax.all_to_all(sent, 'ctx', 0, 0, tiled=True)]
  transfers between devices with their start and end apart: 49 -> 25, of which waited for: 11 -> 10; matrix products, arithmetic and copies ran while one was open for 20% -> 19% of each run, Pallas kernels for 21% -> 25%
where the time goes in v2:
time: 411 us; the launch traced here: 410 us
  waiting for transfers between devices  149 us (36%)
  Pallas kernels  106 us (26%)
  local copies, waits for them, and re-layouts  42.8 us (10%)
  starting transfers between devices  37.7 us (9%)
  other arithmetic  28.8 us (7%)
  matrix products  23.8 us (6%)
  between operations  21.4 us (5%)
    all_gather x1, waiting for transfers between devices, on_device(): packed = lax.all_gather(packed, both, axis=0, tiled=True)  50.3 us
    pallas_call x1, Pallas kernels, attend(): pl.pallas_call(partial(forward_kernel, block), out_shape=(jax.ShapeDtypeS...  49.1 us
    reduce_scatter x1, waiting for transfers between devices, on_device(): lax.psum_scatter(grad_packed, both, scatter_dimension=0, tiled=True)  46.7 us
    pallas_call x1, Pallas kernels, attend_back(): pl.pallas_call(partial(backward_kernel, block), out_shape=(jax.ShapeDtype...  37.6 us
    ppermute x4, waiting for transfers between devices, ring_gather(): held[-step] = lax.ppermute(held[1 - step], 'ctx', forward)  24.2 us
    ppermute x1, waiting for transfers between devices, on_device(): lax.ppermute(sent, 'dp', [(i, (i + shift) % dp_count) for i in range(dp_c...  16.2 us
    unnamed x100, local copies, waits for them, and re-layouts  13.1 us
    pallas_call x2, Pallas kernels, project(): pl.pallas_call(partial(project_kernel, count), grid_spec=pltpu.PrefetchSc...  10.7 us
  transfers between devices with their start and end apart: 25, of which 10 were waited for; matrix products, arithmetic and copies ran while one was open for 19% of the time, Pallas kernels for 25%

profile of v2, /device:TPU:0, one launch (start us, length us, event | category | flops | bytes accessed | tf_op | source)
XLA Modules:
  0.0 410.1 jit_solution(13468142535670269451)
XLA Ops:
  7.3 1.1 copy-done
  8.4 3.0 collective-permute-start
  15.4 1.1 pack_heads.1
  16.4 4.1 %collective-permute-done.refs_1_ = bf16[256,768]{1,0:T(8,128)(2,1)S(1)} collective-permute-done((bf16[256,768]{1,0:T(8,128)(2,1)S(1)}, bf16[256,768]{1,0:T(8,128)(2,1)S(1)}, u32[]{:S(2)}, u32[]{:S(2)}) %collective-permute-start) | collective-permute-done | bytes 393248 | tf_op jit(solution)/shard_map/ppermute | solution.py:570
  20.6 1.4 collective-permute-done.3.refs_2_
  21.9 5.9 %all-to-all-start = ((bf16[16,48,512]{2,1,0:T(8,128)(2,1)}), bf16[16,48,512]{2,1,0:T(8,128)(2,1)S(1)}, u32[]{:S(2)}, u32[]{:S(2)}) async-start(bf16[16,48,512]{2,1,0:T(8,128)(2,1)} %pack_heads.1), calls=%async_computation | async-start | bytes 1572864 | tf_op jit(solution)/shard_map/all_to_all | solution.py:671
  27.9 2.0 collective-permute-start.1
  30.0 20.1 %collective-permute-done.1.refs_3_ = bf16[256,768]{1,0:T(8,128)(2,1)S(1)} collective-permute-done((bf16[256,768]{1,0:T(8,128)(2,1)S(1)}, bf16[256,768]{1,0:T(8,128)(2,1)S(1)}, u32[]{:S(2)}, u32[]{:S(2)}) %collective-permute-start.1) | collective-permute-done | bytes 393248 | tf_op jit(solution)/shard_map/ppermute | solution.py:570
  50.5 1.6 collective-permute-start.2
  59.3 1.8 concatenate.56
  61.7 3.3 stack.95.offset
  65.0 2.0 pad_add_fusion.offset
  67.0 4.5 %collective-permute-start.5 = (bf16[256,768]{1,0:T(8,128)(2,1)}, bf16[256,768]{1,0:T(8,128)(2,1)}, u32[]{:S(2)}, u32[]{:S(2)}) collective-permute-start(bf16[256,768]{1,0:T(8,128)(2,1)} %collective-permute-done.4.refs_4_), channel_id=1, source_target_pairs={{6,2},{10,6},{14,10},{12,14},{8,12},{4,8},{0,4},{2,0},{7,3},{11,7}... | collective-permute-start | bytes 1179656 | tf_op jit(solution)/shard_map/ppermute | solution.py:572
  71.6 1.2 collective-permute-start.6
  73.9 1.3 copy.68.refs_7_.refs_5_
  75.9 2.0 broadcast_in_dim.44.refs_8_
  78.6 6.0 %project.2 = (bf16[2048,768]{1,0:T(8,128)(2,1)}, bf16[2048,640]{1,0:T(8,128)(2,1)S(1)}) custom-call(s32[5]{0:T(128)S(1)} %stack.95.offset, bf16[256,768]{1,0:T(8,128)(2,1)S(1)} %copy-done.5, bf16[256,768]{1,0:T(8,128)(2,1)S(1)} %copy-done.19, bf16[256,768]{1,0:T(8,128)(2,1)S(1)} %copy-done.21, ...), custom_call_target="tpu_custom_call", output_to_operand_aliasing={{0}: (9, {}), {1}: (10, {})} | custom-call | flops 25165824000 | bytes 2359296 | tf_op jit(solution)/shard_map/project/pallas_call | solution.py:416
  84.6 4.7 %project.3 = (bf16[2048,768]{1,0:T(8,128)(2,1)}, bf16[2048,640]{1,0:T(8,128)(2,1)S(1)}) custom-call(s32[3]{0:T(128)S(1)} %pad_add_fusion.offset, bf16[256,768]{1,0:T(8,128)(2,1)} %collective-permute-done.2.refs_0_, bf16[256,768]{1,0:T(8,128)(2,1)} %collective-permute-done.5.refs_1_, ...), custom_call_target="tpu_custom_call", output_to_operand_aliasing={{0}: (7, {}), {1}: (8, {})} | custom-call | flops 15099494400 | bytes 2359296 | tf_op jit(solution)/shard_map/project/pallas_call | solution.py:416
  90.9 49.1 %attend.1 = (f32[12,64,256]{2,1,0:T(8,128)S(1)}, bf16[24,64,128]{2,1,0:T(8,128)(2,1)S(1)}, f32[12,1,256]{2,1,0:T(1,128)S(1)}, f32[12,1,256]{2,1,0:T(1,128)S(1)}) custom-call(s32[12,4]{1,0:T(8,128)S(1)} %copy.69.table, s32[1]{0:T(128)} %bitcast.2.prefix_ref, bf16[2048,640]{1,0:T(8,128)(2,1)S(1)} %get-tuple-element.46.p_ref), custom_call_target="tpu_custom_call" | custom-call | flops 75497472000 | bytes 5242880 | tf_op jit(solution)/shard_map/attend/pallas_call | solution.py:341
  140.8 0.9 copy-done.26
  141.7 3.8 all-to-all-start.1
  145.5 50.3 %all-gather.2.cloned.1.call-done = bf16[768,4736]{1,0:T(8,128)(2,1)} async-done(((bf16[48,4736]{1,0:T(8,128)(2,1)}), bf16[768,4736]{1,0:T(8,128)(2,1)}) %all-gather.2.cloned.1.call-update) | async-done | bytes 7274512 | tf_op jit(solution)/shard_map/all_gather | solution.py:706
  195.8 1.1 slice.117
  197.4 1.5 collective-permute-done.8
  200.4 1.1 convert_reduce_fusion.1
  201.6 3.1 slice.128
  205.1 3.4 convolution_add_fusion.1
  208.5 2.0 fusion.9
  210.6 3.2 convert_reduce_fusion
  213.8 1.4 fusion.13
  215.8 3.0 convolution_convert_fusion
  219.2 1.2 fusion.46
  221.0 0.9 broadcast_select_fusion.1
  221.9 2.8 convolution_convert_fusion.1
  225.4 0.8 copy.71
  226.2 3.7 all-to-all-start.2
  230.2 1.4 copy-done.31
  231.6 4.3 %pad_maximum_fusion = bf16[768,3456]{1,0:T(8,128)(2,1)} fusion(bf16[768,384]{1,0:T(8,128)(2,1)S(1)} %add_convert_fusion.1, bf16[768,1536]{1,0:T(8,128)(2,1)S(1)} %copy-done.31, bf16[768,1536]{1,0:T(8,128)(2,1)} %convolution_convert_fusion.1), kind=kLoop, calls=%fused_computation.1 | loop fusion | flops 15925248 | bytes 10616832 | tf_op jit(solution)/shard_map/concatenate | solution.py:761
  236.0 6.4 %all-to-all-done.2 = bf16[8,192,128]{2,1,0:T(8,128)(2,1)S(1)} async-done(((bf16[8,192,128]{2,1,0:T(8,128)(2,1)}), bf16[8,192,128]{2,1,0:T(8,128)(2,1)S(1)}, u32[]{:S(2)}, u32[]{:S(2)}) %all-to-all-start.2) | async-done | bytes 393248 | tf_op jit(solution)/shard_map/all_to_all | solution.py:750
  242.4 37.6 %attend_back.1 = (bf16[8,272,384]{2,1,0:T(8,128)(2,1)S(1)}, bf16[2048,384]{1,0:T(8,128)(2,1)S(1)}, bf16[16,2048]{1,0:T(8,128)(2,1)S(1)}) custom-call(s32[12,4]{1,0:T(8,128)S(1)} %copy.69.table, s32[1]{0:T(128)} %bitcast.2.prefix_ref, bf16[2048,640]{1,0:T(8,128)(2,1)} %copy-done.2, bf16[24,64,128]{2,1,0:T(8,128)(2,1)S(1)} %bitcast.78, ...), custom_call_target="tpu_custom_call" | custom-call | flops 56623104000 | bytes 5242880 | tf_op jit(solution)/shard_map/attend_back/pallas_call | solution.py:368
  280.0 1.2 copy-done.3
  281.2 1.1 copy-done.24
  282.3 3.7 all-to-all-start.3
  286.1 1.0 fusion.32
  287.5 1.0 copy-done.28
  288.5 2.3 fusion.45
  291.3 2.5 fusion.49
  293.9 5.4 %concatenate.62 = f32[768,512]{0,1:T(8,128)} concatenate(f32[768,384]{0,1:T(8,128)} %fusion.49, f32[768,2]{0,1:T(2,128)S(1)} %fusion.34, f32[768,1]{0,1:T(1,128)S(1)} %stack.108, f32[768,1]{0,1:T(1,128)S(1)} %stack.109, f32[768,1]{0,1:T(1,128)S(1)} %stack.110, f32[768,1]{0,1:T(1,128)S(1)} %stack.111, f32[768,1]{0,1:T(1,128)S(1)} %stack.112, f32[768,1]{0,1:T(1,128)S(1)} %stack.113, ...), dimensions={1} | concatenate | bytes 3145728 | tf_op jit(solution)/shard_map/concatenate | solution.py:796
  299.2 2.4 convert_element_type.102
  301.6 2.5 collective-permute-done.15
  304.1 2.4 add_convert_fusion
  306.5 1.4 copy.73
  308.0 0.8 fusion.23
  308.9 16.2 %collective-permute-done.16 = bf16[8,64,512]{2,1,0:T(8,128)(2,1)} collective-permute-done((bf16[8,64,512]{2,1,0:T(8,128)(2,1)}, bf16[8,64,512]{2,1,0:T(8,128)(2,1)}, u32[]{:S(2)}, u32[]{:S(2)}) %collective-permute-start.16) | collective-permute-done | bytes 524320 | tf_op jit(solution)/shard_map/ppermute | solution.py:811
  325.2 2.0 fusion.17
  327.2 6.3 %all-to-all-start.4 = ((bf16[8,64,512]{2,1,0:T(8,128)(2,1)}), bf16[8,64,512]{2,1,0:T(8,128)(2,1)}, u32[]{:S(2)}, u32[]{:S(2)}) async-start(bf16[8,64,512]{2,1,0:T(8,128)(2,1)} %fusion.17), calls=%async_computation.4 | async-start | bytes 1048576 | tf_op jit(solution)/shard_map/all_to_all | solution.py:814
  333.5 5.7 %maximum_select_fusion.halves_ref = bf16[2,768,1280]{2,1,0:T(8,128)(2,1)} fusion(bf16[1,768,1280]{2,1,0:T(8,128)(2,1)} %bitcast.25, bf16[1,768,1280]{2,1,0:T(8,128)(2,1)} %bitcast.24, pred[]{:T(512)S(6)} %eq.21), kind=kLoop, calls=%fused_computation.4 | loop fusion | flops 5898240 | bytes 7864321 | tf_op jit(solution)/shard_map/jit(_where)/select_n | solution.py:770
  339.2 5.8 %finish_tokens.1 = f32[256,768]{1,0:T(8,128)S(1)} custom-call(bf16[8,272,384]{2,1,0:T(8,128)(2,1)S(1)} %all-to-all-done.3.arrived_ref, bf16[2,768,1280]{2,1,0:T(8,128)(2,1)} %maximum_select_fusion.halves_ref, bf16[256,768]{1,0:T(8,128)(2,1)S(1)} %copy-done.7, f32[256,768]{1,0:T(8,128)S(1)} %get-tuple-element.131.middle_ref, f32[1,768]{1,0:T(1,128)S(1)} %copy-done.17), custom_call_target="tpu_custom_call" | custom-call | tf_op jit(solution)/shard_map/finish_tokens/pallas_call | solution.py:541
  345.1 2.4 maximum_select_fusion.3
  347.6 1.9 unpack_heads.1
  351.3 1.2 maximum_select_fusion.1
  352.6 46.7 %reduce-scatter.2.cloned.1.call-done = bf16[48,3456]{1,0:T(8,128)(2,1)} async-done(((bf16[768,3456]{1,0:T(8,128)(2,1)}), bf16[48,3456]{1,0:T(8,128)(2,1)}) %reduce-scatter.2.cloned.1.call-update) | async-done | bytes 331792 | tf_op jit(solution)/shard_map/reduce_scatter | solution.py:762
  399.2 1.0 convert_element_type.115
  401.6 1.6 slice.165
  (181 shorter events, 20.0 us)
Async XLA Ops:
  7.2 44.8 %copy-start.46 = (s32[8]{0:T(128)S(1)}, s32[8]{0:T(128)}, u32[]{:S(2)}) copy-start(s32[8]{0:T(128)} %constant.134.clone) | copy-start | bytes 100
  7.2 52.1 %copy-start.11 = (bf16[48,384]{1,0:T(8,128)(2,1)S(1)}, bf16[48,384]{1,0:T(8,128)(2,1)}, u32[]{:S(2)}) copy-start(bf16[48,384]{1,0:T(8,128)(2,1)} %query_ref.1) | copy-start | bytes 110596
  7.2 52.1 %copy-start.13 = (bf16[48,384]{1,0:T(8,128)(2,1)S(1)}, bf16[48,384]{1,0:T(8,128)(2,1)}, u32[]{:S(2)}) copy-start(bf16[48,384]{1,0:T(8,128)(2,1)} %key_ref.1) | copy-start | bytes 110596
  7.2 52.0 %copy-start.15 = (bf16[48,384]{1,0:T(8,128)(2,1)S(1)}, bf16[48,384]{1,0:T(8,128)(2,1)}, u32[]{:S(2)}) copy-start(bf16[48,384]{1,0:T(8,128)(2,1)} %value_ref.1) | copy-start | bytes 110596
  7.2 52.0 %copy-start.36 = (bf16[384,48]{0,1:T(8,128)(2,1)S(1)}, bf16[384,48]{0,1:T(8,128)(2,1)}, u32[]{:S(2)}) copy-start(bf16[384,48]{0,1:T(8,128)(2,1)} %param.26) | copy-start | bytes 110596
  7.3 52.0 %copy-start.35 = (bf16[48,1536]{1,0:T(8,128)(2,1)S(1)}, bf16[48,1536]{1,0:T(8,128)(2,1)}, u32[]{:S(2)}) copy-start(bf16[48,1536]{1,0:T(8,128)(2,1)} %param.27) | copy-start | bytes 442372
  8.4 52.7 %copy-start.4 = (bf16[256,768]{1,0:T(8,128)(2,1)}, bf16[256,768]{1,0:T(8,128)(2,1)S(1)}, u32[]{:S(2)}) copy-start(bf16[256,768]{1,0:T(8,128)(2,1)S(1)} %dynamic-slice_bitcast_fusion.2.refs_0_.tokens_ref) | copy-start | bytes 1179652
  8.4 12.2 %collective-permute-start = (bf16[256,768]{1,0:T(8,128)(2,1)S(1)}, bf16[256,768]{1,0:T(8,128)(2,1)S(1)}, u32[]{:S(2)}, u32[]{:S(2)}) collective-permute-start(bf16[256,768]{1,0:T(8,128)(2,1)S(1)} %dynamic-slice_bitcast_fusion.2.refs_0_.tokens_ref), channel_id=1, source_target_pairs={{2,6},{6,10},{10,14},{14,12},{12,8},{8,4},{4,0},{0,2},{3,7},{7,11}... | collective-permute-start | bytes 1179656 | tf_op jit(solution)/shard_map/ppermute | solution.py:570
  11.4 10.6 %collective-permute-start.3 = (bf16[256,768]{1,0:T(8,128)(2,1)S(1)}, bf16[256,768]{1,0:T(8,128)(2,1)S(1)}, u32[]{:S(2)}, u32[]{:S(2)}) collective-permute-start(bf16[256,768]{1,0:T(8,128)(2,1)S(1)} %dynamic-slice_bitcast_fusion.2.refs_0_.tokens_ref), channel_id=1, source_target_pairs={{6,2},{10,6},{14,10},{12,14},{8,12},{4,8},{0,4},{2,0},{7,3},{11,7}... | collective-permute-start | bytes 1179656 | tf_op jit(solution)/shard_map/ppermute | solution.py:572
  15.4 45.7 %copy-start.37 = (s32[8]{0:T(128)S(1)}, s32[8]{0:T(128)}, u32[]{:S(2)}) copy-start(s32[8]{0:T(128)} %constant.135.clone) | copy-start | bytes 100
  20.6 52.3 %copy-start.18 = (bf16[256,768]{1,0:T(8,128)(2,1)}, bf16[256,768]{1,0:T(8,128)(2,1)S(1)}, u32[]{:S(2)}) copy-start(bf16[256,768]{1,0:T(8,128)(2,1)S(1)} %collective-permute-done.refs_1_) | copy-start | bytes 1179652
  21.9 51.0 %copy-start.20 = (bf16[256,768]{1,0:T(8,128)(2,1)}, bf16[256,768]{1,0:T(8,128)(2,1)S(1)}, u32[]{:S(2)}) copy-start(bf16[256,768]{1,0:T(8,128)(2,1)S(1)} %collective-permute-done.3.refs_2_) | copy-start | bytes 1179652
  21.9 28.2 %all-to-all-start = ((bf16[16,48,512]{2,1,0:T(8,128)(2,1)}), bf16[16,48,512]{2,1,0:T(8,128)(2,1)S(1)}, u32[]{:S(2)}, u32[]{:S(2)}) async-start(bf16[16,48,512]{2,1,0:T(8,128)(2,1)} %pack_heads.1), calls=%async_computation | async-start | bytes 1572864 | tf_op jit(solution)/shard_map/all_to_all | solution.py:671
  27.9 167.9 %all-gather.2.cloned.1.call-start = ((), (), s32[]{:S(2)}) async-start(), calls=%async_computation.6 | async-start | bytes 7729152 | tf_op jit(solution)/shard_map/all_gather | solution.py:706
  27.9 22.2 %collective-permute-start.1 = (bf16[256,768]{1,0:T(8,128)(2,1)S(1)}, bf16[256,768]{1,0:T(8,128)(2,1)S(1)}, u32[]{:S(2)}, u32[]{:S(2)}) collective-permute-start(bf16[256,768]{1,0:T(8,128)(2,1)S(1)} %collective-permute-done.refs_1_), channel_id=1, source_target_pairs={{2,6},{6,10},{10,14},{14,12},{12,8},{8,4},{4,0},{0,2},{3,7},{7,11}... | collective-permute-start | bytes 1179656 | tf_op jit(solution)/shard_map/ppermute | solution.py:570
  29.9 20.2 %collective-permute-start.4 = (bf16[256,768]{1,0:T(8,128)(2,1)S(1)}, bf16[256,768]{1,0:T(8,128)(2,1)}, u32[]{:S(2)}, u32[]{:S(2)}) collective-permute-start(bf16[256,768]{1,0:T(8,128)(2,1)S(1)} %collective-permute-done.3.refs_2_), channel_id=1, source_target_pairs={{6,2},{10,6},{14,10},{12,14},{8,12},{4,8},{0,4},{2,0},{7,3},{11,7}... | collective-permute-start | bytes 1179656 | tf_op jit(solution)/shard_map/ppermute | solution.py:572
  50.1 22.9 %copy-start.22 = (bf16[256,768]{1,0:T(8,128)(2,1)}, bf16[256,768]{1,0:T(8,128)(2,1)S(1)}, u32[]{:S(2)}) copy-start(bf16[256,768]{1,0:T(8,128)(2,1)S(1)} %collective-permute-done.1.refs_3_) | copy-start | bytes 1179652
  50.4 22.4 %collective-permute-start.7 = (bf16[768,512]{0,1:T(8,128)(2,1)S(1)}, bf16[768,512]{0,1:T(8,128)(2,1)S(1)}, u32[]{:S(2)}, u32[]{:S(2)}) collective-permute-start(bf16[768,512]{0,1:T(8,128)(2,1)S(1)} %copy.66), channel_id=1, source_target_pairs={{0,1},{1,0},{2,3},{3,2},{4,5},{5,4},{6,7},{7,6},{8,9},{9,8},{10,11... | collective-permute-start | bytes 2359304 | tf_op jit(solution)/shard_map/ppermute | solution.py:578
  50.5 21.1 %collective-permute-start.2 = (bf16[256,768]{1,0:T(8,128)(2,1)S(1)}, bf16[256,768]{1,0:T(8,128)(2,1)}, u32[]{:S(2)}, u32[]{:S(2)}) collective-permute-start(bf16[256,768]{1,0:T(8,128)(2,1)S(1)} %collective-permute-done.1.refs_3_), channel_id=1, source_target_pairs={{2,6},{6,10},{10,14},{14,12},{12,8},{8,4},{4,0},{0,2},{3,7},{7,11}... | collective-permute-start | bytes 1179656 | tf_op jit(solution)/shard_map/ppermute | solution.py:570
  67.0 17.6 %collective-permute-start.5 = (bf16[256,768]{1,0:T(8,128)(2,1)}, bf16[256,768]{1,0:T(8,128)(2,1)}, u32[]{:S(2)}, u32[]{:S(2)}) collective-permute-start(bf16[256,768]{1,0:T(8,128)(2,1)} %collective-permute-done.4.refs_4_), channel_id=1, source_target_pairs={{6,2},{10,6},{14,10},{12,14},{8,12},{4,8},{0,4},{2,0},{7,3},{11,7}... | collective-permute-start | bytes 1179656 | tf_op jit(solution)/shard_map/ppermute | solution.py:572
  71.6 13.1 %collective-permute-start.6 = (bf16[256,768]{1,0:T(8,128)(2,1)}, bf16[256,768]{1,0:T(8,128)(2,1)}, u32[]{:S(2)}, u32[]{:S(2)}) collective-permute-start(bf16[256,768]{1,0:T(8,128)(2,1)} %collective-permute-done.2.refs_0_), channel_id=1, source_target_pairs={{2,6},{6,10},{10,14},{14,12},{12,8},{8,4},{4,0},{0,2},{3,7},{7,11}... | collective-permute-start | bytes 1179656 | tf_op jit(solution)/shard_map/ppermute | solution.py:570
  75.8 8.8 %copy-start.16 = (f32[1,768]{1,0:T(1,128)}, f32[1,768]{1,0:T(1,128)S(1)}, u32[]{:S(2)}) copy-start(f32[1,768]{1,0:T(1,128)S(1)} %get-tuple-element.134.refs_5_.refs_3_.gain_ref) | copy-start | bytes 9220
  75.8 2.2 copy-start.5
  75.8 2.2 copy-start.8
  75.8 2.2 copy-start.19
  75.8 2.5 copy-start.21
  75.8 2.8 copy-start.23
  84.6 4.8 %copy-start.45 = (s32[2,1]{0,1:T(1,128)S(1)}, s32[2,1]{0,1:T(1,128)}, u32[]{:S(2)}) copy-start(s32[2,1]{0,1:T(1,128)} %param.21) | copy-start | bytes 28
  89.4 50.7 %copy-start.2 = (bf16[2048,640]{1,0:T(8,128)(2,1)}, bf16[2048,640]{1,0:T(8,128)(2,1)S(1)}, u32[]{:S(2)}) copy-start(bf16[2048,640]{1,0:T(8,128)(2,1)S(1)} %get-tuple-element.46.p_ref) | copy-start | bytes 7864324
  141.7 57.3 %copy-start.6 = (bf16[256,768]{1,0:T(8,128)(2,1)S(1)}, bf16[256,768]{1,0:T(8,128)(2,1)}, u32[]{:S(2)}) copy-start(bf16[256,768]{1,0:T(8,128)(2,1)} %copy-done.4) | copy-start | bytes 1179652
  141.7 55.3 %all-to-all-start.1 = ((bf16[8,192,128]{2,1,0:T(8,128)(2,1)}), bf16[8,192,128]{2,1,0:T(8,128)(2,1)S(1)}, u32[]{:S(2)}, u32[]{:S(2)}) async-start(bf16[8,192,128]{2,1,0:T(8,128)(2,1)} %bitcast.79), calls=%async_computation.1 | async-start | bytes 786432 | tf_op jit(solution)/shard_map/all_to_all | solution.py:721
  196.9 2.7 copy-start.33
  196.9 2.1 collective-permute-start.8
  199.0 1.5 copy-start.38
  199.8 1.8 copy-start.32
  200.2 4.8 %collective-permute-start.9 = (bf16[256,768]{1,0:T(8,128)(2,1)S(1)}, bf16[256,768]{1,0:T(8,128)(2,1)S(1)}, u32[]{:S(2)}, u32[]{:S(2)}) collective-permute-start(bf16[256,768]{1,0:T(8,128)(2,1)S(1)} %add_convert_fusion.2), channel_id=1, source_target_pairs={{0,1},{1,0},{2,3},{3,2},{4,5},{5,4},{6,7},{7,6},{8,9},{9,8},{10,11... | collective-permute-start | bytes 1179656 | tf_op jit(solution)/shard_map/ppermute | solution.py:578
  201.5 6.9 %slice-start = ((s8[7274496]{0:T(1024)(128)(4,1)}), s8[4194304]{0:T(1024)(128)(4,1)S(1)}, s32[]{:S(2)}) async-start(s8[7274496]{0:T(1024)(128)(4,1)} %bitcast.88), calls=%async_computation.8 | async-start | bytes 8388608
  204.7 3.8 slice-start.1
  204.7 77.6 %collective-permute-start.13 = (bf16[768,1280]{1,0:T(8,128)(2,1)}, bf16[768,1280]{1,0:T(8,128)(2,1)}, u32[]{:S(2)}, u32[]{:S(2)}) collective-permute-start(bf16[768,1280]{1,0:T(8,128)(2,1)} %slice.128), channel_id=1, source_target_pairs={{0,1},{1,0},{2,3},{3,2},{4,5},{5,4},{6,7},{7,6},{8,9},{9,8},{10,11... | collective-permute-start | bytes 5898248 | tf_op jit(solution)/shard_map/ppermute | solution.py:578
  205.1 3.4 copy-start.43
  210.5 8.7 %collective-permute-start.10 = (bf16[256,768]{1,0:T(8,128)(2,1)S(1)}, bf16[256,768]{1,0:T(8,128)(2,1)S(1)}, u32[]{:S(2)}, u32[]{:S(2)}) collective-permute-start(bf16[256,768]{1,0:T(8,128)(2,1)S(1)} %slice.229), channel_id=1, source_target_pairs={{0,1},{1,0},{2,3},{3,2},{4,5},{5,4},{6,7},{7,6},{8,9},{9,8},{10,11... | collective-permute-start | bytes 1179656 | tf_op jit(solution)/shard_map/ppermute | solution.py:578
  215.2 3.5 collective-permute-start.12
  220.4 1.5 copy-start.44
  221.9 2.9 copy-start.34
  221.9 2.9 copy-start.42
  221.9 8.1 %collective-permute-start.17 = (bf16[768,384]{1,0:T(8,128)(2,1)}, bf16[768,384]{1,0:T(8,128)(2,1)S(1)}, u32[]{:S(2)}, u32[]{:S(2)}) collective-permute-start(bf16[768,384]{1,0:T(8,128)(2,1)} %broadcast_select_fusion.1), channel_id=1, source_target_pairs={{0,1},{1,0},{2,3},{3,2},{4,5},{5,4},{6,7},{7,6},{8,9},{9,8},{10,11... | collective-permute-start | bytes 1769480 | tf_op jit(solution)/shard_map/ppermute | solution.py:578
  226.2 16.2 %all-to-all-start.2 = ((bf16[8,192,128]{2,1,0:T(8,128)(2,1)}), bf16[8,192,128]{2,1,0:T(8,128)(2,1)S(1)}, u32[]{:S(2)}, u32[]{:S(2)}) async-start(bf16[8,192,128]{2,1,0:T(8,128)(2,1)} %bitcast.22), calls=%async_computation.2 | async-start | bytes 786432 | tf_op jit(solution)/shard_map/all_to_all | solution.py:750
  229.9 169.4 %reduce-scatter.2.cloned.1.call-start = ((), (), s32[]{:S(2)}) async-start(), calls=%async_computation.7 | async-start | bytes 5640192 | tf_op jit(solution)/shard_map/reduce_scatter | solution.py:762
  229.9 1.7 copy-start.31
  235.9 6.5 %copy-start.27 = (f32[12,64,256]{2,1,0:T(8,128)S(1)}, f32[12,64,256]{2,1,0:T(8,128)}, u32[]{:S(2)}) copy-start(f32[12,64,256]{2,1,0:T(8,128)} %copy-done.26) | copy-start | bytes 2359300
  282.3 3.7 copy-start.30
  282.3 44.8 %all-to-all-start.3 = ((bf16[8,272,384]{2,1,0:T(8,128)(2,1)}), bf16[8,272,384]{2,1,0:T(8,128)(2,1)S(1)}, u32[]{:S(2)}, u32[]{:S(2)}) async-start(bf16[8,272,384]{2,1,0:T(8,128)(2,1)} %copy-done.3), calls=%async_computation.3 | async-start | bytes 3342336 | tf_op jit(solution)/shard_map/all_to_all | solution.py:768
  286.1 1.4 copy-start.25
  286.1 2.4 copy-start.28
  286.1 2.4 copy-start.39
  286.1 2.4 copy-start.40
  301.6 2.5 collective-permute-start.15
  308.8 16.4 %collective-permute-start.16 = (bf16[8,64,512]{2,1,0:T(8,128)(2,1)}, bf16[8,64,512]{2,1,0:T(8,128)(2,1)}, u32[]{:S(2)}, u32[]{:S(2)}) collective-permute-start(bf16[8,64,512]{2,1,0:T(8,128)(2,1)} %fusion.23), channel_id=1, source_target_pairs={{0,16},{16,0},{1,17},{17,1},{2,18},{18,2},{3,19},{19,3},{4,20},{20... | collective-permute-start | bytes 1572872 | tf_op jit(solution)/shard_map/ppermute | solution.py:811
  308.8 36.3 %collective-permute-start.11 = (bf16[256,768]{1,0:T(8,128)(2,1)}, bf16[256,768]{1,0:T(8,128)(2,1)}, u32[]{:S(2)}, u32[]{:S(2)}) collective-permute-start(bf16[256,768]{1,0:T(8,128)(2,1)} %get-tuple-element.132), channel_id=1, source_target_pairs={{0,1},{1,0},{2,3},{3,2},{4,5},{5,4},{6,7},{7,6},{8,9},{9,8},{10,11... | collective-permute-start | bytes 1179656 | tf_op jit(solution)/shard_map/ppermute | solution.py:578
  327.2 20.4 %all-to-all-start.4 = ((bf16[8,64,512]{2,1,0:T(8,128)(2,1)}), bf16[8,64,512]{2,1,0:T(8,128)(2,1)}, u32[]{:S(2)}, u32[]{:S(2)}) async-start(bf16[8,64,512]{2,1,0:T(8,128)(2,1)} %fusion.17), calls=%async_computation.4 | async-start | bytes 1048576 | tf_op jit(solution)/shard_map/all_to_all | solution.py:814
  333.5 5.7 %copy-start.7 = (bf16[256,768]{1,0:T(8,128)(2,1)S(1)}, bf16[256,768]{1,0:T(8,128)(2,1)}, u32[]{:S(2)}) copy-start(bf16[256,768]{1,0:T(8,128)(2,1)} %copy-done.4) | copy-start | bytes 1179652
  333.5 5.7 %copy-start.17 = (f32[1,768]{1,0:T(1,128)S(1)}, f32[1,768]{1,0:T(1,128)}, u32[]{:S(2)}) copy-start(f32[1,768]{1,0:T(1,128)} %copy-done.16) | copy-start | bytes 9220
  345.0 6.3 %collective-permute-start.14 = (f32[256,768]{1,0:T(8,128)S(1)}, f32[256,768]{1,0:T(8,128)S(1)}, u32[]{:S(2)}, u32[]{:S(2)}) collective-permute-start(f32[256,768]{1,0:T(8,128)S(1)} %finish_tokens.1), channel_id=1, source_target_pairs={{0,1},{1,0},{2,3},{3,2},{4,5},{5,4},{6,7},{7,6},{8,9},{9,8},{10,11... | collective-permute-start | bytes 2359304 | tf_op jit(solution)/shard_map/ppermute | solution.py:578
  351.3 52.0 %copy-start.1 = (bf16[2,1,256,768]{3,2,1,0:T(8,128)(2,1)S(1)}, bf16[2,1,256,768]{3,2,1,0:T(8,128)(2,1)}, u32[]{:S(2)}) copy-start(bf16[2,1,256,768]{3,2,1,0:T(8,128)(2,1)} %param.20) | copy-start | bytes 2359300
  (10 other events, 9.1 us)
Sparse Core Ops, SparseCore 0:
  89.5 106.1 all-gather.1
  236.1 163.1 reduce-scatter.1

commit v3 on v2

--- a/solution.py
+++ b/solution.py
@@ -437,7 +437,7 @@
             transcendentals=0,
         ),
         name="project",
-    )(jnp.stack(places).astype(jnp.int32), *tokens, gain, shift, weight, normed, projected)
+    )(places, *tokens, gain, shift, weight, normed, projected)
 
 
 def pack_kernel(pairs, vector_ref, query_ref, key_ref, value_ref, score_ref, out_ref):
@@ -469,33 +469,43 @@
 
 
 def unpack_kernel(
-    near, owners, first, arrived_ref, query_ref, key_ref, value_ref, score_ref, vector_ref, bias_ref
+    near, owners, places, arrived_ref, query_ref, key_ref, value_ref, score_ref, vector_ref, bias_ref
 ):
     rows = query_ref.shape[0]
-    kinds = (query_ref, key_ref, value_ref)
-    sources = [arrived_ref[first[0] + device].astype(jnp.float32) for device in range(near)]
-    lane = lax.broadcasted_iota(jnp.int32, (rows, LANES), 1)
-    scores = jnp.zeros((rows, LANES), jnp.float32)
+    sources = [arrived_ref[places[0] + device].astype(jnp.float32) for device in range(near)]
     for head, terms in enumerate(owners):
-        for kind, ref in enumerate(kinds):
+        for kind, ref in enumerate((query_ref, key_ref, value_ref)):
             at = [kind * LANES + slot * HEAD for _, slot in terms]
             parts = [sources[d][:rows, a : a + HEAD] for (d, _), a in zip(terms, at)]
             ref[:, head * HEAD : (head + 1) * HEAD] = sum(parts[1:], parts[0])
-        parts = [sources[d][:rows, 3 * LANES + slot : 3 * LANES + slot + 1] for d, slot in terms]
-        scores = jnp.where(lane == head, sum(parts[1:], parts[0]), scores)
-    score_ref[...] = scores[:, : score_ref.shape[1]]
+
+    def line(values, index):
+        at = rows + 2 * index
+        return jnp.concatenate([values[at : at + 1], values[at + 1 : at + 2]], axis=1)
+
     total = arrived_ref[0].astype(jnp.float32)
     for device in range(1, arrived_ref.shape[0]):
         total = total + arrived_ref[device].astype(jnp.float32)
-    tail = jnp.concatenate([total[:rows, 3 * LANES :], jnp.zeros((LANES - rows, LANES), jnp.float32)], axis=0)
-    vector_ref[...] = tail.T[:8, :rows]
-    bias_ref[...] = total[rows:]
-
-
-def unpack_heads(near, owners, first, arrived, heads, hidden):
-    sources, rows, lanes = arrived.shape
-    rows = rows - SCORE_ROWS
-    shapes = [(rows, heads * HEAD)] * 3 + [(rows, heads), (8, rows), (SCORE_ROWS, lanes)]
+    lines = [line(total, 2 + index) for index in range(6)]
+    for terms in owners:
+        parts = [line(sources[device], slot) for device, slot in terms]
+        lines.append(sum(parts[1:], parts[0]))
+    width = lines[0].shape[1]
+    sublane = lax.broadcasted_iota(jnp.int32, (SCORE_ROWS, width), 0)
+    table = jnp.zeros((SCORE_ROWS, width), jnp.float32)
+    for index, values in enumerate(lines):
+        table = jnp.where(sublane == index, values, table)
+    table = pltpu.roll(table, width - places[1], 1)[:, :LANES]
+    vector_ref[...] = table[:8, :rows]
+    turned = jnp.concatenate([table, jnp.zeros((LANES - SCORE_ROWS, LANES), jnp.float32)], axis=0).T
+    score_ref[...] = turned[:rows, 6 : 6 + len(owners)]
+    for index in range(2):
+        bias_ref[index : index + 1] = line(total, 8 + index)
+
+
+def unpack_heads(near, owners, places, arrived, rows):
+    lanes = arrived.shape[2]
+    shapes = [(rows, lanes)] * 3 + [(rows, len(owners)), (8, rows), (2, 2 * lanes)]
     return pl.pallas_call(
         partial(unpack_kernel, near, owners),
         out_shape=[jax.ShapeDtypeStruct(shape, jnp.float32) for shape in shapes],
@@ -503,49 +513,56 @@
         out_specs=[in_vmem()] * 6,
         compiler_params=kernel_params(),
         name="unpack_heads",
-    )(first, arrived)
-
-
-def finish_kernel(pairs, arrived_ref, halves_ref, tokens_ref, middle_ref, gain_ref, out_ref):
+    )(places, arrived)
+
+
+def finish_kernel(
+    pairs, core_ref, arrived_ref, own_ref, other_ref, tokens_ref, middle_ref, gain_ref, out_ref
+):
     rows, width = tokens_ref.shape
     near = len(pairs)
     half = width // 2
     total = jnp.zeros((rows, width), jnp.float32)
-    for device in range(arrived_ref.shape[0]):
-        heads = pairs[device % near]
-        side = device // near
-        weight = jnp.concatenate(
-            [
-                halves_ref[side, :, kind * half + head * HEAD : kind * half + (head + 1) * HEAD]
-                for kind in range(3)
+    for columns_ref, side in ((own_ref, core_ref[0]), (other_ref, 1 - core_ref[0])):
+        for device, heads in enumerate(pairs):
+            weight = jnp.concatenate(
+                [
+                    columns_ref[:, kind * half + head * HEAD : kind * half + (head + 1) * HEAD]
+                    for kind in range(3)
+                    for head in heads
+                ],
+                axis=1,
+            )
+            at = side * near + device
+            total += lax.dot_general(
+                arrived_ref[at, :rows], weight, NT, preferred_element_type=jnp.float32
+            )
+            lane = lax.broadcasted_iota(jnp.int32, (width, SCORE_ROWS), 1)
+            columns = [
+                columns_ref[:, 3 * half + head : 3 * half + head + 1].astype(jnp.float32)
                 for head in heads
-            ],
-            axis=1,
-        )
-        total += lax.dot_general(
-            arrived_ref[device, :rows], weight, NT, preferred_element_type=jnp.float32
-        )
-        at = 3 * half
-        lane = lax.broadcasted_iota(jnp.int32, (width, SCORE_ROWS), 1)
-        columns = [halves_ref[side, :, at + head : at + head + 1].astype(jnp.float32) for head in heads]
-        weight = jnp.where(lane == 0, columns[0], jnp.where(lane == 1, columns[1], 0.0))
-        grads = arrived_ref[device, rows:, :rows].astype(jnp.float32).T
-        total += lax.dot_general(
-            grads.astype(jnp.bfloat16), weight.astype(jnp.bfloat16), NT, preferred_element_type=jnp.float32
-        )
+            ]
+            weight = jnp.where(lane == 0, columns[0], jnp.where(lane == 1, columns[1], 0.0))
+            grads = arrived_ref[at, rows:, :rows].astype(jnp.float32).T
+            total += lax.dot_general(
+                grads.astype(jnp.bfloat16),
+                weight.astype(jnp.bfloat16),
+                NT,
+                preferred_element_type=jnp.float32,
+            )
     hat, scale = normalize(tokens_ref[...].astype(jnp.float32))
     out_ref[...] = middle_ref[...] + normalize_back(total, hat, scale, gain_ref[...])
 
 
-def finish_tokens(pairs, arrived, halves, tokens, grad_middle, gain):
+def finish_tokens(pairs, core, arrived, own_columns, other_columns, tokens, grad_middle, gain):
     return pl.pallas_call(
         partial(finish_kernel, pairs),
         out_shape=jax.ShapeDtypeStruct(grad_middle.shape, jnp.float32),
-        in_specs=[in_vmem()] * 5,
+        in_specs=[in_smem()] + [in_vmem()] * 6,
         out_specs=in_vmem(),
         compiler_params=kernel_params(),
         name="finish_tokens",
-    )(arrived, halves, tokens, grad_middle, gain)
+    )(core, arrived, own_columns, other_columns, tokens, grad_middle, gain)
 
 
 def ring_order(count):
@@ -560,18 +577,74 @@
     return walk + [place * wide for place in reversed(range(deep))]
 
 
+def look_up(rows, index):
+    table = jnp.asarray(np.asarray(rows, np.int32))
+    return lax.dynamic_slice(table, (index, jnp.uint32(0)), (1, table.shape[1]))[0]
+
+
+def pick(values, index):
+    start = (index,) + (jnp.uint32(0),) * (values.ndim - 1)
+    return lax.dynamic_slice(values, start, (1,) + values.shape[1:])[0]
+
+
+def place_on(axis):
+    return lax.axis_index(axis).astype(jnp.uint32)
+
+
+def ring_distances(count):
+    return sorted(range(-(count // 2), (count + 1) // 2), key=lambda d: (abs(d), d))
+
+
+def ring_places(order):
+    count = len(order)
+    spots = np.argsort(order)
+    return [[order[(spots[me] + d) % count] for d in ring_distances(count)] for me in range(count)]
+
+
+def ring_hops(order):
+    count = len(order)
+    forward = [(order[i], order[(i + 1) % count]) for i in range(count)]
+    return forward, [(receiver, sender) for sender, receiver in forward]
+
+
 def ring_gather(values, order):
     count = len(order)
-    spot = jnp.asarray(np.argsort(order), jnp.int32)[lax.axis_index("ctx")]
-    forward = [(order[i], order[(i + 1) % count]) for i in range(count)]
-    backward = [(receiver, sender) for sender, receiver in forward]
+    forward, backward = ring_hops(order)
     held = {0: values}
     for step in range(1, count // 2 + 1):
         held[-step] = lax.ppermute(held[1 - step], "ctx", forward)
         if step < count - step:
             held[step] = lax.ppermute(held[step - 1], "ctx", backward)
-    walk = jnp.asarray(order, jnp.int32)
-    return {distance: (walk[(spot + distance) % count], block) for distance, block in held.items()}
+    return held
+
+
+def ring_scatter(terms, order, places):
+    count = len(order)
+    forward, backward = ring_hops(order)
+    at = {d: places[i].astype(jnp.uint32) for i, d in enumerate(ring_distances(count))}
+
+    def own(distance):
+        here = at.get(distance, at.get(distance - count))
+        return sum(pick(term, here).astype(jnp.float32) for term in terms)
+
+    ahead = behind = 0.0
+    for step in range(count // 2, 0, -1):
+        ahead = lax.ppermute((own(step) + ahead).astype(jnp.bfloat16), "ctx", forward)
+        ahead = ahead.astype(jnp.float32)
+        if step < count - step:
+            behind = lax.ppermute((own(-step) + behind).astype(jnp.bfloat16), "ctx", backward)
+            behind = behind.astype(jnp.float32)
+    return own(0) + ahead + behind
+
+
+def dp_terms(values):
+    count = values.shape[0]
+    places = look_up([[(i + shift) % count for shift in range(count)] for i in range(count)], place_on("dp"))
+    terms = [pick(values, places[0].astype(jnp.uint32))]
+    for shift in range(1, count):
+        sent = pick(values, places[shift].astype(jnp.uint32))
+        terms.append(lax.ppermute(sent, "dp", [(i, (i + shift) % count) for i in range(count)]))
+    return terms
 
 
 def other_core(values):
@@ -642,8 +715,8 @@
     local_heads = w_score.shape[1]
     head_count = 2 * local_heads
     assert micro_count == 2 and seq_count == 1
-    core = lax.axis_index("tensor")
-    me = lax.axis_index("ctx")
+    core = place_on("tensor")
+    me = place_on("ctx")
     both = ("dp", "ctx")
     shards = dp_count * ctx_count
     shard_rows = width // shards
@@ -652,13 +725,15 @@
     local_low = [low % local_heads for low in lows[:near]]
     local_high = [min(low + 1, local_heads - 1) for low in local_low]
 
-    own_tokens = lax.dynamic_index_in_dim(tokens, core, 0, keepdims=False)[0]
-    own_cot = lax.dynamic_index_in_dim(cotangent, core, 0, keepdims=False)[0]
-    other_cot = lax.dynamic_index_in_dim(cotangent, 1 - core, 0, keepdims=False)[0]
-    own_prefix = lax.dynamic_index_in_dim(prefix, core, 0, keepdims=False)
-    table = jnp.asarray(tables)[me]
-
-    blocks = ring_gather(own_tokens, ring_order(ctx_count))
+    own_tokens = pick(tokens, core)[0]
+    own_cot = pick(cotangent, core)[0]
+    other_cot = pick(cotangent, 1 - core)[0]
+    own_prefix = pick(prefix, core)
+    table = pick(jnp.asarray(tables), me)
+
+    order = ring_order(ctx_count)
+    blocks = ring_gather(own_tokens, order)
+    places = look_up(ring_places(order), me)
 
     def columns(weight, head):
         return weight[:, head * HEAD : (head + 1) * HEAD]
@@ -667,11 +742,11 @@
     pairs = tuple(zip(local_low, local_high))
     outgoing = pack_heads(shards, pairs, vectors, w_query, w_key, w_value, w_score)
     if ctx_count >= 6:
-        outgoing, *_ = lax.optimization_barrier((outgoing, blocks[-1][1], blocks[1][1]))
+        outgoing, *_ = lax.optimization_barrier((outgoing, blocks[-1], blocks[1]))
     head_weights = lax.all_to_all(outgoing, both, 0, 0, tiled=True).reshape(width, 4 * LANES)
     if ctx_count >= 6:
-        head_weights, *_ = lax.optimization_barrier((head_weights, blocks[-2][1], blocks[2][1]))
-    from_half = (me >= near).astype(jnp.int32)
+        head_weights, *_ = lax.optimization_barrier((head_weights, blocks[-2], blocks[2]))
+    from_half = (me >= near).astype(jnp.uint32)
     head_weights = jnp.where(from_half == core, head_weights, other_core(head_weights))
     gains = head_weights[:, 3 * LANES + 2 : 3 * LANES + 8].astype(f32).T
     gain_one, shift_one, gain_two, shift_two, attn_shift, proj_shift = [gains[i : i + 1] for i in range(6)]
@@ -685,12 +760,12 @@
     length = ctx_count * block
     normed = jnp.zeros((length, width), bf16)
     projected = jnp.zeros((length, 5 * LANES), bf16)
-    near_first = sorted(blocks, key=lambda distance: (abs(distance), distance))
-    batches = [near_first[: ctx_count - 3], near_first[ctx_count - 3 :]]
-    for batch in batches:
+    distances = ring_distances(ctx_count)
+    early = max(ctx_count - 3, 1)
+    for batch, batch_places in ((distances[:early], places[:early]), (distances[early:], places[early:])):
         normed, projected = project(
-            [blocks[d][0] for d in batch],
-            [blocks[d][1] for d in batch],
+            batch_places,
+            [blocks[d] for d in batch],
             gain_one,
             shift_one,
             wide_weights,
@@ -698,19 +773,20 @@
             projected,
         )
 
-    packed = jnp.concatenate(
-        [w_fc, w_proj.T, w_attn_out.T, w_query, w_key, w_value, w_score, jnp.zeros((shard_rows, LANES - local_heads), bf16)],
-        axis=1,
-    )
-    packed, projected = lax.optimization_barrier((packed, projected))
+    packed = jnp.concatenate([w_fc, w_proj.T, w_attn_out.T], axis=1)
+    packed_heads = jnp.concatenate(
+        [w_query, w_key, w_value, w_score, jnp.zeros((shard_rows, LANES - local_heads), bf16)], axis=1
+    )
+    packed, *_ = lax.optimization_barrier((packed, blocks[-2], blocks[2]))
     packed = lax.all_gather(packed, both, axis=0, tiled=True)
     attended, attended_low, log_totals, pivots = attend(table, own_prefix, projected, rows, block)
     packed, _ = lax.optimization_barrier((packed, log_totals))
     hidden = w_fc.shape[1]
     full_fc, full_proj_t = packed[:, :hidden], packed[:, hidden : 2 * hidden]
-    half_out_t = packed[:, 2 * hidden : 2 * hidden + width // 2]
-    half_heads = packed[:, 2 * hidden + width // 2 :]
-    other_out_t, other_heads = other_core(half_out_t), other_core(half_heads)
+    half_out_t = packed[:, 2 * hidden :]
+    other_out_t = other_core(half_out_t)
+    packed_heads, _ = lax.optimization_barrier((packed_heads, other_out_t))
+    half_heads = lax.all_gather(packed_heads, both, axis=0, tiled=True)
     out_t = jnp.where(
         core == 0,
         jnp.concatenate([half_out_t, other_out_t], axis=1),
@@ -759,18 +835,33 @@
     mine, theirs = jnp.where(core == 0, mine, theirs), jnp.where(core == 0, theirs, mine)
     grad_out_t = (mine.astype(f32) + other_core(theirs).astype(f32)).astype(bf16)
     grad_packed = jnp.concatenate([grad_fc.astype(bf16), grad_proj_t.astype(bf16), grad_out_t], axis=1)
-    grad_packed = lax.psum_scatter(grad_packed, both, scatter_dimension=0, tiled=True).astype(f32)
+    grad_packed = grad_packed.reshape(dp_count, ctx_count, shard_rows, grad_packed.shape[1])
+    grad_packed_terms = dp_terms(grad_packed)
+    early_lines = jnp.concatenate(
+        [
+            jnp.sum(grad_two * hat_two, axis=0, keepdims=True),
+            jnp.sum(grad_two, axis=0, keepdims=True),
+            jnp.sum(grad_middle, axis=0, keepdims=True),
+            jnp.sum(cot, axis=0, keepdims=True),
+        ]
+    )
+    bias_lines = jnp.sum(grad_pre.astype(f32), axis=0).reshape(hidden // width, width)
+    bias_lines = jnp.pad(bias_lines, ((0, 8 - bias_lines.shape[0]), (0, 0)))
 
     message, grads, grad_scores = attend_back(
         table, own_prefix, projected, grad_attended, attended, log_totals, pivots, block
     )
 
+    log_totals_after = grad_scores[:1]
+    shard = place_on("dp") * ctx_count + me
     arrived = lax.all_to_all(message, "ctx", 0, 0, tiled=True)
-    half_heads, other_heads, grads = lax.optimization_barrier((half_heads, other_heads, grads))
-    halves = jnp.where(
-        core == 0, jnp.stack([half_heads, other_heads]), jnp.stack([other_heads, half_heads])
-    )
-    tokens_grad = finish_tokens(pairs, arrived, halves, own_tokens, grad_middle, gain_one)
+    half_heads, _ = lax.optimization_barrier((half_heads, log_totals_after))
+    other_heads = other_core(half_heads)
+    *grad_packed_terms, _ = lax.optimization_barrier((*grad_packed_terms, log_totals_after))
+    grad_packed = ring_scatter(grad_packed_terms, order, places)
+    tokens_grad = finish_tokens(
+        pairs, core.astype(jnp.int32)[None], arrived, half_heads, other_heads, own_tokens, grad_middle, gain_one
+    )
 
     grad_normed = lax.dot_general(grads, head_weights[:, : 3 * LANES], NT, preferred_element_type=f32)
     grad_normed = grad_normed + lax.dot_general(
@@ -778,49 +869,40 @@
     )
     hat_one = (normed.astype(f32) - shift_one) / gain_one
 
-    grad_vectors = jnp.stack(
-        [
-            jnp.sum(grad_normed * hat_one, axis=0),
-            jnp.sum(grad_normed, axis=0),
-            jnp.sum(grad_two * hat_two, axis=0),
-            jnp.sum(grad_two, axis=0),
-            jnp.sum(grad_middle, axis=0),
-            jnp.sum(cot, axis=0),
-        ],
-        axis=1,
-    )
     over_rows = (((0,), (0,)), ((), ()))
     grad_heads = lax.dot_general(normed, grads, over_rows, preferred_element_type=f32)
-    grad_columns = lax.dot_general(normed, grad_scores[:2], (((0,), (1,)), ((), ())), preferred_element_type=f32)
-    spare = jnp.zeros((width, LANES - 8), f32)
-    grad_heads = jnp.concatenate([grad_heads, grad_columns, grad_vectors, spare], axis=1)
     grad_heads = grad_heads + other_core(grad_heads.astype(bf16)).astype(f32)
-    bias = jnp.sum(grad_pre.astype(f32), axis=0).reshape(hidden // (4 * LANES), 4 * LANES)
-    bias = jnp.pad(bias, ((0, SCORE_ROWS - bias.shape[0]), (0, 0)))
-    grad_heads = jnp.concatenate(
+    grad_heads = dp_terms(
+        grad_heads.astype(bf16).reshape(dp_count, ctx_count, shard_rows, 3 * LANES)
+    )
+    grad_columns = jnp.dot(grad_scores, normed, preferred_element_type=f32)
+    lines = jnp.concatenate(
         [
-            grad_heads.reshape(dp_count, ctx_count, shard_rows, 4 * LANES),
-            jnp.broadcast_to(bias, (dp_count, ctx_count) + bias.shape),
-        ],
-        axis=2,
-    ).astype(bf16)
-    where = lax.axis_index("dp")
-    summed = lax.dynamic_index_in_dim(grad_heads, where, 0, keepdims=False).astype(f32)
-    for shift in range(1, dp_count):
-        sent = lax.dynamic_index_in_dim(grad_heads, (where + shift) % dp_count, 0, keepdims=False)
-        summed = summed + lax.ppermute(
-            sent, "dp", [(i, (i + shift) % dp_count) for i in range(dp_count)]
-        ).astype(f32)
-    arrived = lax.all_to_all(summed.astype(bf16), "ctx", 0, 0, tiled=True)
+            grad_columns[:2],
+            jnp.sum(grad_normed * hat_one, axis=0, keepdims=True),
+            jnp.sum(grad_normed, axis=0, keepdims=True),
+            early_lines,
+        ]
+    )
+    lines = lines + other_core(lines.astype(bf16)).astype(f32)
+    lines = jnp.concatenate([lines, bias_lines])
+    lines = jnp.broadcast_to(lines.astype(bf16)[None], (dp_count,) + lines.shape)
+    lines = sum(term.astype(f32) for term in dp_terms(lines)).astype(bf16)
+    lines = lines.reshape(2 * lines.shape[0], 3 * LANES)
+    message = sum(term.astype(f32) for term in grad_heads).astype(bf16)
+    message = jnp.concatenate(
+        [message, jnp.broadcast_to(lines[None], (ctx_count,) + lines.shape)], axis=1
+    )
+    message, _ = lax.optimization_barrier((message, arrived))
+    arrived = lax.all_to_all(message, "ctx", 0, 0, tiled=True)
     owners = [[] for _ in range(local_heads)]
     for device in range(near):
         for slot in sorted({entry[0] for entry in tables[device].tolist()}):
             owners[local_low[device] + slot].append((device, slot))
     grad_query, grad_key, grad_value, grad_score, vector_grads, fc_bias_grad = unpack_heads(
-        near, owners, (core * near).astype(jnp.int32)[None], arrived, local_heads, hidden
-    )
-    vector_grads = vector_grads[2:].T
-    fc_bias_grad = fc_bias_grad[: hidden // (4 * LANES)].reshape(hidden)
+        near, owners, jnp.stack([core * near, shard * shard_rows]).astype(jnp.int32), arrived, shard_rows
+    )
+    fc_bias_grad = fc_bias_grad.reshape(hidden)
 
     def both_micro(own):
         other = other_core(own)
@@ -836,13 +918,13 @@
         grad_packed[:, 2 * hidden :].T,
         grad_packed[:, :hidden],
         grad_packed[:, hidden : 2 * hidden].T,
-        vector_grads[:, 0],
-        vector_grads[:, 1],
-        vector_grads[:, 2],
-        vector_grads[:, 3],
-        vector_grads[:, 4],
+        vector_grads[0],
+        vector_grads[1],
+        vector_grads[2],
+        vector_grads[3],
+        vector_grads[4],
         fc_bias_grad,
-        vector_grads[:, 5],
+        vector_grads[5],
     )
 
 

time: 411 us -> 381 us (0.927)
  waiting for transfers between devices: 149 us -> 86.8 us
  starting transfers between devices: 37.7 us -> 64 us
  matrix products: 23.8 us -> 35.9 us
  local copies, waits for them, and re-layouts: 42.8 us -> 37 us
    all_gather x1, waiting for transfers between devices: 50.3 us -> 2.21 us  [on_device(): packed = lax.all_gather(packed, both, axis=0, tiled=True)]
    reduce_scatter x1 -> x0, waiting for transfers between devices: 46.7 us -> none  [on_device(): lax.psum_scatter(grad_packed, both, scatter_dimension=0, tiled=True)]
    ppermute x1 -> x10, starting transfers between devices: 0.01 us -> 27.2 us  [the longest x3 13.3 us: ring_scatter(): lax.ppermute((own(-step) + behind).astype(jnp.bfloat16), 'ctx', backward)]
    ppermute x4, waiting for transfers between devices: 24.2 us -> 37.4 us  [ring_gather(): held[-step] = lax.ppermute(held[1 - step], 'ctx', forward)]
    all_to_all x1 -> x2, waiting for transfers between devices: 0.01 us -> 7.42 us  [on_device(): arrived = lax.all_to_all(message, 'ctx', 0, 0, tiled=True)]
    convert_element_type x3 -> x10, other arithmetic: 5.35 us -> 12.7 us  [the longest x4 7.99 us: ring_scatter(): (own(step) + ahead).astype(jnp.bfloat16)]
    ppermute x1 -> x10, waiting for transfers between devices: 16.2 us -> 23.1 us  [the longest x4 19.8 us: ring_scatter(): lax.ppermute((own(step) + ahead).astype(jnp.bfloat16), 'ctx', forward)]
    all_to_all x1 -> x0, starting transfers between devices: 6.33 us -> none  [on_device(): arrived = lax.all_to_all(summed.astype(bf16), 'ctx', 0, 0, tiled=True)]
  transfers between devices with their start and end apart: 25 -> 35, of which waited for: 10 -> 13; matrix products, arithmetic and copies ran while one was open for 19% -> 22% of each run, Pallas kernels for 25% -> 28%
where the time goes in v3:
time: 381 us; the launch traced here: 379 us
  Pallas kernels  105 us (28%)
  waiting for transfers between devices  86.8 us (23%)
  starting transfers between devices  64 us (17%)
  local copies, waits for them, and re-layouts  37 us (10%)
  matrix products  35.9 us (9%)
  other arithmetic  29.9 us (8%)
  between operations  21.3 us (6%)
    pallas_call x1, Pallas kernels, attend(): pl.pallas_call(partial(forward_kernel, block), out_shape=(jax.ShapeDtypeS...  49.6 us
    pallas_call x1, Pallas kernels, attend_back(): pl.pallas_call(partial(backward_kernel, block), out_shape=(jax.ShapeDtype...  37.6 us
    ppermute x4, waiting for transfers between devices, ring_gather(): held[-step] = lax.ppermute(held[1 - step], 'ctx', forward)  37.4 us
    ppermute x4, waiting for transfers between devices, ring_scatter(): lax.ppermute((own(step) + ahead).astype(jnp.bfloat16), 'ctx', forward)  19.8 us
    unnamed x100, local copies, waits for them, and re-layouts  14.2 us
    ppermute x3, starting transfers between devices, ring_scatter(): lax.ppermute((own(-step) + behind).astype(jnp.bfloat16), 'ctx', backward)  13.3 us
    ppermute x4, starting transfers between devices, ring_scatter(): lax.ppermute((own(step) + ahead).astype(jnp.bfloat16), 'ctx', forward)  10.8 us
    pallas_call x2, Pallas kernels, project(): pl.pallas_call(partial(project_kernel, count), grid_spec=pltpu.PrefetchSc...  9.69 us
  transfers between devices with their start and end apart: 35, of which 13 were waited for; matrix products, arithmetic and copies ran while one was open for 22% of the time, Pallas kernels for 28%

profile of v3, /device:TPU:0, one launch (start us, length us, event | category | flops | bytes accessed | tf_op | source)
XLA Modules:
  0.0 379.5 jit_solution(13557870374510186733)
XLA Ops:
  8.4 3.0 collective-permute-start
  16.4 4.1 %collective-permute-done.refs_1_ = bf16[256,768]{1,0:T(8,128)(2,1)S(1)} collective-permute-done((bf16[256,768]{1,0:T(8,128)(2,1)S(1)}, bf16[256,768]{1,0:T(8,128)(2,1)S(1)}, u32[]{:S(2)}, u32[]{:S(2)}) %collective-permute-start) | collective-permute-done | bytes 393248 | tf_op jit(solution)/shard_map/ppermute | solution.py:615
  20.5 1.4 collective-permute-done.3.refs_2_
  21.9 5.9 %all-to-all-start = ((bf16[16,48,512]{2,1,0:T(8,128)(2,1)}), bf16[16,48,512]{2,1,0:T(8,128)(2,1)S(1)}, u32[]{:S(2)}, u32[]{:S(2)}) async-start(bf16[16,48,512]{2,1,0:T(8,128)(2,1)} %pack_heads.1), calls=%async_computation | async-start | bytes 1572864 | tf_op jit(solution)/shard_map/all_to_all | solution.py:746
  27.9 2.0 collective-permute-start.1
  30.8 19.3 %collective-permute-done.1.refs_3_ = bf16[256,768]{1,0:T(8,128)(2,1)S(1)} collective-permute-done((bf16[256,768]{1,0:T(8,128)(2,1)S(1)}, bf16[256,768]{1,0:T(8,128)(2,1)S(1)}, u32[]{:S(2)}, u32[]{:S(2)}) %collective-permute-start.1) | collective-permute-done | bytes 393248 | tf_op jit(solution)/shard_map/ppermute | solution.py:615
  51.0 1.4 copy.64
  53.8 1.4 collective-permute-start.2
  56.1 4.7 %collective-permute-start.5 = (bf16[256,768]{1,0:T(8,128)(2,1)S(1)}, bf16[256,768]{1,0:T(8,128)(2,1)}, u32[]{:S(2)}, u32[]{:S(2)}) collective-permute-start(bf16[256,768]{1,0:T(8,128)(2,1)S(1)} %collective-permute-done.4.refs_4_), channel_id=1, source_target_pairs={{6,2},{10,6},{14,10},{12,14},{8,12},{4,8},{0,4},{2,0},{7,3},{11,7}... | collective-permute-start | bytes 1179656 | tf_op jit(solution)/shard_map/ppermute | solution.py:617
  60.8 9.0 %collective-permute-done.2.refs_0_ = bf16[256,768]{1,0:T(8,128)(2,1)} collective-permute-done((bf16[256,768]{1,0:T(8,128)(2,1)S(1)}, bf16[256,768]{1,0:T(8,128)(2,1)}, u32[]{:S(2)}, u32[]{:S(2)}) %collective-permute-start.2) | collective-permute-done | bytes 393248 | tf_op jit(solution)/shard_map/ppermute | solution.py:615
  72.7 1.6 copy.66.refs_7_.refs_5_
  74.2 1.8 broadcast_in_dim.66.refs_8_
  76.3 5.0 %project.2 = (bf16[2048,768]{1,0:T(8,128)(2,1)}, bf16[2048,640]{1,0:T(8,128)(2,1)S(1)}) custom-call(s32[5]{0:T(128)S(1)} %slice_bitcast_fusion.8.offset, bf16[256,768]{1,0:T(8,128)(2,1)S(1)} %dynamic-slice_bitcast_fusion.4.refs_0_.tokens_ref, bf16[256,768]{1,0:T(8,128)(2,1)S(1)} %collective-permute-done.refs_1_, ...), custom_call_target="tpu_custom_call", output_to_operand_aliasing={{0}: (9, {}), {1}: (10, {})} | custom-call | flops 25165824000 | bytes 2359296 | tf_op jit(solution)/shard_map/project/pallas_call | solution.py:416
  81.3 5.0 %collective-permute-done.6.refs_2_ = bf16[256,768]{1,0:T(8,128)(2,1)} collective-permute-done((bf16[256,768]{1,0:T(8,128)(2,1)}, bf16[256,768]{1,0:T(8,128)(2,1)}, u32[]{:S(2)}, u32[]{:S(2)}) %collective-permute-start.6) | collective-permute-done | bytes 393248 | tf_op jit(solution)/shard_map/ppermute | solution.py:615
  86.3 4.7 %project.3 = (bf16[2048,768]{1,0:T(8,128)(2,1)}, bf16[2048,640]{1,0:T(8,128)(2,1)S(1)}) custom-call(s32[3]{0:T(128)S(1)} %slice_bitcast_fusion.9.offset, bf16[256,768]{1,0:T(8,128)(2,1)} %collective-permute-done.2.refs_0_, bf16[256,768]{1,0:T(8,128)(2,1)} %collective-permute-done.5.refs_1_, ...), custom_call_target="tpu_custom_call", output_to_operand_aliasing={{0}: (7, {}), {1}: (8, {})} | custom-call | flops 15099494400 | bytes 2359296 | tf_op jit(solution)/shard_map/project/pallas_call | solution.py:416
  91.0 49.6 %attend.1 = (f32[12,64,256]{2,1,0:T(8,128)S(1)}, bf16[24,64,128]{2,1,0:T(8,128)(2,1)}, f32[12,1,256]{2,1,0:T(1,128)S(1)}, f32[12,1,256]{2,1,0:T(1,128)S(1)}) custom-call(s32[12,4]{1,0:T(8,128)S(1)} %copy.67.table, s32[1]{0:T(128)} %bitcast.2.prefix_ref, bf16[2048,640]{1,0:T(8,128)(2,1)S(1)} %get-tuple-element.46.p_ref), custom_call_target="tpu_custom_call" | custom-call | flops 75497472000 | bytes 5242880 | tf_op jit(solution)/shard_map/attend/pallas_call | solution.py:341
  140.6 4.4 %all-to-all-start.1 = ((bf16[8,192,128]{2,1,0:T(8,128)(2,1)}), bf16[8,192,128]{2,1,0:T(8,128)(2,1)S(1)}, u32[]{:S(2)}, u32[]{:S(2)}) async-start(bf16[8,192,128]{2,1,0:T(8,128)(2,1)} %bitcast.13), calls=%async_computation.1 | async-start | bytes 786432 | tf_op jit(solution)/shard_map/all_to_all | solution.py:797
  145.2 2.2 all-gather.3.cloned.1.call-done
  149.8 5.8 %all-to-all-done.1 = bf16[8,192,128]{2,1,0:T(8,128)(2,1)S(1)} async-done(((bf16[8,192,128]{2,1,0:T(8,128)(2,1)}), bf16[8,192,128]{2,1,0:T(8,128)(2,1)S(1)}, u32[]{:S(2)}, u32[]{:S(2)}) %all-to-all-start.1) | async-done | bytes 393248 | tf_op jit(solution)/shard_map/all_to_all | solution.py:797
  156.1 2.3 fusion.55
  167.5 1.8 dynamic-slice_bitcast_fusion.2
  169.3 3.3 convolution_add_fusion.1
  172.7 4.8 %fusion.9 = f32[512,768]{1,0:T(8,128)S(1)} fusion(bf16[768,3456]{1,0:T(8,128)(2,1)} %all-gather.3.cloned.1.call-done, f32[512,1536]{1,0:T(8,128)S(1)} %convolution_add_fusion.1), kind=kOutput, calls=%fused_computation.20 | convolution fusion | flops 1215037440 | bytes 7077888 | tf_op jit(solution)/shard_map/dot_general | solution.py:809
  177.6 3.2 fusion.56
  180.8 1.4 fusion.13
  185.5 5.1 %convolution_convert_fusion = bf16[768,1536]{1,0:T(8,128)(2,1)} fusion(bf16[256,768]{1,0:T(8,128)(2,1)} %dynamic-slice_bitcast_fusion.2, bf16[256,768]{1,0:T(8,128)(2,1)S(1)} %get-tuple-element.131, f32[512,1536]{1,0:T(8,128)} %copy-done.44), kind=kOutput, calls=%fused_computation.5 | convolution fusion | flops 1217789952 | bytes 6291456 | tf_op jit(solution)/shard_map/dot_general | solution.py:829
  191.8 2.4 fusion.52
  196.2 3.9 %convolution_convert_fusion.1 = bf16[768,1536]{1,0:T(8,128)(2,1)} fusion(bf16[512,1536]{1,0:T(8,128)(2,1)S(1)} %copy-done.46, bf16[256,768]{1,0:T(8,128)(2,1)} %collective-permute-done.9, bf16[256,768]{1,0:T(8,128)(2,1)S(1)} %copy-done.34), kind=kOutput, calls=%fused_computation.6 | convolution fusion | flops 1210712064 | bytes 4718592 | tf_op jit(solution)/shard_map/dot_general | solution.py:828
  200.2 1.8 convolution_convert_fusion.3
  203.0 3.7 all-to-all-start.2
  206.7 1.4 add_convert_fusion
  208.5 2.6 pad_maximum_fusion
  211.1 2.8 dynamic-slice_bitcast_fusion
  214.9 9.4 %all-to-all-done.2 = bf16[8,192,128]{2,1,0:T(8,128)(2,1)S(1)} async-done(((bf16[8,192,128]{2,1,0:T(8,128)(2,1)}), bf16[8,192,128]{2,1,0:T(8,128)(2,1)S(1)}, u32[]{:S(2)}, u32[]{:S(2)}) %all-to-all-start.2) | async-done | bytes 393248 | tf_op jit(solution)/shard_map/all_to_all | solution.py:826
  224.3 37.6 %attend_back.1 = (bf16[8,272,384]{2,1,0:T(8,128)(2,1)S(1)}, bf16[2048,384]{1,0:T(8,128)(2,1)S(1)}, bf16[16,2048]{1,0:T(8,128)(2,1)S(1)}) custom-call(s32[12,4]{1,0:T(8,128)S(1)} %copy.67.table, s32[1]{0:T(128)} %bitcast.2.prefix_ref, bf16[2048,640]{1,0:T(8,128)(2,1)} %copy-done.2, bf16[24,64,128]{2,1,0:T(8,128)(2,1)S(1)} %bitcast.120, ...), custom_call_target="tpu_custom_call" | custom-call | flops 56623104000 | bytes 5242880 | tf_op jit(solution)/shard_map/attend_back/pallas_call | solution.py:368
  261.9 1.2 copy-done.4
  264.3 4.1 %all-to-all-start.3 = ((bf16[8,272,384]{2,1,0:T(8,128)(2,1)}), bf16[8,272,384]{2,1,0:T(8,128)(2,1)S(1)}, u32[]{:S(2)}, u32[]{:S(2)}) async-start(bf16[8,272,384]{2,1,0:T(8,128)(2,1)} %copy-done.4), calls=%async_computation.3 | async-start | bytes 3342336 | tf_op jit(solution)/shard_map/all_to_all | solution.py:857
  268.4 1.9 fusion.38
  271.0 2.3 fusion.51
  273.9 3.3 collective-permute-done.20
  277.3 1.4 fusion.32
  278.7 1.5 collective-permute-start.21
  280.9 15.1 %collective-permute-done.21 = bf16[48,3456]{1,0:T(8,128)(2,1)S(1)} collective-permute-done((bf16[48,3456]{1,0:T(8,128)(2,1)S(1)}, bf16[48,3456]{1,0:T(8,128)(2,1)S(1)}, u32[]{:S(2)}, u32[]{:S(2)}) %collective-permute-start.21) | collective-permute-done | bytes 331808 | tf_op jit(solution)/shard_map/ppermute | solution.py:632
  296.0 1.9 fusion.22
  298.0 5.8 %collective-permute-start.22 = (bf16[48,3456]{1,0:T(8,128)(2,1)}, bf16[48,3456]{1,0:T(8,128)(2,1)}, u32[]{:S(2)}, u32[]{:S(2)}) collective-permute-start(bf16[48,3456]{1,0:T(8,128)(2,1)} %fusion.22), channel_id=1, source_target_pairs={{2,6},{6,10},{10,14},{14,12},{12,8},{8,4},{4,0},{0,2},{3,7},{7,11}... | collective-permute-start | bytes 995336 | tf_op jit(solution)/shard_map/ppermute | solution.py:632
  303.8 4.9 %fusion.57 = (bf16[768,384]{1,0:T(8,128)(2,1)}, f32[768,384]{1,0:T(8,128)}) fusion(bf16[2048,768]{1,0:T(8,128)(2,1)} %get-tuple-element.57, bf16[2048,384]{1,0:T(8,128)(2,1)S(1)} %copy-done.7), kind=kOutput, calls=%fused_computation.138 | convolution fusion | flops 1208254464 | bytes 6488064 | tf_op jit(solution)/shard_map/dot_general | solution.py:873
  308.7 11.1 %collective-permute-start.25 = (bf16[48,3456]{1,0:T(8,128)(2,1)S(1)}, bf16[48,3456]{1,0:T(8,128)(2,1)}, u32[]{:S(2)}, u32[]{:S(2)}) collective-permute-start(bf16[48,3456]{1,0:T(8,128)(2,1)S(1)} %get-tuple-element.137), channel_id=1, source_target_pairs={{6,2},{10,6},{14,10},{12,14},{8,12},{4,8},{0,4},{2,0},{7,3},{11,7}... | collective-permute-start | bytes 995336 | tf_op jit(solution)/shard_map/ppermute | solution.py:635
  320.2 2.0 fusion.23
  322.2 1.5 collective-permute-start.23
  323.7 1.5 add_convert_fusion.1
  326.8 1.3 collective-permute-start.16
  328.2 4.2 %collective-permute-done.23 = bf16[48,3456]{1,0:T(8,128)(2,1)} collective-permute-done((bf16[48,3456]{1,0:T(8,128)(2,1)}, bf16[48,3456]{1,0:T(8,128)(2,1)}, u32[]{:S(2)}, u32[]{:S(2)}) %collective-permute-start.23) | collective-permute-done | bytes 331808 | tf_op jit(solution)/shard_map/ppermute | solution.py:632
  332.4 2.6 fusion.24
  335.0 1.7 collective-permute-start.26
  338.6 5.4 %all-to-all-start.4 = ((bf16[8,80,384]{2,1,0:T(8,128)(2,1)}), bf16[8,80,384]{2,1,0:T(8,128)(2,1)S(1)}, u32[]{:S(2)}, u32[]{:S(2)}) async-start(bf16[8,80,384]{2,1,0:T(8,128)(2,1)} %pad_maximum_fusion.8), calls=%async_computation.4 | async-start | bytes 983040 | tf_op jit(solution)/shard_map/all_to_all | solution.py:897
  344.0 2.0 collective-permute-start.24
  346.0 2.0 fusion.21
  348.5 2.4 maximum_select_fusion.2
  350.9 7.4 %all-to-all-done.4.arrived_ref = bf16[8,80,384]{2,1,0:T(8,128)(2,1)S(1)} async-done(((bf16[8,80,384]{2,1,0:T(8,128)(2,1)}), bf16[8,80,384]{2,1,0:T(8,128)(2,1)S(1)}, u32[]{:S(2)}, u32[]{:S(2)}) %all-to-all-start.4) | async-done | bytes 491552 | tf_op jit(solution)/shard_map/all_to_all | solution.py:897
  358.3 1.4 unpack_heads.1
  361.5 1.5 copy-done.3
  363.1 5.2 %finish_tokens.1 = f32[256,768]{1,0:T(8,128)S(1)} custom-call(s32[1]{0:T(128)} %bitcast.20.core_ref, bf16[8,272,384]{2,1,0:T(8,128)(2,1)S(1)} %all-to-all-done.3.arrived_ref, bf16[768,1280]{1,0:T(8,128)(2,1)S(1)} %copy-done.3, bf16[768,1280]{1,0:T(8,128)(2,1)} %collective-permute-done.13.other_ref, ...), custom_call_target="tpu_custom_call" | custom-call | tf_op jit(solution)/shard_map/finish_tokens/pallas_call | solution.py:558
  368.4 1.5 fusion.25
  371.4 1.2 maximum_select_fusion
  (208 shorter events, 38.9 us)
Async XLA Ops:
  7.2 46.0 %copy-start.42 = (s32[2,1]{0,1:T(1,128)S(1)}, s32[2,1]{0,1:T(1,128)}, u32[]{:S(2)}) copy-start(s32[2,1]{0,1:T(1,128)} %param.22) | copy-start | bytes 28
  7.2 48.0 %copy-start.38 = (bf16[384,48]{0,1:T(8,128)(2,1)S(1)}, bf16[384,48]{0,1:T(8,128)(2,1)}, u32[]{:S(2)}) copy-start(bf16[384,48]{0,1:T(8,128)(2,1)} %param.27) | copy-start | bytes 110596
  7.2 48.0 %copy-start.36 = (bf16[1536,48]{0,1:T(8,128)(2,1)S(1)}, bf16[1536,48]{0,1:T(8,128)(2,1)}, u32[]{:S(2)}) copy-start(bf16[1536,48]{0,1:T(8,128)(2,1)} %param.29) | copy-start | bytes 442372
  7.2 48.0 %copy-start.37 = (bf16[48,1536]{1,0:T(8,128)(2,1)S(1)}, bf16[48,1536]{1,0:T(8,128)(2,1)}, u32[]{:S(2)}) copy-start(bf16[48,1536]{1,0:T(8,128)(2,1)} %param.28) | copy-start | bytes 442372
  8.4 12.2 %collective-permute-start = (bf16[256,768]{1,0:T(8,128)(2,1)S(1)}, bf16[256,768]{1,0:T(8,128)(2,1)S(1)}, u32[]{:S(2)}, u32[]{:S(2)}) collective-permute-start(bf16[256,768]{1,0:T(8,128)(2,1)S(1)} %dynamic-slice_bitcast_fusion.4.refs_0_.tokens_ref), channel_id=1, source_target_pairs={{2,6},{6,10},{10,14},{14,12},{12,8},{8,4},{4,0},{0,2},{3,7},{7,11}... | collective-permute-start | bytes 1179656 | tf_op jit(solution)/shard_map/ppermute | solution.py:615
  11.3 10.6 %collective-permute-start.3 = (bf16[256,768]{1,0:T(8,128)(2,1)S(1)}, bf16[256,768]{1,0:T(8,128)(2,1)S(1)}, u32[]{:S(2)}, u32[]{:S(2)}) collective-permute-start(bf16[256,768]{1,0:T(8,128)(2,1)S(1)} %dynamic-slice_bitcast_fusion.4.refs_0_.tokens_ref), channel_id=1, source_target_pairs={{6,2},{10,6},{14,10},{12,14},{8,12},{4,8},{0,4},{2,0},{7,3},{11,7}... | collective-permute-start | bytes 1179656 | tf_op jit(solution)/shard_map/ppermute | solution.py:617
  21.9 28.2 %all-to-all-start = ((bf16[16,48,512]{2,1,0:T(8,128)(2,1)}), bf16[16,48,512]{2,1,0:T(8,128)(2,1)S(1)}, u32[]{:S(2)}, u32[]{:S(2)}) async-start(bf16[16,48,512]{2,1,0:T(8,128)(2,1)} %pack_heads.1), calls=%async_computation | async-start | bytes 1572864 | tf_op jit(solution)/shard_map/all_to_all | solution.py:746
  27.9 119.5 %all-gather.3.cloned.1.call-start = ((), (), s32[]{:S(2)}) async-start(), calls=%async_computation.5 | async-start | bytes 5640192 | tf_op jit(solution)/shard_map/all_gather | solution.py:781
  27.9 22.2 %collective-permute-start.1 = (bf16[256,768]{1,0:T(8,128)(2,1)S(1)}, bf16[256,768]{1,0:T(8,128)(2,1)S(1)}, u32[]{:S(2)}, u32[]{:S(2)}) collective-permute-start(bf16[256,768]{1,0:T(8,128)(2,1)S(1)} %collective-permute-done.refs_1_), channel_id=1, source_target_pairs={{2,6},{6,10},{10,14},{14,12},{12,8},{8,4},{4,0},{0,2},{3,7},{7,11}... | collective-permute-start | bytes 1179656 | tf_op jit(solution)/shard_map/ppermute | solution.py:615
  29.9 20.2 %collective-permute-start.4 = (bf16[256,768]{1,0:T(8,128)(2,1)S(1)}, bf16[256,768]{1,0:T(8,128)(2,1)S(1)}, u32[]{:S(2)}, u32[]{:S(2)}) collective-permute-start(bf16[256,768]{1,0:T(8,128)(2,1)S(1)} %collective-permute-done.3.refs_2_), channel_id=1, source_target_pairs={{6,2},{10,6},{14,10},{12,14},{8,12},{4,8},{0,4},{2,0},{7,3},{11,7}... | collective-permute-start | bytes 1179656 | tf_op jit(solution)/shard_map/ppermute | solution.py:617
  52.4 17.6 %collective-permute-start.7 = (bf16[768,512]{0,1:T(8,128)(2,1)S(1)}, bf16[768,512]{0,1:T(8,128)(2,1)}, u32[]{:S(2)}, u32[]{:S(2)}) collective-permute-start(bf16[768,512]{0,1:T(8,128)(2,1)S(1)} %copy.64), channel_id=1, source_target_pairs={{0,1},{1,0},{2,3},{3,2},{4,5},{5,4},{6,7},{7,6},{8,9},{9,8},{10,11... | collective-permute-start | bytes 2359304 | tf_op jit(solution)/shard_map/ppermute | solution.py:651
  53.8 15.9 %collective-permute-start.2 = (bf16[256,768]{1,0:T(8,128)(2,1)S(1)}, bf16[256,768]{1,0:T(8,128)(2,1)}, u32[]{:S(2)}, u32[]{:S(2)}) collective-permute-start(bf16[256,768]{1,0:T(8,128)(2,1)S(1)} %collective-permute-done.1.refs_3_), channel_id=1, source_target_pairs={{2,6},{6,10},{10,14},{14,12},{12,8},{8,4},{4,0},{0,2},{3,7},{7,11}... | collective-permute-start | bytes 1179656 | tf_op jit(solution)/shard_map/ppermute | solution.py:615
  56.1 25.2 %collective-permute-start.5 = (bf16[256,768]{1,0:T(8,128)(2,1)S(1)}, bf16[256,768]{1,0:T(8,128)(2,1)}, u32[]{:S(2)}, u32[]{:S(2)}) collective-permute-start(bf16[256,768]{1,0:T(8,128)(2,1)S(1)} %collective-permute-done.4.refs_4_), channel_id=1, source_target_pairs={{6,2},{10,6},{14,10},{12,14},{8,12},{4,8},{0,4},{2,0},{7,3},{11,7}... | collective-permute-start | bytes 1179656 | tf_op jit(solution)/shard_map/ppermute | solution.py:617
  69.7 16.5 %collective-permute-start.6 = (bf16[256,768]{1,0:T(8,128)(2,1)}, bf16[256,768]{1,0:T(8,128)(2,1)}, u32[]{:S(2)}, u32[]{:S(2)}) collective-permute-start(bf16[256,768]{1,0:T(8,128)(2,1)} %collective-permute-done.2.refs_0_), channel_id=1, source_target_pairs={{2,6},{6,10},{10,14},{14,12},{12,8},{8,4},{4,0},{0,2},{3,7},{7,11}... | collective-permute-start | bytes 1179656 | tf_op jit(solution)/shard_map/ppermute | solution.py:615
  71.6 14.6 %copy-start.14 = (f32[1,768]{1,0:T(1,128)}, f32[1,768]{1,0:T(1,128)S(1)}, u32[]{:S(2)}) copy-start(f32[1,768]{1,0:T(1,128)S(1)} %get-tuple-element.144.refs_5_.refs_3_.gain_ref) | copy-start | bytes 9220
  91.0 49.6 %copy-start.2 = (bf16[2048,640]{1,0:T(8,128)(2,1)}, bf16[2048,640]{1,0:T(8,128)(2,1)S(1)}, u32[]{:S(2)}) copy-start(bf16[2048,640]{1,0:T(8,128)(2,1)S(1)} %get-tuple-element.46.p_ref) | copy-start | bytes 7864324
  91.0 57.7 %copy-start.43 = (s32[2,2]{1,0:T(2,128)S(1)}, s32[2,2]{1,0:T(2,128)}, u32[]{:S(2)}) copy-start(s32[2,2]{1,0:T(2,128)} %constant.58.clone) | copy-start | bytes 52
  140.6 15.5 %copy-start.16 = (f32[12,64,256]{2,1,0:T(8,128)}, f32[12,64,256]{2,1,0:T(8,128)S(1)}, u32[]{:S(2)}) copy-start(f32[12,64,256]{2,1,0:T(8,128)S(1)} %get-tuple-element.51.o_ref) | copy-start | bytes 2359300
  140.6 15.1 %all-to-all-start.1 = ((bf16[8,192,128]{2,1,0:T(8,128)(2,1)}), bf16[8,192,128]{2,1,0:T(8,128)(2,1)S(1)}, u32[]{:S(2)}, u32[]{:S(2)}) async-start(bf16[8,192,128]{2,1,0:T(8,128)(2,1)} %bitcast.13), calls=%async_computation.1 | async-start | bytes 786432 | tf_op jit(solution)/shard_map/all_to_all | solution.py:797
  145.0 183.2 %all-gather.5.cloned.1.call-start = ((), (), s32[]{:S(2)}) async-start(), calls=%async_computation.6 | async-start | bytes 2088960 | tf_op jit(solution)/shard_map/all_gather | solution.py:789
  148.5 7.6 %copy-start.30 = (bf16[768,384]{1,0:T(8,128)(2,1)}, bf16[768,384]{1,0:T(8,128)(2,1)S(1)}, u32[]{:S(2)}) copy-start(bf16[768,384]{1,0:T(8,128)(2,1)S(1)} %slice.181) | copy-start | bytes 1769476
  148.5 7.5 %collective-permute-start.8 = (bf16[768,384]{1,0:T(8,128)(2,1)S(1)}, bf16[768,384]{1,0:T(8,128)(2,1)}, u32[]{:S(2)}, u32[]{:S(2)}) collective-permute-start(bf16[768,384]{1,0:T(8,128)(2,1)S(1)} %slice.181), channel_id=1, source_target_pairs={{0,1},{1,0},{2,3},{3,2},{4,5},{5,4},{6,7},{7,6},{8,9},{9,8},{10,11... | collective-permute-start | bytes 1769480 | tf_op jit(solution)/shard_map/ppermute | solution.py:651
  156.1 3.5 copy-start.39
  156.1 3.5 copy-start.9
  156.1 3.5 copy-start.11
  156.1 3.5 copy-start.13
  158.9 13.8 %copy-start.33 = (bf16[256,768]{1,0:T(8,128)(2,1)}, bf16[256,768]{1,0:T(8,128)(2,1)S(1)}, u32[]{:S(2)}) copy-start(bf16[256,768]{1,0:T(8,128)(2,1)S(1)} %add_convert_fusion.2) | copy-start | bytes 1179652
  158.9 10.4 %collective-permute-start.9 = (bf16[256,768]{1,0:T(8,128)(2,1)S(1)}, bf16[256,768]{1,0:T(8,128)(2,1)}, u32[]{:S(2)}, u32[]{:S(2)}) collective-permute-start(bf16[256,768]{1,0:T(8,128)(2,1)S(1)} %add_convert_fusion.2), channel_id=1, source_target_pairs={{0,1},{1,0},{2,3},{3,2},{4,5},{5,4},{6,7},{7,6},{8,9},{9,8},{10,11... | collective-permute-start | bytes 1179656 | tf_op jit(solution)/shard_map/ppermute | solution.py:651
  169.3 8.2 %slice-start = ((s8[5308416]{0:T(1024)(128)(4,1)}), s8[4194304]{0:T(1024)(128)(4,1)S(1)}, s32[]{:S(2)}) async-start(s8[5308416]{0:T(1024)(128)(4,1)} %bitcast.131), calls=%async_computation.7 | async-start | bytes 8388608
  172.7 4.9 %copy-start.44 = (f32[512,1536]{1,0:T(8,128)}, f32[512,1536]{1,0:T(8,128)S(1)}, u32[]{:S(2)}) copy-start(f32[512,1536]{1,0:T(8,128)S(1)} %convolution_add_fusion.1) | copy-start | bytes 9437188
  172.7 4.9 %copy-start.35 = (bf16[256,768]{1,0:T(8,128)(2,1)S(1)}, bf16[256,768]{1,0:T(8,128)(2,1)}, u32[]{:S(2)}) copy-start(bf16[256,768]{1,0:T(8,128)(2,1)} %dynamic-slice_bitcast_fusion.2) | copy-start | bytes 1179652
  172.7 4.9 %slice-start.1 = ((s8[5308416]{0:T(1024)(128)(4,1)}), s8[1114112]{0:T(1024)(128)(4,1)S(1)}, s32[]{:S(2)}) async-start(s8[5308416]{0:T(1024)(128)(4,1)} %bitcast.131), calls=%async_computation.8 | async-start | bytes 2228224
  177.5 7.2 %copy-start.28 = (f32[512,768]{1,0:T(8,128)}, f32[512,768]{1,0:T(8,128)S(1)}, u32[]{:S(2)}) copy-start(f32[512,768]{1,0:T(8,128)S(1)} %fusion.9) | copy-start | bytes 4718596
  184.2 6.5 %collective-permute-start.12 = (bf16[256,768]{1,0:T(8,128)(2,1)}, bf16[256,768]{1,0:T(8,128)(2,1)S(1)}, u32[]{:S(2)}, u32[]{:S(2)}) collective-permute-start(bf16[256,768]{1,0:T(8,128)(2,1)} %slice.306), channel_id=1, source_target_pairs={{0,1},{1,0},{2,3},{3,2},{4,5},{5,4},{6,7},{7,6},{8,9},{9,8},{10,11... | collective-permute-start | bytes 1179656 | tf_op jit(solution)/shard_map/ppermute | solution.py:651
  185.5 5.6 %collective-permute-start.10 = (bf16[256,768]{1,0:T(8,128)(2,1)}, bf16[256,768]{1,0:T(8,128)(2,1)S(1)}, u32[]{:S(2)}, u32[]{:S(2)}) collective-permute-start(bf16[256,768]{1,0:T(8,128)(2,1)} %slice.307), channel_id=1, source_target_pairs={{0,1},{1,0},{2,3},{3,2},{4,5},{5,4},{6,7},{7,6},{8,9},{9,8},{10,11... | collective-permute-start | bytes 1179656 | tf_op jit(solution)/shard_map/ppermute | solution.py:651
  185.5 5.1 %copy-start.23 = (f32[512,768]{1,0:T(8,128)S(1)}, f32[512,768]{1,0:T(8,128)}, u32[]{:S(2)}) copy-start(f32[512,768]{1,0:T(8,128)} %copy-done.22) | copy-start | bytes 4718596
  185.5 6.4 %copy-start.29 = (f32[512,768]{1,0:T(8,128)S(1)}, f32[512,768]{1,0:T(8,128)}, u32[]{:S(2)}) copy-start(f32[512,768]{1,0:T(8,128)} %copy-done.28) | copy-start | bytes 4718596
  195.6 4.6 %copy-start.31 = (bf16[768,384]{1,0:T(8,128)(2,1)S(1)}, bf16[768,384]{1,0:T(8,128)(2,1)}, u32[]{:S(2)}) copy-start(bf16[768,384]{1,0:T(8,128)(2,1)} %copy-done.30) | copy-start | bytes 1769476
  195.6 11.0 %collective-permute-start.19 = (bf16[768,384]{1,0:T(8,128)(2,1)}, bf16[768,384]{1,0:T(8,128)(2,1)}, u32[]{:S(2)}, u32[]{:S(2)}) collective-permute-start(bf16[768,384]{1,0:T(8,128)(2,1)} %broadcast_select_fusion.1), channel_id=1, source_target_pairs={{0,1},{1,0},{2,3},{3,2},{4,5},{5,4},{6,7},{7,6},{8,9},{9,8},{10,11... | collective-permute-start | bytes 1769480 | tf_op jit(solution)/shard_map/ppermute | solution.py:651
  200.0 148.5 %collective-permute-start.11 = (bf16[256,768]{1,0:T(8,128)(2,1)}, bf16[256,768]{1,0:T(8,128)(2,1)}, u32[]{:S(2)}, u32[]{:S(2)}) collective-permute-start(bf16[256,768]{1,0:T(8,128)(2,1)} %get-tuple-element.140), channel_id=1, source_target_pairs={{0,1},{1,0},{2,3},{3,2},{4,5},{5,4},{6,7},{7,6},{8,9},{9,8},{10,11... | collective-permute-start | bytes 1179656 | tf_op jit(solution)/shard_map/ppermute | solution.py:651
  203.0 21.4 %all-to-all-start.2 = ((bf16[8,192,128]{2,1,0:T(8,128)(2,1)}), bf16[8,192,128]{2,1,0:T(8,128)(2,1)S(1)}, u32[]{:S(2)}, u32[]{:S(2)}) async-start(bf16[8,192,128]{2,1,0:T(8,128)(2,1)} %bitcast.24), calls=%async_computation.2 | async-start | bytes 786432 | tf_op jit(solution)/shard_map/all_to_all | solution.py:826
  211.0 13.3 %copy-start.17 = (f32[12,64,256]{2,1,0:T(8,128)S(1)}, f32[12,64,256]{2,1,0:T(8,128)}, u32[]{:S(2)}) copy-start(f32[12,64,256]{2,1,0:T(8,128)} %copy-done.16) | copy-start | bytes 2359300
  213.8 63.4 %collective-permute-start.20 = (bf16[8,48,3456]{2,1,0:T(8,128)(2,1)}, bf16[8,48,3456]{2,1,0:T(8,128)(2,1)}, u32[]{:S(2)}, u32[]{:S(2)}) collective-permute-start(bf16[8,48,3456]{2,1,0:T(8,128)(2,1)} %get-tuple-element.138), channel_id=1, source_target_pairs={{0,16},{16,0},{1,17},{17,1},{2,18},{18,2},{3,19},{19,3},{4,20},{20... | collective-permute-start | bytes 7962632 | tf_op jit(solution)/shard_map/ppermute | solution.py:646
  264.3 74.3 %all-to-all-start.3 = ((bf16[8,272,384]{2,1,0:T(8,128)(2,1)}), bf16[8,272,384]{2,1,0:T(8,128)(2,1)S(1)}, u32[]{:S(2)}, u32[]{:S(2)}) async-start(bf16[8,272,384]{2,1,0:T(8,128)(2,1)} %copy-done.4), calls=%async_computation.3 | async-start | bytes 3342336 | tf_op jit(solution)/shard_map/all_to_all | solution.py:857
  268.4 2.5 copy-start.21
  268.4 2.5 copy-start.40
  273.8 30.0 %copy-start.7 = (bf16[2048,384]{1,0:T(8,128)(2,1)S(1)}, bf16[2048,384]{1,0:T(8,128)(2,1)}, u32[]{:S(2)}) copy-start(bf16[2048,384]{1,0:T(8,128)(2,1)} %copy-done.5) | copy-start | bytes 4718596
  273.8 6.4 %collective-permute-start.17 = (bf16[8,768]{1,0:T(8,128)(2,1)S(1)}, bf16[8,768]{1,0:T(8,128)(2,1)S(1)}, u32[]{:S(2)}, u32[]{:S(2)}) collective-permute-start(bf16[8,768]{1,0:T(8,128)(2,1)S(1)} %convert_element_type.341), channel_id=1, source_target_pairs={{0,1},{1,0},{2,3},{3,2},{4,5},{5,4},{6,7},{7,6},{8,9},{9,8},{10,11... | collective-permute-start | bytes 36872 | tf_op jit(solution)/shard_map/ppermute | solution.py:651
  278.7 17.3 %collective-permute-start.21 = (bf16[48,3456]{1,0:T(8,128)(2,1)S(1)}, bf16[48,3456]{1,0:T(8,128)(2,1)S(1)}, u32[]{:S(2)}, u32[]{:S(2)}) collective-permute-start(bf16[48,3456]{1,0:T(8,128)(2,1)S(1)} %get-tuple-element.136), channel_id=1, source_target_pairs={{2,6},{6,10},{10,14},{14,12},{12,8},{8,4},{4,0},{0,2},{3,7},{7,11}... | collective-permute-start | bytes 995336 | tf_op jit(solution)/shard_map/ppermute | solution.py:632
  280.2 28.5 %collective-permute-start.18 = (bf16[16,768]{1,0:T(8,128)(2,1)S(1)}, bf16[16,768]{1,0:T(8,128)(2,1)S(1)}, u32[]{:S(2)}, u32[]{:S(2)}) collective-permute-start(bf16[16,768]{1,0:T(8,128)(2,1)S(1)} %fusion.37), channel_id=1, source_target_pairs={{0,16},{16,0},{1,17},{17,1},{2,18},{18,2},{3,19},{19,3},{4,20},{20... | collective-permute-start | bytes 73736 | tf_op jit(solution)/shard_map/ppermute | solution.py:646
  298.0 22.2 %collective-permute-start.22 = (bf16[48,3456]{1,0:T(8,128)(2,1)}, bf16[48,3456]{1,0:T(8,128)(2,1)}, u32[]{:S(2)}, u32[]{:S(2)}) collective-permute-start(bf16[48,3456]{1,0:T(8,128)(2,1)} %fusion.22), channel_id=1, source_target_pairs={{2,6},{6,10},{10,14},{14,12},{12,8},{8,4},{4,0},{0,2},{3,7},{7,11}... | collective-permute-start | bytes 995336 | tf_op jit(solution)/shard_map/ppermute | solution.py:632
  308.7 15.0 %collective-permute-start.15 = (bf16[768,384]{1,0:T(8,128)(2,1)}, bf16[768,384]{1,0:T(8,128)(2,1)}, u32[]{:S(2)}, u32[]{:S(2)}) collective-permute-start(bf16[768,384]{1,0:T(8,128)(2,1)} %get-tuple-element.165), channel_id=1, source_target_pairs={{0,1},{1,0},{2,3},{3,2},{4,5},{5,4},{6,7},{7,6},{8,9},{9,8},{10,11... | collective-permute-start | bytes 1769480 | tf_op jit(solution)/shard_map/ppermute | solution.py:651
  308.7 19.4 %collective-permute-start.25 = (bf16[48,3456]{1,0:T(8,128)(2,1)S(1)}, bf16[48,3456]{1,0:T(8,128)(2,1)}, u32[]{:S(2)}, u32[]{:S(2)}) collective-permute-start(bf16[48,3456]{1,0:T(8,128)(2,1)S(1)} %get-tuple-element.137), channel_id=1, source_target_pairs={{6,2},{10,6},{14,10},{12,14},{8,12},{4,8},{0,4},{2,0},{7,3},{11,7}... | collective-permute-start | bytes 995336 | tf_op jit(solution)/shard_map/ppermute | solution.py:635
  322.2 10.1 %collective-permute-start.23 = (bf16[48,3456]{1,0:T(8,128)(2,1)}, bf16[48,3456]{1,0:T(8,128)(2,1)}, u32[]{:S(2)}, u32[]{:S(2)}) collective-permute-start(bf16[48,3456]{1,0:T(8,128)(2,1)} %fusion.23), channel_id=1, source_target_pairs={{2,6},{6,10},{10,14},{14,12},{12,8},{8,4},{4,0},{0,2},{3,7},{7,11}... | collective-permute-start | bytes 995336 | tf_op jit(solution)/shard_map/ppermute | solution.py:632
  326.8 9.9 %collective-permute-start.16 = (bf16[8,48,384]{2,1,0:T(8,128)(2,1)}, bf16[8,48,384]{2,1,0:T(8,128)(2,1)}, u32[]{:S(2)}, u32[]{:S(2)}) collective-permute-start(bf16[8,48,384]{2,1,0:T(8,128)(2,1)} %dynamic-slice_bitcast_fusion.5), channel_id=1, source_target_pairs={{0,16},{16,0},{1,17},{17,1},{2,18},{18,2},{3,19},{19,3},{4,20},{20... | collective-permute-start | bytes 884744 | tf_op jit(solution)/shard_map/ppermute | solution.py:646
  328.1 8.6 %copy-start.25 = (bf16[768,384]{1,0:T(8,128)(2,1)S(1)}, bf16[768,384]{1,0:T(8,128)(2,1)}, u32[]{:S(2)}) copy-start(bf16[768,384]{1,0:T(8,128)(2,1)} %copy-done.24) | copy-start | bytes 1769476
  328.1 33.4 %collective-permute-start.13 = (bf16[768,1280]{1,0:T(8,128)(2,1)}, bf16[768,1280]{1,0:T(8,128)(2,1)}, u32[]{:S(2)}, u32[]{:S(2)}) collective-permute-start(bf16[768,1280]{1,0:T(8,128)(2,1)} %all-gather.5.cloned.1.call-done.own_ref), channel_id=1, source_target_pairs={{0,1},{1,0},{2,3},{3,2},{4,5},{5,4},{6,7},{7,6},{8,9},{9,8},{10,11... | collective-permute-start | bytes 5898248 | tf_op jit(solution)/shard_map/ppermute | solution.py:651
  335.0 11.0 %collective-permute-start.26 = (bf16[48,3456]{1,0:T(8,128)(2,1)}, bf16[48,3456]{1,0:T(8,128)(2,1)}, u32[]{:S(2)}, u32[]{:S(2)}) collective-permute-start(bf16[48,3456]{1,0:T(8,128)(2,1)} %get-tuple-element.135), channel_id=1, source_target_pairs={{6,2},{10,6},{14,10},{12,14},{8,12},{4,8},{0,4},{2,0},{7,3},{11,7}... | collective-permute-start | bytes 995336 | tf_op jit(solution)/shard_map/ppermute | solution.py:635
  337.8 23.7 %copy-start.15 = (f32[1,768]{1,0:T(1,128)S(1)}, f32[1,768]{1,0:T(1,128)}, u32[]{:S(2)}) copy-start(f32[1,768]{1,0:T(1,128)} %copy-done.14) | copy-start | bytes 9220
  338.6 19.7 %all-to-all-start.4 = ((bf16[8,80,384]{2,1,0:T(8,128)(2,1)}), bf16[8,80,384]{2,1,0:T(8,128)(2,1)S(1)}, u32[]{:S(2)}, u32[]{:S(2)}) async-start(bf16[8,80,384]{2,1,0:T(8,128)(2,1)} %pad_maximum_fusion.8), calls=%async_computation.4 | async-start | bytes 983040 | tf_op jit(solution)/shard_map/all_to_all | solution.py:897
  344.0 24.4 %collective-permute-start.24 = (bf16[48,3456]{1,0:T(8,128)(2,1)}, bf16[48,3456]{1,0:T(8,128)(2,1)}, u32[]{:S(2)}, u32[]{:S(2)}) collective-permute-start(bf16[48,3456]{1,0:T(8,128)(2,1)} %get-tuple-element.134), channel_id=1, source_target_pairs={{2,6},{6,10},{10,14},{14,12},{12,8},{8,4},{4,0},{0,2},{3,7},{7,11}... | collective-permute-start | bytes 995336 | tf_op jit(solution)/shard_map/ppermute | solution.py:632
  348.0 20.3 %collective-permute-start.27 = (bf16[48,3456]{1,0:T(8,128)(2,1)}, bf16[48,3456]{1,0:T(8,128)(2,1)}, u32[]{:S(2)}, u32[]{:S(2)}) collective-permute-start(bf16[48,3456]{1,0:T(8,128)(2,1)} %fusion.21), channel_id=1, source_target_pairs={{6,2},{10,6},{14,10},{12,14},{8,12},{4,8},{0,4},{2,0},{7,3},{11,7}... | collective-permute-start | bytes 995336 | tf_op jit(solution)/shard_map/ppermute | solution.py:635
  368.3 3.1 collective-permute-start.14
  368.4 4.3 %copy-start.1 = (bf16[2,1,256,768]{3,2,1,0:T(8,128)(2,1)S(1)}, bf16[2,1,256,768]{3,2,1,0:T(8,128)(2,1)}, u32[]{:S(2)}) copy-start(bf16[2,1,256,768]{3,2,1,0:T(8,128)(2,1)} %param.21) | copy-start | bytes 2359300
  (20 other events, 26.6 us)
Sparse Core Ops, SparseCore 0:
  56.2 91.1 all-gather.2
  169.4 61.1 all-gather.4
